TPU v7x, 128 devices: a whole 4x4x4 slice. The times are simulated.
128 devices in a mesh: seq: 16 (over y_hi, z, core), wt: 8 (over x, y_lo).
Axes of the slice: x: 4, y: 4 (y_hi: 2, y_lo: 2; y = y_hi * 2 + y_lo), z: 4, core: 2. Of those that a mesh axis runs over, the one named last changes fastest.
Arguments:
- layer_in: bfloat16 [8, 2048, 2048], P('wt', 'seq'), may hold values from -6 to 6
- segment_ids: int32 [8, 2048], P('wt'), may hold values from 0 to 2, as said below
- norm_one_gain: float32 [2048], replicated, may hold values from 0.5 to 1.5
- norm_one_shift: float32 [2048], replicated, may hold values from -3 to 3
- qkv_weight: bfloat16 [2048, 6144], P(None, 'wt'), may hold values from -0.125 to 0.125
- qkv_bias: float32 [6144], replicated, may hold values from -3 to 3
- out_weight: bfloat16 [2048, 2048], P(None, 'wt'), may hold values from -0.5 to 0.5
- norm_two_gain: float32 [2048], replicated, may hold values from 0.5 to 1.5
- norm_two_shift: float32 [2048], replicated, may hold values from -3 to 3
- gate_up_weight: bfloat16 [2048, 2, 5632], P(None, None, 'wt'), may hold values from -0.125 to 0.125
- down_weight: bfloat16 [5632, 2048], P('wt'), may hold values from -0.078125 to 0.078125
- layer_grad: bfloat16 [8, 2048, 2048], P('wt', 'seq'), may hold values from -6 to 6
Outputs:
- layer_out: bfloat16 [8, 2048, 2048], P('wt', 'seq')
- input_grad: bfloat16 [8, 2048, 2048], P('wt', 'seq')
- norm_one_gain_grad: float32 [2048], P(('seq', 'wt'))
- norm_one_shift_grad: float32 [2048], P(('seq', 'wt'))
- qkv_weight_grad: float32 [2048, 6144], P('seq', 'wt')
- qkv_bias_grad: float32 [6144], P(('seq', 'wt'))
- out_weight_grad: float32 [2048, 2048], P('seq', 'wt')
- norm_two_gain_grad: float32 [2048], P(('seq', 'wt'))
- norm_two_shift_grad: float32 [2048], P(('seq', 'wt'))
- gate_up_grad: float32 [2048, 2, 5632], P('seq', None, 'wt')
- down_grad: float32 [5632, 2048], P('wt', 'seq')
Inputs may be any that keep to these rules, and one draw needn't show every extreme that they name: `segment_ids`: in each row the segment ids never fall and form three documents; the middle one starts within the first 128 positions and ends within the last 128 positions.
All inputs are finite; a program needn't handle non-finite values.
Results may differ from a plain program's by a relative error of at most 0.025.
Values may be sent and summed in bfloat16 or wider, within the bound.
A program may use at most 320 MiB of HBM per device.

v0:
```python
import math

import jax
import jax.numpy as jnp
from jax import lax
from jax.sharding import PartitionSpec as P

HEADS = 32
HEAD_DIM = 64
ROT = 16


norm_eps = 1e-05
theta_base = 10000.0


def layer_norm_parts(values, gain, shift):
    average = jnp.mean(values, axis=-1, keepdims=True)
    centred = values - average
    spread = jnp.mean(centred * centred, axis=-1, keepdims=True)
    inverse = lax.rsqrt(spread + norm_eps)
    scaled = centred * inverse
    return (scaled * gain + shift, scaled, inverse)


def layer_norm_back(upward, scaled, inverse, gain):
    weighted = upward * gain
    first_mean = jnp.mean(weighted, axis=-1, keepdims=True)
    second_mean = jnp.mean(weighted * scaled, axis=-1, keepdims=True)
    return inverse * (weighted - first_mean - scaled * second_mean)


def rotary_tables(positions, own_segments, segment_row):
    doc_start = jnp.sum((segment_row[None, :] < own_segments[:, None]).astype(jnp.int32), axis=1)
    offsets = (positions - doc_start).astype(jnp.float32)
    inv_freq = jnp.exp(
        jnp.arange(ROT // 2, dtype=jnp.float32) * (-2.0 * math.log(theta_base) / ROT)
    )
    angles = offsets[:, None] * inv_freq[None, :]
    return (jnp.cos(angles), jnp.sin(angles))


def rotate(values, cosine, sine):
    half_rot = ROT // 2
    leading = values[..., :half_rot]
    trailing = values[..., half_rot:ROT]
    passive = values[..., ROT:]
    cos_wide = cosine[:, None, :]
    sin_wide = sine[:, None, :]
    return jnp.concatenate(
        [
            leading * cos_wide - trailing * sin_wide,
            trailing * cos_wide + leading * sin_wide,
            passive,
        ],
        axis=-1,
    )


def unrotate(values, cosine, sine):
    half_rot = ROT // 2
    leading = values[..., :half_rot]
    trailing = values[..., half_rot:ROT]
    passive = values[..., ROT:]
    cos_wide = cosine[:, None, :]
    sin_wide = sine[:, None, :]
    return jnp.concatenate(
        [
            leading * cos_wide + trailing * sin_wide,
            trailing * cos_wide - leading * sin_wide,
            passive,
        ],
        axis=-1,
    )


def masked_scores(queries, keys_seen, query_segments, key_segments, first_row):
    scores = jnp.einsum("qhd,khd->hqk", queries, keys_seen, preferred_element_type=jnp.float32)
    query_place = first_row + jnp.arange(queries.shape[0], dtype=jnp.int32)
    key_place = jnp.arange(keys_seen.shape[0], dtype=jnp.int32)
    allowed = (query_place[:, None] >= key_place[None, :]) & (
        query_segments[:, None] == key_segments[None, :]
    )
    return jnp.where(allowed[None], scores, -jnp.inf)


def swiglu_back(hidden_grad, gate_up):
    gate_part = gate_up[:, 0]
    up_part = gate_up[:, 1]
    sigma = jax.nn.sigmoid(gate_part)
    gate_grad = hidden_grad * up_part * sigma * (1.0 + gate_part * (1.0 - sigma))
    up_grad = hidden_grad * gate_part * sigma
    return jnp.stack([gate_grad, up_grad], axis=1).astype(jnp.bfloat16)


def contract_first(left, right):
    return lax.dot_general(
        left, right, (((0,), (0,)), ((), ())), preferred_element_type=jnp.float32
    )


def contract_last(left, right):
    return lax.dot_general(
        left, right, (((1,), (1,)), ((), ())), preferred_element_type=jnp.float32
    )


def per_device(
    layer_in,
    segment_ids,
    norm_one_gain,
    norm_one_shift,
    qkv_weight,
    qkv_bias,
    out_weight,
    norm_two_gain,
    norm_two_shift,
    gate_up_weight,
    down_weight,
    layer_grad,
):
    seq_count = lax.axis_size("seq")
    wt_count = lax.axis_size("wt")
    tok_rows = layer_in.shape[1]
    width = layer_in.shape[2]
    heads_local = HEADS // seq_count
    group_width = heads_local * HEAD_DIM
    seq_rows = tok_rows * seq_count
    score_scale = 1.0 / math.sqrt(HEAD_DIM)
    inputs = layer_in.reshape(tok_rows, width).astype(jnp.float32)
    upstream = layer_grad.reshape(tok_rows, width)
    segment_row = segment_ids.reshape(seq_rows)
    row_offset = lax.axis_index("seq") * tok_rows
    positions = row_offset + jnp.arange(tok_rows, dtype=jnp.int32)
    own_segments = lax.dynamic_slice_in_dim(segment_row, row_offset, tok_rows, 0)
    cosine, sine = rotary_tables(positions, own_segments, segment_row)
    normed_one, scaled_one, inverse_one = layer_norm_parts(inputs, norm_one_gain, norm_one_shift)
    normed_one_low = normed_one.astype(jnp.bfloat16)
    projected = (
        jnp.dot(
            normed_one_low,
            lax.all_gather(qkv_weight, "wt", axis=1, tiled=True),
            preferred_element_type=jnp.float32,
        )
        + qkv_bias
    )
    projected = projected.reshape(tok_rows, 3, HEADS, HEAD_DIM)
    queries = (rotate(projected[:, 0], cosine, sine) * score_scale).astype(jnp.bfloat16)
    keys_new = rotate(projected[:, 1], cosine, sine).astype(jnp.bfloat16)
    values_new = projected[:, 2].astype(jnp.bfloat16)
    stacked = jnp.stack([queries, keys_new, values_new], axis=1).reshape(
        tok_rows, 3, seq_count, group_width
    )
    regrouped = lax.all_to_all(stacked, "seq", split_axis=2, concat_axis=0, tiled=True).reshape(
        seq_rows, 3, heads_local, HEAD_DIM
    )
    query_heads = regrouped[:, 0]
    key_heads = regrouped[:, 1]
    value_heads = regrouped[:, 2]
    block_rows = min(seq_rows, max(512, seq_rows // 8))
    block_count = seq_rows // block_rows
    head_outputs = []
    log_sums = []
    for block_index in range(block_count):
        first_row = block_index * block_rows
        key_end = first_row + block_rows
        scores = masked_scores(
            query_heads[first_row:key_end],
            key_heads[:key_end],
            segment_row[first_row:key_end],
            segment_row[:key_end],
            first_row,
        )
        peak = jnp.max(scores, axis=-1, keepdims=True)
        expo = jnp.exp(scores - peak)
        totals = jnp.sum(expo, axis=-1, keepdims=True)
        weights_low = (expo / totals).astype(jnp.bfloat16)
        log_sums.append(peak + jnp.log(totals))
        block_out = jnp.einsum(
            "hqk,khd->qhd", weights_low, value_heads[:key_end], preferred_element_type=jnp.float32
        )
        head_outputs.append(block_out.astype(jnp.bfloat16))
    attended_heads = jnp.concatenate(head_outputs, axis=0).reshape(seq_rows, 1, group_width)
    attended = lax.all_to_all(
        attended_heads, "seq", split_axis=0, concat_axis=1, tiled=True
    ).reshape(tok_rows, width)
    branch = jnp.dot(
        attended,
        lax.all_gather(out_weight, "wt", axis=1, tiled=True),
        preferred_element_type=jnp.float32,
    )
    middle = inputs + branch
    normed_two, scaled_two, inverse_two = layer_norm_parts(middle, norm_two_gain, norm_two_shift)
    normed_two_low = normed_two.astype(jnp.bfloat16)
    gate_up = jnp.einsum(
        "td,dcf->tcf",
        normed_two_low,
        lax.all_gather(gate_up_weight, "wt", axis=2, tiled=True),
        preferred_element_type=jnp.float32,
    )
    hidden_low = (jax.nn.silu(gate_up[:, 0]) * gate_up[:, 1]).astype(jnp.bfloat16)
    ffn_out = jnp.dot(
        hidden_low,
        lax.all_gather(down_weight, "wt", axis=0, tiled=True),
        preferred_element_type=jnp.float32,
    )
    hidden_grad = contract_last(upstream, lax.all_gather(down_weight, "wt", axis=0, tiled=True))
    gate_up_low = swiglu_back(hidden_grad, gate_up)
    part_cols = gate_up_low
    normed_two_grad = jnp.einsum(
        "tcf,dcf->td",
        part_cols,
        lax.all_gather(gate_up_weight, "wt", axis=2, tiled=True),
        preferred_element_type=jnp.float32,
    )
    rows_two, rows_upstream = (
        lax.all_gather(normed_two_low, "wt", axis=0, tiled=True),
        lax.all_gather(upstream, "wt", axis=0, tiled=True),
    )
    joined_cols = jnp.concatenate([gate_up_low, hidden_low[:, None, :]], axis=1)
    joined_cols = lax.all_to_all(joined_cols, "wt", split_axis=2, concat_axis=0, tiled=True)
    gate_weight_grad = jnp.einsum(
        "td,tcf->dcf", rows_two, joined_cols[:, 0:2], preferred_element_type=jnp.float32
    )
    down_weight_grad = contract_first(joined_cols[:, 2], rows_upstream)
    layer_out = (middle + ffn_out).astype(jnp.bfloat16).reshape(1, tok_rows, width)
    upstream_wide = upstream.astype(jnp.float32)
    gain_two_grad = jnp.sum(normed_two_grad * scaled_two, axis=0)
    shift_two_grad = jnp.sum(normed_two_grad, axis=0)
    middle_grad = upstream_wide + layer_norm_back(
        normed_two_grad, scaled_two, inverse_two, norm_two_gain
    )
    branch_grad = middle_grad.astype(jnp.bfloat16)
    part_cols = branch_grad
    attended_grad = contract_last(
        part_cols, lax.all_gather(out_weight, "wt", axis=1, tiled=True)
    ).astype(jnp.bfloat16)
    heads_grad = lax.all_to_all(
        attended_grad.reshape(tok_rows, seq_count, group_width),
        "seq",
        split_axis=1,
        concat_axis=0,
        tiled=True,
    )
    heads_grad = heads_grad.reshape(seq_rows, heads_local, HEAD_DIM)
    query_grads = []
    key_grad = jnp.zeros((seq_rows, heads_local, HEAD_DIM), jnp.float32)
    value_grad = jnp.zeros((seq_rows, heads_local, HEAD_DIM), jnp.float32)
    for block_index in range(block_count):
        first_row = block_index * block_rows
        key_end = first_row + block_rows
        scores = masked_scores(
            query_heads[first_row:key_end],
            key_heads[:key_end],
            segment_row[first_row:key_end],
            segment_row[:key_end],
            first_row,
        )
        weights_full = jnp.exp(scores - log_sums[block_index])
        weights_low = weights_full.astype(jnp.bfloat16)
        grad_block = heads_grad[first_row:key_end]
        weight_grad = jnp.einsum(
            "qhd,khd->hqk", grad_block, value_heads[:key_end], preferred_element_type=jnp.float32
        )
        row_inner = jnp.sum(weights_full * weight_grad, axis=-1, keepdims=True)
        score_grad = (weights_full * (weight_grad - row_inner)).astype(jnp.bfloat16)
        query_grads.append(
            jnp.einsum(
                "hqk,khd->qhd", score_grad, key_heads[:key_end], preferred_element_type=jnp.float32
            )
        )
        key_grad = key_grad.at[:key_end].add(
            jnp.einsum(
                "hqk,qhd->khd",
                score_grad,
                query_heads[first_row:key_end],
                preferred_element_type=jnp.float32,
            )
        )
        value_grad = value_grad.at[:key_end].add(
            jnp.einsum("hqk,qhd->khd", weights_low, grad_block, preferred_element_type=jnp.float32)
        )
    query_grad = jnp.concatenate(query_grads, axis=0)
    stacked_grad = (
        jnp.stack([query_grad, key_grad, value_grad], axis=1)
        .astype(jnp.bfloat16)
        .reshape(seq_rows, 3, 1, group_width)
    )
    returned = (
        lax.all_to_all(stacked_grad, "seq", split_axis=0, concat_axis=2, tiled=True)
        .reshape(tok_rows, 3, HEADS, HEAD_DIM)
        .astype(jnp.float32)
    )
    query_lin = unrotate(returned[:, 0] * score_scale, cosine, sine)
    key_lin = unrotate(returned[:, 1], cosine, sine)
    projected_grad = (
        jnp.stack([query_lin, key_lin, returned[:, 2]], axis=1)
        .reshape(tok_rows, 3 * width)
        .astype(jnp.bfloat16)
    )
    bias_grad = jnp.sum(projected_grad.astype(jnp.float32), axis=0)
    part_cols = projected_grad
    normed_one_grad = contract_last(part_cols, lax.all_gather(qkv_weight, "wt", axis=1, tiled=True))
    gain_one_grad = jnp.sum(normed_one_grad * scaled_one, axis=0)
    shift_one_grad = jnp.sum(normed_one_grad, axis=0)
    input_full = middle_grad + layer_norm_back(
        normed_one_grad, scaled_one, inverse_one, norm_one_gain
    )
    input_grad = input_full.astype(jnp.bfloat16).reshape(1, tok_rows, width)

    def blocks_of(vector):
        return vector.reshape(seq_count, wt_count, vector.shape[0] // (seq_count * wt_count))

    small_grads = jnp.concatenate(
        [
            blocks_of(vector)
            for vector in (gain_one_grad, shift_one_grad, bias_grad, gain_two_grad, shift_two_grad)
        ],
        axis=2,
    )
    qkv_weight_sum = contract_first(normed_one_low, projected_grad)
    out_weight_sum = contract_first(attended, branch_grad)
    qkv_weight_sum, out_weight_sum, small_grads, gate_weight_grad, down_weight_grad = (
        lax.psum_scatter(
            qkv_weight_sum.astype(jnp.bfloat16), "seq", scatter_dimension=0, tiled=True
        ).astype(jnp.float32),
        lax.psum_scatter(
            out_weight_sum.astype(jnp.bfloat16), "seq", scatter_dimension=0, tiled=True
        ).astype(jnp.float32),
        lax.psum_scatter(
            small_grads.astype(jnp.bfloat16), "seq", scatter_dimension=0, tiled=True
        ).astype(jnp.float32),
        lax.psum_scatter(
            gate_weight_grad.astype(jnp.bfloat16), "seq", scatter_dimension=0, tiled=True
        ).astype(jnp.float32),
        lax.psum_scatter(
            down_weight_grad.astype(jnp.bfloat16), "seq", scatter_dimension=1, tiled=True
        ).astype(jnp.float32),
    )
    qkv_weight_sum, out_weight_sum, small_grads = (
        lax.psum_scatter(qkv_weight_sum, "wt", scatter_dimension=1, tiled=True),
        lax.psum_scatter(out_weight_sum, "wt", scatter_dimension=1, tiled=True),
        lax.psum_scatter(small_grads, "wt", scatter_dimension=1, tiled=True),
    )
    small_flat = small_grads.reshape(-1)
    piece_len = width // (seq_count * wt_count)
    return (
        layer_out,
        input_grad,
        small_flat[0:piece_len],
        small_flat[piece_len : 2 * piece_len],
        qkv_weight_sum,
        small_flat[2 * piece_len : 5 * piece_len],
        out_weight_sum,
        small_flat[5 * piece_len : 6 * piece_len],
        small_flat[6 * piece_len : 7 * piece_len],
        gate_weight_grad,
        down_weight_grad,
    )


def solution(mesh):
    placed = (
        P("wt", "seq", None),
        P("wt", None),
        P(),
        P(),
        P(None, "wt"),
        P(),
        P(None, "wt"),
        P(),
        P(),
        P(None, None, "wt"),
        P("wt", None),
        P("wt", "seq", None),
    )
    return jax.shard_map(
        per_device,
        mesh=mesh,
        in_specs=placed,
        out_specs=(
            P("wt", "seq", None),
            P("wt", "seq", None),
            P(("seq", "wt")),
            P(("seq", "wt")),
            P("seq", "wt"),
            P(("seq", "wt")),
            P("seq", "wt"),
            P(("seq", "wt")),
            P(("seq", "wt")),
            P("seq", None, "wt"),
            P("wt", "seq"),
        ),
        check_vma=False,
    )
```

profile of v0, /device:TPU:1, one launch (start us, length us, event | category | flops | bytes accessed | tf_op | source)
XLA Modules:
  0.0 2876.6 jit_solution(10598120552359273494)
XLA Ops:
  11.6 484.3 %all-gather.8.cloned.1.call-done = bf16[2048,6144]{1,0:T(8,128)(2,1)} async-done(((bf16[2048,768]{1,0:T(8,128)(2,1)}), bf16[2048,6144]{1,0:T(8,128)(2,1)}) %all-gather.8.cloned.1.call-update) | async-done | bytes 25165840 | tf_op jit(solution)/shard_map/all_gather | solution.py:142
  495.9 13.5 convolution_add_fusion
  514.0 7.5 all-to-all-start
  525.6 47.0 %all-to-all-done = bf16[128,3,16,128]{0,3,1,2:T(8,128)(2,1)S(1)} async-done(((bf16[128,3,16,128]{0,3,1,2:T(8,128)(2,1)}), bf16[128,3,16,128]{0,3,1,2:T(8,128)(2,1)S(1)}, u32[]{:S(2)}, u32[]{:S(2)}) %all-to-all-start) | async-done | bytes 1572896 | tf_op jit(solution)/shard_map/all_to_all | solution.py:154
  610.7 17.6 all-to-all-done.1
  636.2 53.0 %all-gather.10.cloned.1.call-done = bf16[2048,2048]{1,0:T(8,128)(2,1)} async-done(((bf16[2048,256]{1,0:T(8,128)(2,1)}), bf16[2048,2048]{1,0:T(8,128)(2,1)}) %all-gather.10.cloned.1.call-update) | async-done | bytes 8388624 | tf_op jit(solution)/shard_map/all_gather | solution.py:189
  689.2 5.1 fusion.174
  696.4 876.1 %all-gather.12.cloned.1.call-done = bf16[2048,2,5632]{0,2,1:T(8,128)(2,1)} async-done(((bf16[2048,2,704]{0,2,1:T(8,128)(2,1)}), bf16[2048,2,5632]{0,2,1:T(8,128)(2,1)}) %all-gather.12.cloned.1.call-update) | async-done | bytes 46137360 | tf_op jit(solution)/shard_map/all_gather | solution.py:198
  1572.5 23.0 fusion.137
  1595.5 423.2 %all-gather.14.cloned.1.call-done = bf16[5632,2048]{1,0:T(8,128)(2,1)} async-done(((bf16[704,2048]{1,0:T(8,128)(2,1)}), bf16[5632,2048]{1,0:T(8,128)(2,1)}) %all-gather.14.cloned.1.call-update) | async-done | bytes 23068688 | tf_op jit(solution)/shard_map/all_gather | solution.py:204
  2018.6 15.1 fusion.79
  2033.7 20.4 multiply_reduce_fusion.4
  2056.4 6.7 fusion.91
  2064.1 7.2 all-to-all-start.2
  2071.4 7.0 convolution_convert_fusion.1
  2078.4 16.1 all-to-all-done.2
  2164.8 71.1 %all_to_all.72 = bf16[2048,3,1,128]{3,1,2,0:T(4,128)(2,1)S(1)} all-to-all(bf16[2048,3,1,128]{3,1,2,0:T(4,128)(2,1)S(1)} %pad_maximum_fusion.1), channel_id=1, replica_groups=mesh['seq'=16,'wt'=8] {'seq'}, dimensions={0} | all-to-all | bytes 3145728 | tf_op jit(solution)/shard_map/all_to_all | solution.py:290
  2243.8 14.3 convolution_convert_fusion
  2265.1 9.5 copy.108
  2274.6 74.3 %all_to_all.73 = bf16[128,3,5632]{0,1,2:T(4,128)(2,1)S(1)} all-to-all(bf16[128,3,5632]{0,1,2:T(4,128)(2,1)} %copy.108), channel_id=1, replica_groups=mesh['seq'=16,'wt'=8] {'wt'}, dimensions={2} | all-to-all | bytes 8650752 | tf_op jit(solution)/shard_map/all_to_all | solution.py:221
  2352.9 7.5 fusion.15
  2365.1 10.6 convolution_convert_fusion.2
  2375.7 8.4 copy.121
  2384.2 10.3 reduce-scatter.16.cloned.1.call-done
  2397.0 191.4 %reduce-scatter.12.cloned.1.call-done = bf16[128,6144]{1,0:T(8,128)(2,1)} async-done(((bf16[2048,6144]{1,0:T(8,128)(2,1)}), bf16[128,6144]{1,0:T(8,128)(2,1)}) %reduce-scatter.12.cloned.1.call-update) | async-done | bytes 1572880 | tf_op jit(solution)/shard_map/reduce_scatter | solution.py:324
  2593.2 13.8 fusion.67
  2607.0 15.2 fusion.118
  2622.7 60.8 %all-reduce.2 = bf16[16,8,112]{2,1,0:T(8,128)(2,1)S(1)} all-reduce(bf16[16,8,112]{2,1,0:T(8,128)(2,1)S(1)} %concatenate.79), channel_id=3, replica_groups=mesh['seq'=16,'wt'=8] {'seq'}, use_global_device_ids=true, to_apply=%region_26.27.clone | all-reduce | flops 14336 | bytes 57344
  2684.1 15.2 all-reduce.3
  2705.5 49.8 %reduce-scatter.20.cloned.1.call-done = bf16[128,1408]{1,0:T(8,128)(2,1)} async-done(((bf16[2048,1408]{1,0:T(8,128)(2,1)}), bf16[128,1408]{1,0:T(8,128)(2,1)}) %reduce-scatter.20.cloned.1.call-update) | async-done | bytes 360464
  2757.5 35.2 %reduce-scatter.18.cloned.1.call-done = f32[128,256]{1,0:T(8,128)} async-done(((f32[128,2048]{1,0:T(8,128)}), f32[128,256]{1,0:T(8,128)}) %reduce-scatter.18.cloned.1.call-update) | async-done | bytes 131088 | tf_op jit(solution)/shard_map/reduce_scatter | solution.py:342
  2792.7 76.8 %reduce-scatter.14.cloned.1.call-done = f32[128,768]{1,0:T(8,128)} async-done(((f32[128,6144]{1,0:T(8,128)}), f32[128,768]{1,0:T(8,128)}) %reduce-scatter.14.cloned.1.call-update) | async-done | bytes 393232 | tf_op jit(solution)/shard_map/reduce_scatter | solution.py:341
  (290 shorter events, 173.8 us)
Async XLA Ops:
  7.2 488.7 %all-gather.8.cloned.1.call-start = ((), (), s32[]{:S(2)}) async-start(), calls=%async_computation.11 | async-start | bytes 28311552 | tf_op jit(solution)/shard_map/all_gather | solution.py:142
  7.9 681.3 %all-gather.10.cloned.1.call-start = ((), (), s32[]{:S(2)}) async-start(), calls=%async_computation.12 | async-start | bytes 9437184 | tf_op jit(solution)/shard_map/all_gather | solution.py:189
  8.7 1563.8 %all-gather.12.cloned.1.call-start = ((), (), s32[]{:S(2)}) async-start(), calls=%async_computation.13 | async-start | bytes 51904512 | tf_op jit(solution)/shard_map/all_gather | solution.py:198
  9.4 486.5 %copy-start.35 = (f32[2048]{0:T(1024)S(1)}, f32[2048]{0:T(1024)}, u32[]{:S(2)}) copy-start(f32[2048]{0:T(1024)} %param.34) | copy-start | bytes 24580
  9.4 486.4 %copy-start.37 = (f32[2048]{0:T(1024)S(1)}, f32[2048]{0:T(1024)}, u32[]{:S(2)}) copy-start(f32[2048]{0:T(1024)} %param.35) | copy-start | bytes 24580
  9.4 486.4 %copy-start.50 = (f32[6144]{0:T(1024)S(1)}, f32[6144]{0:T(1024)}, u32[]{:S(2)}) copy-start(f32[6144]{0:T(1024)} %param.37) | copy-start | bytes 73732
  9.5 2009.2 %all-gather.14.cloned.1.call-start = ((), (), s32[]{:S(2)}) async-start(), calls=%async_computation.14 | async-start | bytes 25952256 | tf_op jit(solution)/shard_map/all_gather | solution.py:204
  10.0 2342.9 %all-gather.18.cloned.1.call-start = ((), (), s32[]{:S(2)}) async-start(), calls=%async_computation.20 | async-start | bytes 4718592 | tf_op jit(solution)/shard_map/all_gather | solution.py:218
  10.9 498.5 %copy-start.45 = (f32[128]{0:T(128)}, f32[128]{0:T(128)S(1)}, u32[]{:S(2)}) copy-start(f32[128]{0:T(128)S(1)} %broadcast_multiply_fusion.5) | copy-start | bytes 1540
  11.2 498.2 %copy-start.48 = (f32[128]{0:T(128)}, f32[128]{0:T(128)S(1)}, u32[]{:S(2)}) copy-start(f32[128]{0:T(128)S(1)} %add_rsqrt_fusion.1) | copy-start | bytes 1540
  11.6 500.7 %copy-start.41 = (f32[128,8]{0,1:T(8,128)}, f32[128,8]{0,1:T(8,128)S(1)}, u32[]{:S(2)}) copy-start(f32[128,8]{0,1:T(8,128)S(1)} %get-tuple-element.159) | copy-start | bytes 12292
  11.6 500.7 %copy-start.43 = (f32[128,8]{0,1:T(8,128)}, f32[128,8]{0,1:T(8,128)S(1)}, u32[]{:S(2)}) copy-start(f32[128,8]{0,1:T(8,128)S(1)} %get-tuple-element.160) | copy-start | bytes 12292
  514.0 58.6 %all-to-all-start = ((bf16[128,3,16,128]{0,3,1,2:T(8,128)(2,1)}), bf16[128,3,16,128]{0,3,1,2:T(8,128)(2,1)S(1)}, u32[]{:S(2)}, u32[]{:S(2)}) async-start(bf16[128,3,16,128]{0,3,1,2:T(8,128)(2,1)} %copy.90), calls=%async_computation | async-start | bytes 3145728 | tf_op jit(solution)/shard_map/all_to_all | solution.py:154
  525.6 53.5 %copy-start.8 = (pred[512,1536]{1,0:T(8,128)(4,1)}, pred[512,1536]{1,0:T(8,128)(4,1)S(1)}, u32[]{:S(2)}) copy-start(pred[512,1536]{1,0:T(8,128)(4,1)S(1)} %fusion.22) | copy-start | bytes 2359300
  579.1 15.9 copy-start.1
  605.7 22.6 all-to-all-start.1
  610.6 1754.6 %all-gather.16.cloned.1.call-start = ((), (), s32[]{:S(2)}) async-start(), calls=%async_computation.19 | async-start | bytes 4718592 | tf_op jit(solution)/shard_map/all_gather | solution.py:217
  2064.1 30.4 %all-to-all-start.2 = ((bf16[128,16,128]{2,0,1:T(8,128)(2,1)}), bf16[128,16,128]{2,0,1:T(8,128)(2,1)}, u32[]{:S(2)}, u32[]{:S(2)}) async-start(bf16[128,16,128]{2,0,1:T(8,128)(2,1)} %bitcast.397), calls=%async_computation.2 | async-start | bytes 1048576 | tf_op jit(solution)/shard_map/all_to_all | solution.py:238
  2071.3 323.2 %reduce-scatter.16.cloned.1.call-start = ((), (), s32[]{:S(2)}) async-start(), calls=%async_computation.17 | async-start | bytes 8912896 | tf_op jit(solution)/shard_map/reduce_scatter | solution.py:327
  2078.4 27.5 copy-start.27
  2078.4 510.0 %reduce-scatter.12.cloned.1.call-start = ((), (), s32[]{:S(2)}) async-start(), calls=%async_computation.15 | async-start | bytes 26738688 | tf_op jit(solution)/shard_map/reduce_scatter | solution.py:324
  2258.2 445.4 %reduce-scatter.22.cloned.1.call-start = ((), (), s32[]{:S(2)}) async-start(), calls=%async_computation.22 | async-start | bytes 3342336
  2365.1 390.3 %reduce-scatter.20.cloned.1.call-start = ((), (), s32[]{:S(2)}) async-start(), calls=%async_computation.21 | async-start | bytes 6127616
  2384.1 408.5 %reduce-scatter.18.cloned.1.call-start = ((), (), s32[]{:S(2)}) async-start(), calls=%async_computation.18 | async-start | bytes 1179648 | tf_op jit(solution)/shard_map/reduce_scatter | solution.py:342
  2396.7 195.2 %copy-start.55 = (u32[128]{0:T(128)S(1)}, u32[128]{0:T(128)}, u32[]{:S(2)}) copy-start(u32[128]{0:T(128)} %constant.250) | copy-start | bytes 1540
  2396.7 195.7 %copy-start.54 = (u32[128]{0:T(128)S(1)}, u32[128]{0:T(128)}, u32[]{:S(2)}) copy-start(u32[128]{0:T(128)} %constant.254) | copy-start | bytes 1540
  2396.7 196.3 %copy-start.53 = (bf16[2048]{0:T(1024)(128)(2,1)S(1)}, bf16[2048]{0:T(1024)(128)(2,1)}, u32[]{:S(2)}) copy-start(bf16[2048]{0:T(1024)(128)(2,1)} %get-tuple-element.123) | copy-start | bytes 12292
  2396.7 196.4 %copy-start.52 = (bf16[2048]{0:T(1024)(128)(2,1)S(1)}, bf16[2048]{0:T(1024)(128)(2,1)}, u32[]{:S(2)}) copy-start(bf16[2048]{0:T(1024)(128)(2,1)} %get-tuple-element.129) | copy-start | bytes 12292
  2396.7 196.5 %copy-start.24 = (f32[128,2048]{1,0:T(8,128)S(1)}, f32[128,2048]{1,0:T(8,128)}, u32[]{:S(2)}) copy-start(f32[128,2048]{1,0:T(8,128)} %copy-done.23) | copy-start | bytes 3145732
  2396.7 472.8 %reduce-scatter.14.cloned.1.call-start = ((), (), s32[]{:S(2)}) async-start(), calls=%async_computation.16 | async-start | bytes 3538944 | tf_op jit(solution)/shard_map/reduce_scatter | solution.py:341
  2607.0 15.4 copy-start.40
  2607.0 94.1 %copy-start.22 = (f32[128,2048]{1,0:T(8,128)S(1)}, f32[128,2048]{1,0:T(8,128)}, u32[]{:S(2)}) copy-start(f32[128,2048]{1,0:T(8,128)} %copy-done.21) | copy-start | bytes 3145732
  (45 other events, 167.8 us)
Sparse Core Ops, SparseCore 0:
  9.7 486.1 all-gather.7
  497.4 191.7 all-gather.9
  690.9 881.5 all-gather.11
  1574.0 444.6 all-gather.13
  2020.1 96.2 all-gather.17
  2118.5 111.0 all-gather.15
  2233.8 160.6 reduce-scatter.15
  2398.8 189.4 reduce-scatter.11
  2592.4 72.8 reduce-scatter.21
  2669.4 85.9 reduce-scatter.19
  2758.3 34.3 reduce-scatter.17
  2795.5 73.9 reduce-scatter.13
where the time goes:
time: 2880 us
  waiting for transfers between devices  2280 us (79%)
  blocking collectives  221 us (8%)
  matrix products  197 us (7%)
  local copies, waits for them, and re-layouts  88.4 us (3%)
  other arithmetic  49.8 us (2%)
    all_gather x1, waiting for transfers between devices, per_device(): lax.all_gather(gate_up_weight, 'wt', axis=2, tiled=True)  876 us
    all_gather x1, waiting for transfers between devices, per_device(): lax.all_gather(qkv_weight, 'wt', axis=1, tiled=True)  484 us
    all_gather x1, waiting for transfers between devices, per_device(): lax.all_gather(down_weight, 'wt', axis=0, tiled=True)  423 us
    reduce_scatter x1, waiting for transfers between devices, per_device(): lax.psum_scatter(qkv_weight_sum.astype(jnp.bfloat16), 'seq', scatter_dime...  191 us
    reduce_scatter x1, waiting for transfers between devices, per_device(): lax.psum_scatter(qkv_weight_sum, 'wt', scatter_dimension=1, tiled=True)  76.8 us
    unnamed x2, blocking collectives  75.9 us
    all_to_all x1, blocking collectives, per_device(): lax.all_to_all(joined_cols, 'wt', split_axis=2, concat_axis=0, tiled=True)  74.3 us
    all_to_all x1, blocking collectives, per_device(): lax.all_to_all(stacked_grad, 'seq', split_axis=0, concat_axis=2, tiled=True)  71.1 us
  transfers between devices with their start and end apart: 15, of which 12 were waited for; matrix products, arithmetic and copies ran while one was open for 11% of the time, Pallas kernels for 0%

commit v1 on v0

v1 whole, which is shorter than its diff:
```python
import functools, math
import jax, jax.numpy as jnp
from jax import lax
from jax.experimental import pallas as pl
from jax.experimental.pallas import tpu as pltpu
from jax.sharding import PartitionSpec as P

MESH = pl.DeviceIdType.MESH

def coords():
    s = lax.axis_index("seq")
    w = lax.axis_index("wt")
    return s // 8, lax.rem(s // 2, 4), lax.rem(s, 2), w // 2, lax.rem(w, 2)

def at(yh, z, c, x, yl):
    return {"seq": yh * 8 + z * 2 + c, "wt": x * 2 + yl}

class Plane:
    def __init__(self, axis):
        self.axis = axis
        yh, z, c, x, yl = coords()
        self.c = c
        if axis == "wt":
            self.a, self.b = x, yl
            move = lambda da, db: at(yh, z, c, lax.rem(x + da + 4, 4), lax.rem(yl + db, 2))
        else:
            self.a, self.b = z, yh
            move = lambda da, db: at(lax.rem(yh + db, 2), lax.rem(z + da + 4, 4), c, x, yl)
        self.left, self.right, self.pair = move(-1, 0), move(1, 0), move(0, 1)
        self.twin = at(yh, z, 1 - c, x, yl)

    def block(self, da, db):
        a, b = lax.rem(self.a + da + 4, 4), lax.rem(self.b + db, 2)
        return a * 2 + b if self.axis == "wt" else b * 4 + a

def remote(src, dst, ssem, rsem, k, target):
    return pltpu.make_async_remote_copy(src_ref=src, dst_ref=dst, send_sem=ssem.at[k], recv_sem=rsem.at[k], device_id=target, device_id_type=MESH)

def greet(targets):
    bar = pltpu.get_barrier_semaphore()
    for t in targets:
        pl.semaphore_signal(bar, inc=1, device_id=t, device_id_type=MESH)
    pl.semaphore_wait(bar, len(targets))

GATHER_MSGS = 18
def gather_steps(pn, own, buf, rows, ssem, rsem, index=lambda j: j):
    h, q = rows // 2, rows // 4
    P_, Q_ = (0, h), (h, h)
    P0, P1, Q0, Q1 = (0, q), (q, q), (h, q), (h + q, q)
    L, Rt, Y = pn.left, pn.right, pn.pair
    table = {
        0: (Y, (0, 0), P_, (0, 1)),
        1: (Rt, (0, 0), Q_, (-1, 0)),
        2: (L, (0, 0), Q_, (1, 0)),
        3: (Rt, (0, 0), P_, (-1, 0)),
        4: (L, (0, 0), P_, (1, 0)),
        5: (Y, (0, 0), Q_, (0, 1)),
        6: (Rt, (-1, 0), Q0, (2, 0)),
        7: (Y, (-1, 0), Q_, (-1, 1)),
        8: (L, (1, 0), Q1, (2, 0)),
        9: (Y, (1, 0), Q_, (1, 1)),
        10: (Rt, (0, 1), P_, (-1, 1)),
        11: (L, (0, 1), P_, (1, 1)),
        12: (Rt, (-1, 0), P0, (2, 0)),
        13: (L, (1, 0), P1, (2, 0)),
        14: (Y, (2, 0), Q0, (2, 1)),
        15: (Y, (2, 0), Q1, (2, 1)),
        16: (Rt, (-1, 1), P0, (2, 1)),
        17: (L, (1, 1), P1, (2, 1)),
    }
    def part(d, r):
        return buf.at[index(pn.block(*d)), pl.ds(*r)]
    def send(k):
        t, d, r, _ = table[k]
        src = own.at[pl.ds(*r)] if d == (0, 0) else part(d, r)
        remote(src, part(d, r), ssem, rsem, k, t).start()
    def got(k):
        t, _, r, d = table[k]
        remote(part(d, r), part(d, r), ssem, rsem, k, t).wait_recv()
    def sent(k):
        t, d, r, _ = table[k]
        remote(part(d, r), part(d, r), ssem, rsem, k, t).wait_send()
    def first():
        for k in (0, 1, 2, 3, 4, 5): send(k)
    def after(k, *next_):
        def f():
            got(k)
            for n in next_: send(n)
        return f
    steps = [first, after(1, 6, 7), after(2, 8, 9), after(0, 10, 11), after(3, 12), after(4, 13),
             after(6, 14), after(8, 15), after(10, 16), after(11, 17)]
    tail = [after(5), after(7), after(9), after(12), after(13), after(14), after(15), after(16), after(17)]
    def done():
        for k in range(18): sent(k)
    return steps, tail, done

SUM_MSGS = 17
def sum_steps(pn, buf, land, rows, ssem, rsem, out, index=lambda j: j, add=None):
    h, q = rows // 2, rows // 4
    P_, Q_ = (0, h), (h, h)
    P0, P1, Q0, Q1 = (0, q), (q, q), (h, q), (h + q, q)
    L, Rt, Y = pn.left, pn.right, pn.pair
    table = {}
    off = 0
    def msg(k, t, d, r, r_to):
        nonlocal off
        table[k] = (t, d, r, off, r_to)
        off += r[1]
    msg(0, L, (-2, 0), P0, (-1, 0)); msg(1, Rt, (2, 0), P1, (1, 0))
    msg(2, L, (-2, 1), P0, (-1, 1)); msg(3, Rt, (2, 1), P1, (1, 1))
    msg(4, Y, (2, 1), Q_, (2, 0)); msg(5, Y, (-1, 1), Q_, (-1, 0)); msg(6, Y, (1, 1), Q_, (1, 0)); msg(7, Y, (0, 1), Q_, (0, 0))
    msg(8, L, (-1, 1), P_, (0, 1)); msg(9, Rt, (1, 1), P_, (0, 1))
    msg(10, L, (-1, 0), P_, (0, 0)); msg(11, Rt, (1, 0), P_, (0, 0))
    msg(12, L, (-2, 0), Q0, (-1, 0)); msg(13, Rt, (2, 0), Q1, (1, 0))
    msg(14, L, (-1, 0), Q_, (0, 0)); msg(15, Rt, (1, 0), Q_, (0, 0))
    msg(16, Y, (0, 1), P_, (0, 0))
    assert off <= 7 * rows, off
    def part(d, r):
        return buf.at[index(pn.block(*d)), pl.ds(*r)]
    def landing(k):
        _, _, r, o, _ = table[k]
        return land.at[pl.ds(o, r[1])]
    def send(k):
        t, d, r, _, _ = table[k]
        remote(part(d, r), landing(k), ssem, rsem, k, t).start()
    def got(k):
        remote(landing(k), landing(k), ssem, rsem, k, table[k][0]).wait_recv()
    def sent(k):
        remote(landing(k), landing(k), ssem, rsem, k, table[k][0]).wait_send()
    def accumulate(d, r, ks, to=None):
        j = index(pn.block(*d))
        step = 16
        def body(i, _):
            at_ = pl.multiple_of(r[0] + i * step, step)
            v = buf[j, pl.ds(at_, step)].astype(jnp.float32)
            for k in ks:
                v = v + land[pl.ds(pl.multiple_of(table[k][3] + i * step, step), step)].astype(jnp.float32)
            if to is None:
                buf[j, pl.ds(at_, step)] = v.astype(buf.dtype)
            else:
                to[pl.ds(at_, step)] = v.astype(to.dtype)
            return 0
        lax.fori_loop(0, r[1] // step, body, 0)
    def s0():
        for k in range(8): send(k)
    def s1():
        got(2); accumulate((-1, 1), P0, [2]); send(8)
        got(3); accumulate((1, 1), P1, [3]); send(9)
    def s2():
        got(0); accumulate((-1, 0), P0, [0]); send(10)
        got(1); accumulate((1, 0), P1, [1]); send(11)
    def s3():
        got(4); accumulate((2, 0), Q_, [4]); send(12); send(13)
    def s4():
        got(5); accumulate((-1, 0), Q_, [5]); got(12); accumulate((-1, 0), Q0, [12]); send(14)
        got(6); accumulate((1, 0), Q_, [6]); got(13); accumulate((1, 0), Q1, [13]); send(15)
    def s5():
        got(8); got(9); accumulate((0, 1), P_, [8, 9]); send(16)
    def s6():
        got(7); got(14); got(15); accumulate((0, 0), Q_, [7, 14, 15], out)
        got(10); got(11); got(16); accumulate((0, 0), P_, [10, 11, 16], out)
    def done():
        for k in range(17): sent(k)
    return [s0, s1, s2, s3, s4, s5, s6], done
ANY = pl.BlockSpec(memory_space=pl.ANY)
QB, KB = 512, 256
MASKED = -1e30
NT = (((1,), (1,)), ((), ()))

def halves(ref, kept):
    lane = lax.broadcasted_iota(jnp.int32, (1, 128), 1)
    low = (lane < 64).astype(jnp.float32)
    v = ref[...].astype(jnp.float32)
    kept[0] = (v * low).astype(jnp.bfloat16)
    kept[1] = (v * (1.0 - low)).astype(jnp.bfloat16)

def allowed(i, j, start):
    key = j * KB + lax.broadcasted_iota(jnp.int32, (KB, QB), 0)
    query = i * QB + lax.broadcasted_iota(jnp.int32, (KB, QB), 1)
    return (key <= query) & (key >= start)

def attn_fwd(q_ref, k_ref, v_ref, start_ref, o_ref, ot_ref, lse_ref, kept, vt):
    halves(k_ref, kept)
    vt[...] = v_ref[...].astype(jnp.float32).T.astype(jnp.bfloat16)
    n = q_ref.shape[0] // QB
    for i in range(n):
        q = q_ref[QB * i:QB * (i + 1)]
        start = start_ref[:, QB * i:QB * (i + 1)]
        def step(masked, j, carry):
            r = pl.ds(pl.multiple_of(j * KB, KB), KB)
            out = []
            for h in range(2):
                m, l, acc = carry[h]
                s = lax.dot_general(kept[h, r], q, NT, preferred_element_type=jnp.float32)
                if masked:
                    s = jnp.where(allowed(i, j, start), s, MASKED)
                top = jnp.maximum(m, jnp.max(s, axis=0, keepdims=True))
                p = jnp.exp(s - top)
                fade = jnp.exp(m - top)
                l = l * fade + jnp.sum(p, axis=0, keepdims=True)
                acc = acc * fade + jnp.dot(vt[64 * h:64 * h + 64, r], p.astype(jnp.bfloat16), preferred_element_type=jnp.float32)
                out.append((top, l, acc))
            return tuple(out)
        one = (jnp.full((1, QB), MASKED, jnp.float32), jnp.zeros((1, QB), jnp.float32), jnp.zeros((64, QB), jnp.float32))
        carry = (one, one)
        if i == n - 1:
            carry = lax.fori_loop(0, 2 * i + 2, functools.partial(step, True), carry)
        else:
            if i:
                carry = step(True, 0, carry)
                carry = lax.fori_loop(1, 2 * i, functools.partial(step, False), carry)
            carry = lax.fori_loop(2 * i, 2 * i + 2, functools.partial(step, True), carry)
        cols = pl.ds(QB * i, QB)
        for h in range(2):
            m, l, acc = carry[h]
            ot_ref[64 * h:64 * h + 64, cols] = acc / l
            lse_ref[h:h + 1, cols] = m + jnp.log(l)
        o_ref[QB * i:QB * (i + 1)] = ot_ref[:, cols].T.astype(jnp.bfloat16)

def attn_bwd(q_ref, k_ref, v_ref, start_ref, ot_ref, lse_ref, do_ref, dq_ref, dk_ref, dv_ref, keptk, keptv, keptq, keptd, kt, dot_):
    halves(k_ref, keptk)
    halves(v_ref, keptv)
    halves(q_ref, keptq)
    halves(do_ref, keptd)
    kt[...] = k_ref[...].astype(jnp.float32).T.astype(jnp.bfloat16)
    dot_[...] = do_ref[...].astype(jnp.float32).T
    dk_ref[...] = jnp.zeros_like(dk_ref)
    dv_ref[...] = jnp.zeros_like(dv_ref)
    n = q_ref.shape[0] // QB
    for i in range(n):
        rows = pl.ds(QB * i, QB)
        q = q_ref[rows]
        do = do_ref[rows]
        start = start_ref[:, rows]
        both = ot_ref[:, rows] * dot_[:, rows]
        inner = [jnp.sum(both[64 * h:64 * h + 64], axis=0, keepdims=True) for h in range(2)]
        lse = [lse_ref[h:h + 1, rows] for h in range(2)]
        def step(masked, j, carry):
            r = pl.ds(pl.multiple_of(j * KB, KB), KB)
            out, ps, ds = [], [], []
            for h in range(2):
                s = lax.dot_general(keptk[h, r], q, NT, preferred_element_type=jnp.float32)
                if masked:
                    s = jnp.where(allowed(i, j, start), s, MASKED)
                p = jnp.exp(s - lse[h])
                dp = lax.dot_general(keptv[h, r], do, NT, preferred_element_type=jnp.float32)
                g = (p * (dp - inner[h])).astype(jnp.bfloat16)
                out.append(carry[h] + jnp.dot(kt[64 * h:64 * h + 64, r], g, preferred_element_type=jnp.float32))
                ps.append(p.astype(jnp.bfloat16))
                ds.append(g)
            dv_ref[r] += sum(jnp.dot(ps[h], keptd[h, rows], preferred_element_type=jnp.float32) for h in range(2))
            dk_ref[r] += sum(jnp.dot(ds[h], keptq[h, rows], preferred_element_type=jnp.float32) for h in range(2))
            return tuple(out)
        carry = (jnp.zeros((64, QB), jnp.float32),) * 2
        if i == n - 1:
            carry = lax.fori_loop(0, 2 * i + 2, functools.partial(step, True), carry)
        else:
            if i:
                carry = step(True, 0, carry)
                carry = lax.fori_loop(1, 2 * i, functools.partial(step, False), carry)
            carry = lax.fori_loop(2 * i, 2 * i + 2, functools.partial(step, True), carry)
        dq_ref[rows] = jnp.concatenate(carry, axis=0).T

VM = pl.BlockSpec(memory_space=pltpu.VMEM)

def attention_forward(q, k, v, start):
    rows = q.shape[0]
    f = jax.ShapeDtypeStruct
    return pl.pallas_call(
        attn_fwd, out_shape=(f((rows, 128), jnp.bfloat16), f((128, rows), jnp.float32), f((8, rows), jnp.float32)),
        in_specs=[VM] * 4, out_specs=(VM,) * 3,
        scratch_shapes=[pltpu.VMEM((2, rows, 128), jnp.bfloat16), pltpu.VMEM((128, rows), jnp.bfloat16)],
        compiler_params=pltpu.CompilerParams(vmem_limit_bytes=56 * 2**20), name="attend",
    )(q, k, v, start)

def attention_backward(q, k, v, start, ot, lse, do):
    rows = q.shape[0]
    f = jax.ShapeDtypeStruct
    return pl.pallas_call(
        attn_bwd, out_shape=(f((rows, 128), jnp.float32),) * 3,
        in_specs=[VM] * 7, out_specs=(VM,) * 3,
        scratch_shapes=[pltpu.VMEM((2, rows, 128), jnp.bfloat16)] * 4 + [pltpu.VMEM((128, rows), jnp.bfloat16), pltpu.VMEM((128, rows), jnp.float32)],
        compiler_params=pltpu.CompilerParams(vmem_limit_bytes=56 * 2**20), name="attend_back",
    )(q, k, v, start, ot, lse, do)
def params(cid):
    return pltpu.CompilerParams(collective_id=cid, has_side_effects=True, vmem_limit_bytes=56 * 2**20)

def dma(n):
    return pltpu.SemaphoreType.DMA((n,))

def gather_kernel(axis, x, o, ss, rs, ls):
    pn = Plane(axis)
    greet([pn.left, pn.right, pn.pair])
    cp = pltpu.make_async_copy(x, o.at[pn.block(0, 0)], ls)
    cp.start()
    steps, tail, done = gather_steps(pn, x, o, x.shape[0], ss, rs)
    for f in steps + tail:
        f()
    done()
    cp.wait()

def gather(axis, cid, x):
    return pl.pallas_call(
        functools.partial(gather_kernel, axis), out_shape=jax.ShapeDtypeStruct((8,) + x.shape, x.dtype),
        in_specs=[VM], out_specs=VM, scratch_shapes=[dma(18), dma(18), pltpu.SemaphoreType.DMA],
        compiler_params=params(cid), name="gather_" + axis)(x)

def gather_both_kernel(axis, x, o, ss, rs, ls, ts, tr):
    pn = Plane(axis)
    greet([pn.left, pn.right, pn.pair, pn.twin])
    index = lambda j: 2 * j + pn.c
    mine = index(pn.block(0, 0))
    cp = pltpu.make_async_copy(x, o.at[mine], ls)
    cp.start()
    cp.wait()
    steps, tail, done = gather_steps(pn, x, o, x.shape[0], ss, rs, index)
    order = [(0, 0), (0, 1), (-1, 1), (1, 1), (-1, 0), (1, 0), (2, 0), (2, 1)]
    def hand(k):
        j = index(pn.block(*order[k]))
        remote(o.at[j], o.at[j], ts, tr, k, pn.twin).start()
    steps[0]()
    hand(0)
    for f in steps[1:]:
        f()
    ready = {0: [1], 1: [2], 2: [3], 3: [4], 4: [5], 6: [6], 8: [7]}
    for i, f in enumerate(tail):
        f()
        for k in ready.get(i, []):
            hand(k)
    done()
    for k in range(8):
        j = 2 * pn.block(*order[k]) + 1 - pn.c
        remote(o.at[j], o.at[j], ts, tr, k, pn.twin).wait()

def gather_both(axis, cid, x):
    return pl.pallas_call(
        functools.partial(gather_both_kernel, axis), out_shape=jax.ShapeDtypeStruct((16,) + x.shape, x.dtype),
        in_specs=[VM], out_specs=VM, scratch_shapes=[dma(18), dma(18), pltpu.SemaphoreType.DMA, dma(8), dma(8)],
        compiler_params=params(cid), name="gather_both_" + axis)(x)

def scatter_kernel(axis, x, o, buf, land, ss, rs, ls):
    pn = Plane(axis)
    cp = pltpu.make_async_copy(x, buf, ls)
    cp.start()
    greet([pn.left, pn.right, pn.pair])
    cp.wait()
    steps, done = sum_steps(pn, buf, land, x.shape[1], ss, rs, o)
    for f in steps:
        f()
    done()

def scatter(axis, cid, x):
    _, rows, cols = x.shape
    return pl.pallas_call(
        functools.partial(scatter_kernel, axis), out_shape=jax.ShapeDtypeStruct((rows, cols), jnp.float32),
        in_specs=[ANY], out_specs=VM,
        scratch_shapes=[pltpu.VMEM(x.shape, x.dtype), pltpu.VMEM((7 * rows, cols), x.dtype), dma(17), dma(17), pltpu.SemaphoreType.DMA],
        compiler_params=params(cid), name="scatter_" + axis)(x)

def scatter_both_kernel(axis, x, o, buf, tland, land, ss, rs, ls, ts, tr):
    pn = Plane(axis)
    rows = x.shape[1]
    cp = pltpu.make_async_copy(x, buf, ls)
    cp.start()
    greet([pn.left, pn.right, pn.pair, pn.twin])
    cp.wait()
    order = [(2, 0), (2, 1), (-1, 1), (1, 1), (-1, 0), (1, 0), (0, 1), (0, 0)]
    for k in range(8):
        j = pn.block(*order[k])
        remote(buf.at[2 * j + 1 - pn.c], tland.at[k], ts, tr, k, pn.twin).start()
    for k in range(8):
        j = 2 * pn.block(*order[k]) + pn.c
        remote(tland.at[k], tland.at[k], ts, tr, k, pn.twin).wait_recv()
        def body(i, _):
            r = pl.ds(pl.multiple_of(i * 16, 16), 16)
            buf[j, r] = (buf[j, r].astype(jnp.float32) + tland[k, r].astype(jnp.float32)).astype(buf.dtype)
            return 0
        lax.fori_loop(0, rows // 16, body, 0)
    steps, done = sum_steps(pn, buf, land, rows, ss, rs, o, lambda j: 2 * j + pn.c)
    for f in steps:
        f()
    done()
    for k in range(8):
        remote(tland.at[k], tland.at[k], ts, tr, k, pn.twin).wait_send()

def scatter_both(axis, cid, x):
    _, rows, cols = x.shape
    return pl.pallas_call(
        functools.partial(scatter_both_kernel, axis), out_shape=jax.ShapeDtypeStruct((rows, cols), jnp.float32),
        in_specs=[ANY], out_specs=VM,
        scratch_shapes=[pltpu.VMEM(x.shape, x.dtype), pltpu.VMEM((8, rows, cols), x.dtype), pltpu.VMEM((7 * rows, cols), x.dtype),
                        dma(17), dma(17), pltpu.SemaphoreType.DMA, dma(8), dma(8)],
        compiler_params=params(cid), name="scatter_both_" + axis)(x)

def swap_kernel(axis, n, x, o, ss, rs, ls):
    me = lax.axis_index(axis)
    peers = [lax.rem(me + d, n) for d in range(1, n)]
    bar = pltpu.get_barrier_semaphore()
    for p in peers:
        pl.semaphore_signal(bar, inc=1, device_id={axis: p}, device_id_type=MESH)
    cp = pltpu.make_async_copy(x.at[me], o.at[me], ls)
    cp.start()
    pl.semaphore_wait(bar, n - 1)
    def copy(d):
        return remote(x.at[lax.rem(me + d, n)], o.at[me], ss, rs, d - 1, {axis: lax.rem(me + d, n)})
    for d in range(1, n):
        copy(d).start()
    for d in range(1, n):
        j = lax.rem(me - d + n, n)
        remote(x.at[j], o.at[j], ss, rs, d - 1, {axis: j}).wait()
    cp.wait()

def swap(axis, n, cid, x):
    return pl.pallas_call(
        functools.partial(swap_kernel, axis, n), out_shape=jax.ShapeDtypeStruct(x.shape, x.dtype),
        in_specs=[VM], out_specs=VM, scratch_shapes=[dma(n - 1), dma(n - 1), pltpu.SemaphoreType.DMA],
        compiler_params=params(cid), name="swap_" + axis)(x)

def fetch_kernel(x, o, ss, rs, ls):
    s, w = lax.axis_index("seq"), lax.axis_index("wt")
    bar = pltpu.get_barrier_semaphore()
    for d in range(1, 8):
        pl.semaphore_signal(bar, inc=1, device_id={"wt": lax.rem(w + d, 8)}, device_id_type=MESH)
    pl.semaphore_wait(bar, 7)
    for p in range(3):
        g = 16 * p + s
        @pl.when(w == g // 6)
        def _():
            src = x.at[lax.rem(g, 6)]
            cp = pltpu.make_async_copy(src, o.at[p], ls)
            cp.start()
            for d in range(1, 8):
                remote(src, o.at[p], ss.at[p], rs, p, {"wt": lax.rem(w + d, 8)}).start() if False else pltpu.make_async_remote_copy(src_ref=src, dst_ref=o.at[p], send_sem=ss.at[p, d - 1], recv_sem=rs.at[p], device_id={"wt": lax.rem(w + d, 8)}, device_id_type=MESH).start()
            cp.wait()
    for p in range(3):
        g = 16 * p + s
        @pl.when(w == g // 6)
        def _():
            for d in range(1, 8):
                pltpu.make_async_remote_copy(src_ref=o.at[p], dst_ref=o.at[p], send_sem=ss.at[p, d - 1], recv_sem=rs.at[p], device_id={"wt": lax.rem(w + d, 8)}, device_id_type=MESH).wait_send()
        @pl.when(w != g // 6)
        def _():
            pltpu.make_async_remote_copy(src_ref=o.at[p], dst_ref=o.at[p], send_sem=ss.at[p, 0], recv_sem=rs.at[p], device_id={"wt": lax.rem(w + 1, 8)}, device_id_type=MESH).wait_recv()

def fetch(cid, x):
    return pl.pallas_call(
        fetch_kernel, out_shape=jax.ShapeDtypeStruct((3,) + x.shape[1:], x.dtype),
        in_specs=[VM], out_specs=VM, scratch_shapes=[pltpu.SemaphoreType.DMA((3, 7)), dma(3), pltpu.SemaphoreType.DMA],
        compiler_params=params(cid), name="fetch_heads")(x)

def place_kernel(x, o, ss, rs, ls):
    s, w = lax.axis_index("seq"), lax.axis_index("wt")
    bar = pltpu.get_barrier_semaphore()
    def source(b):
        g = 6 * w + b
        return lax.rem(g, 16), s // 2
    def target(i, p):
        g = 16 * p + s
        return 2 * w + i, g // 6, lax.rem(g, 6)
    own = jnp.int32(0)
    for b in range(6):
        ts, tw = source(b)
        same = (ts == s) & (tw == w)
        own += same.astype(jnp.int32)
        @pl.when(jnp.logical_not(same))
        def _():
            pl.semaphore_signal(bar, inc=1, device_id={"seq": ts, "wt": tw}, device_id_type=MESH)
    pl.semaphore_wait(bar, 6 - own)
    def copy(i, p):
        ts, tw, slot = target(i, p)
        return pltpu.make_async_remote_copy(src_ref=x.at[i, p], dst_ref=o.at[slot], send_sem=ss.at[i, p], recv_sem=rs.at[slot], device_id={"seq": ts, "wt": tw}, device_id_type=MESH)
    def local(i, p):
        return pltpu.make_async_copy(x.at[i, p], o.at[target(i, p)[2]], ls.at[i, p])
    for i in range(2):
        for p in range(3):
            ts, tw, _ = target(i, p)
            same = (ts == s) & (tw == w)
            @pl.when(same)
            def _():
                local(i, p).start()
            @pl.when(jnp.logical_not(same))
            def _():
                copy(i, p).start()
    for i in range(2):
        for p in range(3):
            ts, tw, _ = target(i, p)
            same = (ts == s) & (tw == w)
            @pl.when(same)
            def _():
                local(i, p).wait()
            @pl.when(jnp.logical_not(same))
            def _():
                copy(i, p).wait_send()
    for b in range(6):
        ts, tw = source(b)
        @pl.when(jnp.logical_not((ts == s) & (tw == w)))
        def _():
            pltpu.make_async_remote_copy(src_ref=o.at[b], dst_ref=o.at[b], send_sem=ss.at[0, 0], recv_sem=rs.at[b], device_id={"seq": ts, "wt": tw}, device_id_type=MESH).wait_recv()

def place(cid, x):
    return pl.pallas_call(
        place_kernel, out_shape=jax.ShapeDtypeStruct((6, 128, 128), x.dtype),
        in_specs=[VM], out_specs=VM, scratch_shapes=[pltpu.SemaphoreType.DMA((2, 3)), dma(6), pltpu.SemaphoreType.DMA((2, 3))],
        compiler_params=params(cid), name="place_qkv")(x)

def small_kernel(x, o, land, mid, land2, ss, rs, ss2, rs2):
    s, w = lax.axis_index("seq"), lax.axis_index("wt")
    bar = pltpu.get_barrier_semaphore()
    for d in range(1, 8):
        pl.semaphore_signal(bar, inc=1, device_id={"wt": lax.rem(w + d, 8)}, device_id_type=MESH)
    for d in range(1, 16):
        pl.semaphore_signal(bar, inc=1, device_id={"seq": lax.rem(s + d, 16)}, device_id_type=MESH)
    pl.semaphore_wait(bar, 22)
    for d in range(1, 8):
        remote(x.at[lax.rem(w + d, 8)], land.at[d - 1], ss, rs, d - 1, {"wt": lax.rem(w + d, 8)}).start()
    for d in range(1, 8):
        remote(x.at[0], land.at[d - 1], ss, rs, d - 1, {"wt": lax.rem(w + d, 8)}).wait()
    mid[:, 0] = x[w] + jnp.sum(land[...], axis=0)
    for d in range(1, 16):
        remote(mid.at[lax.rem(s + d, 16)], land2.at[d - 1], ss2, rs2, d - 1, {"seq": lax.rem(s + d, 16)}).start()
    for d in range(1, 16):
        remote(mid.at[0], land2.at[d - 1], ss2, rs2, d - 1, {"seq": lax.rem(s + d, 16)}).wait()
    o[...] = mid[s] + jnp.sum(land2[...], axis=0)

def small_sum(cid, x):
    f = jnp.float32
    return pl.pallas_call(
        small_kernel, out_shape=jax.ShapeDtypeStruct((1, 128), f),
        in_specs=[VM], out_specs=VM,
        scratch_shapes=[pltpu.VMEM((7, 16, 128), f), pltpu.VMEM((16, 1, 128), f), pltpu.VMEM((15, 1, 128), f), dma(7), dma(7), dma(15), dma(15)],
        compiler_params=params(cid), name="small_sum")(x)


norm_eps = 1e-05
theta_base = 10000.0
ROT = 16
HEAD_DIM = 64


def layer_norm_parts(values, gain, shift):
    average = jnp.mean(values, axis=-1, keepdims=True)
    centred = values - average
    spread = jnp.mean(centred * centred, axis=-1, keepdims=True)
    inverse = lax.rsqrt(spread + norm_eps)
    scaled = centred * inverse
    return (scaled * gain + shift, scaled, inverse)


def layer_norm_back(upward, scaled, inverse, gain):
    weighted = upward * gain
    first_mean = jnp.mean(weighted, axis=-1, keepdims=True)
    second_mean = jnp.mean(weighted * scaled, axis=-1, keepdims=True)
    return inverse * (weighted - first_mean - scaled * second_mean)


def rotary_tables(segment_row):
    rows = segment_row.shape[0]
    ends = [jnp.sum((segment_row < i).astype(jnp.int32)) for i in (1, 2)]
    start = jnp.where(segment_row == 0, 0, jnp.where(segment_row == 1, ends[0], ends[1]))
    offsets = (jnp.arange(rows, dtype=jnp.int32) - start).astype(jnp.float32)
    inv_freq = jnp.exp(jnp.arange(ROT // 2, dtype=jnp.float32) * (-2.0 * math.log(theta_base) / ROT))
    angles = offsets[:, None] * inv_freq[None, :]
    c, s = jnp.cos(angles), jnp.sin(angles)
    one, nil = jnp.ones((rows, 48), jnp.float32), jnp.zeros((rows, 56), jnp.float32)
    z8 = jnp.zeros((rows, 8), jnp.float32)
    keep = jnp.concatenate([c, c, one] * 2, axis=1)
    ahead = jnp.concatenate([-s, nil] * 2, axis=1)
    behind = jnp.concatenate([z8, s, nil[:, :48]] * 2, axis=1)
    return start, keep, ahead, behind


def rotate(v, keep, ahead, behind):
    return v * keep + jnp.roll(v, -8, axis=1) * ahead + jnp.roll(v, 8, axis=1) * behind


def contract_first(left, right):
    return lax.dot_general(left, right, (((0,), (0,)), ((), ())), preferred_element_type=jnp.float32)


def contract_last(left, right):
    return lax.dot_general(left, right, (((1,), (1,)), ((), ())), preferred_element_type=jnp.float32)


def per_device(layer_in, segment_ids, norm_one_gain, norm_one_shift, qkv_weight, qkv_bias, out_weight, norm_two_gain,
               norm_two_shift, gate_up_weight, down_weight, layer_grad):
    f32, bf16 = jnp.float32, jnp.bfloat16
    s, w = lax.axis_index("seq"), lax.axis_index("wt")
    tok, width = layer_in.shape[1:]
    rows = segment_ids.shape[1]
    hidden = down_weight.shape[0]
    scale = 1.0 / math.sqrt(HEAD_DIM)
    inputs = layer_in.reshape(tok, width).astype(f32)
    upstream = layer_grad.reshape(tok, width)
    start, keep, ahead, behind = rotary_tables(segment_ids.reshape(rows))
    start = start.reshape(1, rows)
    normed_one, scaled_one, inverse_one = layer_norm_parts(inputs, norm_one_gain, norm_one_shift)
    row_normed = gather_both("seq", 0, normed_one.astype(bf16)).reshape(rows, width)
    head_weight = fetch(1, qkv_weight.reshape(width, 6, 128).transpose(1, 0, 2))
    head_weight = head_weight.transpose(1, 0, 2).reshape(width, 384)
    bias = lax.dynamic_index_in_dim(qkv_bias.reshape(3, 16, 128), s, 1, keepdims=False).reshape(384)
    proj = jnp.dot(row_normed, head_weight, preferred_element_type=f32) + bias
    q = (rotate(proj[:, :128], keep, ahead, behind) * scale).astype(bf16)
    k = rotate(proj[:, 128:256], keep, ahead, behind).astype(bf16)
    v = proj[:, 256:].astype(bf16)
    o, ot, lse = attention_forward(q, k, v, start)
    attended = swap("seq", 16, 2, o.reshape(16, tok, 128)).transpose(1, 0, 2).reshape(tok, width)
    half = lax.dynamic_slice_in_dim(out_weight, (s % 2) * (width // 2), width // 2, 0)
    out_all = gather_both("wt", 3, half).reshape(8, 2, width // 2, 256)
    branch = jnp.einsum("tck,wckn->twn", attended.reshape(tok, 2, width // 2), out_all, preferred_element_type=f32).reshape(tok, width)
    middle = inputs + branch
    normed_two, scaled_two, inverse_two = layer_norm_parts(middle, norm_two_gain, norm_two_shift)
    all_two = gather("wt", 4, normed_two.astype(bf16)).reshape(8 * tok, width)
    all_up = gather("wt", 5, upstream).reshape(8 * tok, width)
    weight_gu = gate_up_weight.reshape(width, 2 * hidden)
    gu = jnp.dot(all_two, weight_gu, preferred_element_type=f32)
    g, u = gu[:, :hidden], gu[:, hidden:]
    sigma = jax.nn.sigmoid(g)
    act = (g * sigma * u).astype(bf16)
    ffn_part = jnp.dot(act, down_weight, preferred_element_type=f32).astype(bf16)
    dact = contract_last(all_up, down_weight)
    dg = (dact * u * sigma * (1.0 + g * (1.0 - sigma))).astype(bf16)
    du = (dact * g * sigma).astype(bf16)
    dgu = jnp.concatenate([dg, du], axis=1)
    dh2_part = contract_last(dgu, weight_gu).astype(bf16)
    dh2 = scatter("wt", 6, dh2_part.reshape(8, tok, width))
    ffn_out = scatter("wt", 7, ffn_part.reshape(8, tok, width))
    layer_out = (middle + ffn_out).astype(bf16).reshape(1, tok, width)
    gain_two = jnp.sum(dh2 * scaled_two, axis=0)
    shift_two = jnp.sum(dh2, axis=0)
    middle_grad = upstream.astype(f32) + layer_norm_back(dh2, scaled_two, inverse_two, norm_two_gain)
    da = middle_grad.astype(bf16)
    dout = jnp.einsum("twn,wckn->tck", da.reshape(tok, 8, 256), out_all, preferred_element_type=f32).astype(bf16)
    do = swap("seq", 16, 8, dout.reshape(tok, 16, 128).transpose(1, 0, 2)).reshape(rows, 128)
    dq, dk, dv = attention_backward(q, k, v, start, ot, lse, do)
    low = lambda t: t.astype(bf16).astype(f32)
    dproj = jnp.concatenate([rotate(low(dq) * scale, keep, -ahead, -behind), rotate(low(dk), keep, -ahead, -behind), dv], axis=1).astype(bf16)
    dh1_part = contract_last(dproj, head_weight).astype(bf16)
    dh1 = scatter_both("seq", 9, dh1_part.reshape(16, tok, width))
    gain_one = jnp.sum(dh1 * scaled_one, axis=0)
    shift_one = jnp.sum(dh1, axis=0)
    dx = middle_grad + layer_norm_back(dh1, scaled_one, inverse_one, norm_one_gain)
    input_grad = dx.astype(bf16).reshape(1, tok, width)
    qkv_part = contract_first(row_normed, dproj).astype(bf16)
    qkv_rows = scatter("wt", 10, qkv_part.reshape(8, 256, 384)).astype(bf16)
    qkv_grad = place(11, qkv_rows.reshape(2, 128, 3, 128).transpose(0, 2, 1, 3))
    qkv_grad = qkv_grad.transpose(1, 0, 2).reshape(128, 768).astype(f32)
    all_att = gather("wt", 12, attended).reshape(8 * tok, width)
    da_cols = swap("wt", 8, 13, da.reshape(tok, 8, 256).transpose(1, 0, 2)).reshape(8 * tok, 256)
    out_part = contract_first(all_att, da_cols).astype(bf16)
    gate_part = contract_first(all_two, dgu).astype(bf16)
    down_part = contract_first(all_up, act).astype(bf16)
    joined = jnp.concatenate([gate_part, down_part, out_part], axis=1).reshape(16, 128, 3 * hidden + 256)
    joined = scatter_both("seq", 14, joined)
    gate_grad = joined[:, :2 * hidden].reshape(128, 2, hidden)
    down_grad = joined[:, 2 * hidden:3 * hidden].T
    out_grad = joined[:, 3 * hidden:]
    bias_grad = lax.dynamic_update_slice(jnp.zeros((3, 16, 128), f32), jnp.sum(dproj.astype(f32), axis=0).reshape(3, 1, 128), (0, s, 0))
    blocks = [t.reshape(16, 8, -1) for t in (gain_one, shift_one, bias_grad, gain_two, shift_two, jnp.zeros((16 * 8 * 16,), f32))]
    small = small_sum(15, jnp.concatenate(blocks, axis=2).transpose(1, 0, 2))[0]
    return (layer_out, input_grad, small[0:16], small[16:32], qkv_grad, small[32:80], out_grad, small[80:96], small[96:112], gate_grad, down_grad)


def solution(mesh):
    both = P(("seq", "wt"))
    return jax.shard_map(
        per_device, mesh=mesh,
        in_specs=(P("wt", "seq", None), P("wt", None), P(), P(), P(None, "wt"), P(), P(None, "wt"), P(), P(), P(None, None, "wt"), P("wt", None), P("wt", "seq", None)),
        out_specs=(P("wt", "seq", None), P("wt", "seq", None), both, both, P("seq", "wt"), both, P("seq", "wt"), both, both, P("seq", None, "wt"), P("wt", "seq")),
        check_vma=False)
```

time: 2880 us -> 786 us (0.27)
  waiting for transfers between devices: 2280 us -> 0 us
  Pallas kernels: 0 us -> 551 us
  blocking collectives: 221 us -> 0 us
  matrix products: 197 us -> 89.2 us
    all_gather x6 -> x0, waiting for transfers between devices: 1840 us -> none  [the longest x1 876 us: per_device(): lax.all_gather(gate_up_weight, 'wt', axis=2, tiled=True)]
    pallas_call x0 -> x18, Pallas kernels: none -> 551 us  [the longest x3 108 us: gather(): pl.pallas_call(functools.partial(gather_kernel, axis), out_shape=jax.Shap...]
    reduce_scatter x4 -> x0, waiting for transfers between devices: 314 us -> none  [the longest x1 191 us: per_device(): lax.psum_scatter(qkv_weight_sum.astype(jnp.bfloat16), 'seq', scatter_dime...]
    all_to_all x2 -> x0, blocking collectives: 145 us -> none  [the longest x1 74.3 us: per_device(): lax.all_to_all(joined_cols, 'wt', split_axis=2, concat_axis=0, tiled=True)]
    dot_general x30 -> x5, matrix products: 131 us -> 37 us  [the longest x1 11.8 us: per_device(): gu = jnp.dot(all_two, weight_gu, preferred_element_type=f32)]
    all_to_all x3 -> x0, waiting for transfers between devices: 80.7 us -> none  [the longest x1 47 us: per_device(): lax.all_to_all(stacked, 'seq', split_axis=2, concat_axis=0, tiled=True)]
    unnamed x2 -> x0, blocking collectives: 75.9 us -> none
    unnamed x14 -> x0, waiting for transfers between devices: 53.1 us -> none
  transfers between devices with their start and end apart: 15 -> 0, of which waited for: 12 -> 0; matrix products, arithmetic and copies ran while one was open for 11% -> 0% of each run, Pallas kernels for 0% -> 0%
where the time goes in v1:
time: 786 us; the launch traced here: 781 us
  Pallas kernels  551 us (70%)
  matrix products  89.2 us (11%)
  local copies, waits for them, and re-layouts  83.9 us (11%)
  other arithmetic  54.6 us (7%)
    pallas_call x3, Pallas kernels, gather(): pl.pallas_call(functools.partial(gather_kernel, axis), out_shape=jax.Shap...  108 us
    pallas_call x2, Pallas kernels, scatter_both(): pl.pallas_call(functools.partial(scatter_both_kernel, axis), out_shape=ja...  99.7 us
    pallas_call x2, Pallas kernels, gather_both(): pl.pallas_call(functools.partial(gather_both_kernel, axis), out_shape=jax...  84.3 us
    pallas_call x3, Pallas kernels, scatter(): pl.pallas_call(functools.partial(scatter_kernel, axis), out_shape=jax.Sha...  79.3 us
    pallas_call x3, Pallas kernels, swap(): pl.pallas_call(functools.partial(swap_kernel, axis, n), out_shape=jax.Sha...  55.2 us
    pallas_call x1, Pallas kernels, fetch(): pl.pallas_call(fetch_kernel, out_shape=jax.ShapeDtypeStruct((3,) + x.shap...  51.6 us
    dot_general x3, matrix products, contract_last(): lax.dot_general(left, right, (((1,), (1,)), ((), ())), preferred_element_...  27.6 us
    pallas_call x1, Pallas kernels, attention_backward(): pl.pallas_call(attn_bwd, out_shape=(f((rows, 128), jnp.float32),) * 3, in...  27.4 us

profile of v1, /device:TPU:1, one launch (start us, length us, event | category | flops | bytes accessed | tf_op | source)
XLA Modules:
  0.0 780.7 jit_solution(17439653978610258001)
XLA Ops:
  11.1 6.1 concatenate.48
  18.8 44.2 %gather_both_seq.1 = bf16[16,128,2048]{2,1,0:T(8,128)(2,1)} custom-call(bf16[128,2048]{1,0:T(8,128)(2,1)} %fusion.12.x), custom_call_target="tpu_custom_call" | custom-call | tf_op jit(solution)/shard_map/gather_both_seq/pallas_call | solution.py:336
  72.3 51.6 %fetch_heads.1 = bf16[3,2048,128]{2,1,0:T(8,128)(2,1)} custom-call(bf16[6,2048,128]{2,1,0:T(8,128)(2,1)} %bitcast.143), custom_call_target="tpu_custom_call" | custom-call | tf_op jit(solution)/shard_map/fetch_heads/pallas_call | solution.py:446
  127.5 7.5 convolution_add_fusion
  148.4 6.5 fusion.26.q_ref
  158.6 20.8 %attend.1 = (bf16[2048,128]{1,0:T(8,128)(2,1)}, f32[128,2048]{1,0:T(8,128)}, f32[8,2048]{1,0:T(8,128)}) custom-call(bf16[2048,128]{1,0:T(8,128)(2,1)} %fusion.26.q_ref, bf16[2048,128]{1,0:T(8,128)(2,1)} %fusion.22.k_ref, bf16[2048,128]{1,0:T(8,128)(2,1)} %slice.202.v_ref, s32[1,2048]{1,0:T(1,128)} %copy-done.32), custom_call_target="tpu_custom_call" | custom-call | tf_op jit(solution)/shard_map/attend/pallas_call | solution.py:269
  179.5 27.5 %swap_seq.2 = bf16[16,128,128]{2,1,0:T(8,128)(2,1)} custom-call(bf16[16,128,128]{2,1,0:T(8,128)(2,1)} %bitcast.170), custom_call_target="tpu_custom_call" | custom-call | tf_op jit(solution)/shard_map/swap_seq/pallas_call | solution.py:414
  210.9 40.2 %gather_both_wt.1 = bf16[16,1024,256]{2,1,0:T(8,128)(2,1)} custom-call(bf16[1024,256]{1,0:T(8,128)(2,1)} %constant_dynamic-slice_fusion.x), custom_call_target="tpu_custom_call" | custom-call | tf_op jit(solution)/shard_map/gather_both_wt/pallas_call | solution.py:336
  251.1 11.7 %copy.68 = bf16[8,256,2,1024]{3,1,0,2:T(8,128)(2,1)} copy(bf16[8,256,2,1024]{1,3,2,0:T(8,128)(2,1)} %bitcast.139) | data formatting | bytes 16777216 | tf_op jit(solution)/shard_map/tck,wckn->twn/dot_general | solution.py:609
  262.8 6.5 fusion.47
  270.6 35.1 %gather_wt.3 = bf16[8,128,2048]{2,1,0:T(8,128)(2,1)} custom-call(bf16[128,2048]{1,0:T(8,128)(2,1)} %add_convert_fusion.1.x), custom_call_target="tpu_custom_call" | custom-call | tf_op jit(solution)/shard_map/gather_wt/pallas_call | solution.py:303
  305.8 11.8 %fusion.48 = f32[1024,1408]{1,0:T(8,128)} fusion(bf16[1024,2048]{1,0:T(8,128)(2,1)} %bitcast.154, bf16[2048,1408]{0,1:T(8,128)(2,1)} %bitcast.175), kind=kOutput, calls=%fused_computation.118 | convolution fusion | flops 5905580032 | bytes 15728640 | tf_op jit(solution)/shard_map/dot_general | solution.py:615
  317.6 33.9 %gather_wt.4 = bf16[8,128,2048]{2,1,0:T(8,128)(2,1)} custom-call(bf16[128,2048]{1,0:T(8,128)(2,1)} %bitcast.162), custom_call_target="tpu_custom_call" | custom-call | tf_op jit(solution)/shard_map/gather_wt/pallas_call | solution.py:303
  351.5 8.2 %multiply_convert_fusion.1 = (bf16[1024,704]{1,0:T(8,128)(2,1)S(1)}, bf16[1024,704]{1,0:T(8,128)(2,1)S(1)}, bf16[1024,704]{1,0:T(8,128)(2,1)S(1)}) fusion(f32[1024,1408]{1,0:T(8,128)} %fusion.48, bf16[1024,2048]{1,0:T(8,128)(2,1)} %bitcast.156, bf16[704,2048]{1,0:T(8,128)(2,1)S(1)} %copy-done), kind=kOutput, calls=%fused_computation.8 | convolution fusion | flops 2964324352 | bytes 17170432 | tf_op jit(solution)/shard_map/dot_general | solution.py:581
  359.8 12.6 %convolution_convert_fusion.2 = bf16[1024,2048]{1,0:T(8,128)(2,1)} fusion(bf16[2048,1408]{0,1:T(8,128)(2,1)} %bitcast.176, bf16[1024,704]{1,0:T(8,128)(2,1)S(1)} %get-tuple-element.69, bf16[1024,704]{1,0:T(8,128)(2,1)S(1)} %get-tuple-element.68), kind=kOutput, calls=%fused_computation.3 | convolution fusion | flops 5913444352 | bytes 12845056 | tf_op jit(solution)/shard_map/dot_general | solution.py:581
  372.3 32.0 %scatter_wt.4 = f32[128,2048]{1,0:T(8,128)} custom-call(bf16[8,128,2048]{2,1,0:T(8,128)(2,1)} %bitcast.152), custom_call_target="tpu_custom_call" | custom-call | tf_op jit(solution)/shard_map/scatter_wt/pallas_call | solution.py:354
  411.1 30.6 %scatter_wt.3 = f32[128,2048]{1,0:T(8,128)} custom-call(bf16[8,128,2048]{2,1,0:T(8,128)(2,1)} %bitcast.153), custom_call_target="tpu_custom_call" | custom-call | tf_op jit(solution)/shard_map/scatter_wt/pallas_call | solution.py:354
  444.9 6.3 fusion.4
  452.5 17.9 %swap_seq.3 = bf16[16,128,128]{2,1,0:T(8,128)(2,1)} custom-call(bf16[16,128,128]{2,1,0:T(8,128)(2,1)} %bitcast.160), custom_call_target="tpu_custom_call" | custom-call | tf_op jit(solution)/shard_map/swap_seq/pallas_call | solution.py:414
  470.4 27.4 %attend_back.1 = (f32[2048,128]{1,0:T(8,128)}, f32[2048,128]{1,0:T(8,128)}, f32[2048,128]{1,0:T(8,128)}) custom-call(bf16[2048,128]{1,0:T(8,128)(2,1)} %fusion.26.q_ref, bf16[2048,128]{1,0:T(8,128)(2,1)} %fusion.22.k_ref, bf16[2048,128]{1,0:T(8,128)(2,1)} %slice.202.v_ref, s32[1,2048]{1,0:T(1,128)} %copy-done.32, f32[128,2048]{1,0:T(8,128)} %get-tuple-element.18.ot_ref, ...), custom_call_target="tpu_custom_call" | custom-call | tf_op jit(solution)/shard_map/attend_back/pallas_call | solution.py:279
  506.9 6.8 convolution_convert_fusion.1
  513.8 45.1 %scatter_both_seq.2 = f32[128,2048]{1,0:T(8,128)} custom-call(bf16[16,128,2048]{2,1,0:T(8,128)(2,1)} %bitcast.145), custom_call_target="tpu_custom_call" | custom-call | tf_op jit(solution)/shard_map/scatter_both_seq/pallas_call | solution.py:388
  566.0 14.5 %small_sum.1 = f32[1,128]{1,0:T(1,128)} custom-call(f32[8,16,128]{2,1,0:T(8,128)} %bitcast.171), custom_call_target="tpu_custom_call" | custom-call | tf_op jit(solution)/shard_map/small_sum/pallas_call | solution.py:527
  581.9 9.1 %convolution_convert_fusion.5 = bf16[2048,384]{1,0:T(8,128)(2,1)} fusion(bf16[2048,2048]{1,0:T(8,128)(2,1)} %bitcast.147, bf16[2048,128]{1,0:T(8,128)(2,1)S(1)} %copy-done.25, bf16[2048,128]{1,0:T(8,128)(2,1)S(1)} %copy-done.27, bf16[2048,128]{1,0:T(8,128)(2,1)S(1)} %copy-done.29), kind=kOutput, calls=%fused_computation.14 | convolution fusion | flops 3226730496 | bytes 11534336 | tf_op jit(solution)/shard_map/dot_general | solution.py:577
  591.0 16.7 %scatter_wt.5 = f32[256,384]{1,0:T(8,128)} custom-call(bf16[8,256,384]{2,1,0:T(8,128)(2,1)} %bitcast.167), custom_call_target="tpu_custom_call" | custom-call | tf_op jit(solution)/shard_map/scatter_wt/pallas_call | solution.py:354
  609.5 10.4 %place_qkv.1 = bf16[6,128,128]{2,1,0:T(8,128)(2,1)} custom-call(bf16[2,3,128,128]{3,2,1,0:T(8,128)(2,1)} %bitcast.168), custom_call_target="tpu_custom_call" | custom-call | tf_op jit(solution)/shard_map/place_qkv/pallas_call | solution.py:501
  623.3 38.8 %gather_wt.5 = bf16[8,128,2048]{2,1,0:T(8,128)(2,1)} custom-call(bf16[128,2048]{1,0:T(8,128)(2,1)} %copy_bitcast_fusion.x), custom_call_target="tpu_custom_call" | custom-call | tf_op jit(solution)/shard_map/gather_wt/pallas_call | solution.py:303
  663.1 9.8 %swap_wt.1 = bf16[8,128,256]{2,1,0:T(8,128)(2,1)} custom-call(bf16[8,128,256]{2,1,0:T(8,128)(2,1)} %bitcast.161), custom_call_target="tpu_custom_call" | custom-call | tf_op jit(solution)/shard_map/swap_wt/pallas_call | solution.py:414
  680.5 8.3 %convolution_convert_fusion = bf16[2048,1408]{0,1:T(8,128)(2,1)S(1)} fusion(bf16[1024,2048]{1,0:T(8,128)(2,1)S(1)} %bitcast.155, bf16[1024,704]{1,0:T(8,128)(2,1)S(1)} %copy-done.43, bf16[1024,704]{1,0:T(8,128)(2,1)S(1)} %copy-done.41), kind=kOutput, calls=%fused_computation.1 | convolution fusion | flops 5914230784 | bytes 12845056 | tf_op jit(solution)/shard_map/dot_general | solution.py:577
  688.8 15.7 %pad_maximum_fusion = bf16[2048,2368]{0,1:T(8,128)(2,1)} fusion(bf16[2048,256]{0,1:T(8,128)(2,1)S(1)} %fusion.1, bf16[2048,704]{0,1:T(8,128)(2,1)S(1)} %fusion, bf16[2048,1408]{0,1:T(8,128)(2,1)S(1)} %convolution_convert_fusion), kind=kLoop, calls=%fused_computation | loop fusion | flops 29097984 | bytes 19398656 | tf_op jit(solution)/shard_map/concatenate | solution.py:652
  704.5 13.3 %copy.88 = bf16[2048,2368]{1,0:T(8,128)(2,1)} copy(bf16[2048,2368]{0,1:T(8,128)(2,1)} %pad_maximum_fusion) | data formatting | bytes 19398656 | tf_op jit(solution)/shard_map/concatenate | solution.py:652
  717.8 54.6 %scatter_both_seq.3 = f32[128,2368]{1,0:T(8,128)} custom-call(bf16[16,128,2368]{2,1,0:T(8,128)(2,1)} %bitcast.141), custom_call_target="tpu_custom_call" | custom-call | tf_op jit(solution)/shard_map/scatter_both_seq/pallas_call | solution.py:388
  (170 shorter events, 97.5 us)
Async XLA Ops:
  0.6 350.9 %copy-start = (bf16[704,2048]{1,0:T(8,128)(2,1)S(1)}, bf16[704,2048]{1,0:T(8,128)(2,1)}, u32[]{:S(2)}) copy-start(bf16[704,2048]{1,0:T(8,128)(2,1)} %param.22) | copy-start | bytes 8650756
  4.2 13.0 %copy-start.32 = (s32[1,2048]{1,0:T(1,128)}, s32[1,2048]{1,0:T(1,128)S(1)}, u32[]{:S(2)}) copy-start(s32[1,2048]{1,0:T(1,128)S(1)} %compare_select_fusion.1.start_ref) | copy-start | bytes 24580
  11.1 6.1 copy-start.12
  11.1 6.6 copy-start.34
  11.1 6.6 copy-start.36
  148.2 6.6 copy-start.23
  148.3 6.5 copy-start.10
  148.3 6.5 copy-start.3
  148.3 6.5 copy-start.4
  148.3 6.5 copy-start.6
  148.3 6.5 copy-start.8
  148.3 6.5 copy-start.20
  148.3 6.9 copy-start.21
  148.4 7.2 copy-start.22
  262.8 6.8 copy-start.33
  262.8 6.8 copy-start.37
  359.7 12.6 %copy-start.40 = (bf16[1024,704]{1,0:T(8,128)(2,1)}, bf16[1024,704]{1,0:T(8,128)(2,1)S(1)}, u32[]{:S(2)}) copy-start(bf16[1024,704]{1,0:T(8,128)(2,1)S(1)} %get-tuple-element.68) | copy-start | bytes 4325380
  359.7 12.6 %copy-start.42 = (bf16[1024,704]{1,0:T(8,128)(2,1)}, bf16[1024,704]{1,0:T(8,128)(2,1)S(1)}, u32[]{:S(2)}) copy-start(bf16[1024,704]{1,0:T(8,128)(2,1)S(1)} %get-tuple-element.69) | copy-start | bytes 4325380
  359.8 46.3 %copy-start.38 = (bf16[1024,704]{1,0:T(8,128)(2,1)}, bf16[1024,704]{1,0:T(8,128)(2,1)S(1)}, u32[]{:S(2)}) copy-start(bf16[1024,704]{1,0:T(8,128)(2,1)S(1)} %get-tuple-element.70) | copy-start | bytes 4325380
  411.0 30.7 %copy-start.13 = (f32[128,2048]{1,0:T(8,128)S(1)}, f32[128,2048]{1,0:T(8,128)}, u32[]{:S(2)}) copy-start(f32[128,2048]{1,0:T(8,128)} %scatter_wt.4) | copy-start | bytes 3145732
  411.0 30.7 %copy-start.30 = (bf16[1,128,2048]{2,1,0:T(8,128)(2,1)S(1)}, bf16[1,128,2048]{2,1,0:T(8,128)(2,1)}, u32[]{:S(2)}) copy-start(bf16[1,128,2048]{2,1,0:T(8,128)(2,1)} %param.23) | copy-start | bytes 1572868
  499.1 7.8 copy-start.24
  506.9 6.9 copy-start.28
  513.8 46.9 %copy-start.19 = (f32[128,2048]{1,0:T(8,128)S(1)}, f32[128,2048]{1,0:T(8,128)}, u32[]{:S(2)}) copy-start(f32[128,2048]{1,0:T(8,128)} %get-tuple-element.67) | copy-start | bytes 3145732
  558.8 4.5 copy-start.25
  558.8 4.5 copy-start.27
  563.2 18.8 %copy-start.29 = (bf16[2048,128]{1,0:T(8,128)(2,1)S(1)}, bf16[2048,128]{1,0:T(8,128)(2,1)}, u32[]{:S(2)}) copy-start(bf16[2048,128]{1,0:T(8,128)(2,1)} %copy-done.28) | copy-start | bytes 1572868
  591.0 30.9 %copy-start.35 = (f32[1,128]{1,0:T(1,128)S(1)}, f32[1,128]{1,0:T(1,128)}, u32[]{:S(2)}) copy-start(f32[1,128]{1,0:T(1,128)} %small_sum.1) | copy-start | bytes 1540
  591.0 31.5 %copy-start.14 = (bf16[16,128,128]{2,1,0:T(8,128)(2,1)S(1)}, bf16[16,128,128]{2,1,0:T(8,128)(2,1)}, u32[]{:S(2)}) copy-start(bf16[16,128,128]{2,1,0:T(8,128)(2,1)} %swap_seq.2) | copy-start | bytes 1572868
  672.9 3.8 copy-start.18
  672.9 4.1 copy-start.39
  717.8 62.5 %copy-start.1 = (bf16[704,2048]{1,0:T(8,128)(2,1)S(1)}, bf16[704,2048]{1,0:T(8,128)(2,1)}, u32[]{:S(2)}) copy-start(bf16[704,2048]{1,0:T(8,128)(2,1)} %param.22) | copy-start | bytes 8650756
  (12 other events, 26.7 us)

commit v2 on v1

--- a/solution.py
+++ b/solution.py
@@ -282,6 +282,323 @@
         scratch_shapes=[pltpu.VMEM((2, rows, 128), jnp.bfloat16)] * 4 + [pltpu.VMEM((128, rows), jnp.bfloat16), pltpu.VMEM((128, rows), jnp.float32)],
         compiler_params=pltpu.CompilerParams(vmem_limit_bytes=56 * 2**20), name="attend_back",
     )(q, k, v, start, ot, lse, do)
+ORDER = [(0, 0), (0, 1), (-1, 1), (1, 1), (-1, 0), (1, 0), (2, 0), (2, 1)]
+
+class Gather:
+    def __init__(self, pn, own, buf, rows, ss, rs, twin=None):
+        self.pn, self.buf, self.twin = pn, buf, twin
+        self.index = (lambda j: 2 * j + pn.c) if twin else (lambda j: j)
+        steps, tail, done = gather_steps(pn, own, buf, rows, ss, rs, self.index)
+        self.done = done
+        ready = {0: [1], 1: [2], 2: [3], 3: [4], 4: [5], 6: [6], 8: [7]}
+        def follow(i, f):
+            def g():
+                f()
+                for k in ready.get(i, []):
+                    self.hand(k)
+            return g
+        def first():
+            steps[0]()
+            self.hand(0)
+        self.steps = [first] + steps[1:] + [follow(i, f) for i, f in enumerate(tail)]
+
+    def handed(self, k, mine):
+        c = self.pn.c if mine else 1 - self.pn.c
+        j = self.buf.at[2 * self.pn.block(*ORDER[k]) + c]
+        return remote(j, j, self.twin[0], self.twin[1], k, self.pn.twin)
+
+    def hand(self, k):
+        if self.twin:
+            self.handed(k, True).start()
+
+    def wait_twin(self, k):
+        self.handed(k, False).wait_recv()
+
+    def finish(self, waited=()):
+        self.done()
+        if self.twin:
+            for k in range(8):
+                self.handed(k, True).wait_send()
+                if k not in waited:
+                    self.wait_twin(k)
+
+def fetch_steps(pn, weight, hw, ss, rs, ls):
+    s = lax.axis_index("seq")
+    rows = hw.shape[0]
+    h, q = rows // 2, rows // 4
+    W = {"P": (0, h), "Q": (h, h), "P0": (0, q), "P1": (q, q), "Q0": (h, q), "Q1": (h + q, q)}
+    kinds = ["P", "P0", "P1", "Q", "Q0", "Q1"]
+    both = []
+    for p in range(3):
+        g = 16 * p + s
+        src = g // 6
+        da = lax.rem(pn.a - src // 2 + 4, 4)
+        b0 = pn.b == lax.rem(src, 2)
+        both.append((p, lax.rem(g, 6), da, b0))
+    def part(p, kind):
+        return hw.at[pl.ds(*W[kind]), pl.ds(128 * p, 128)]
+    def send(p, kind, slot, target):
+        pltpu.make_async_remote_copy(src_ref=part(p, kind), dst_ref=part(p, kind), send_sem=ss.at[6 * p + slot],
+                                     recv_sem=rs.at[6 * p + kinds.index(kind)], device_id=target, device_id_type=MESH).start()
+    def wait(p, kind, slot=None):
+        cp = pltpu.make_async_remote_copy(src_ref=part(p, kind), dst_ref=part(p, kind), send_sem=ss.at[6 * p + (slot or 0)],
+                                          recv_sem=rs.at[6 * p + kinds.index(kind)], device_id=pn.right, device_id_type=MESH)
+        cp.wait_recv() if slot is None else cp.wait_send()
+    no = jnp.logical_not
+    def local(p, b):
+        return pltpu.make_async_copy(weight.at[:, pl.ds(pl.multiple_of(128 * b, 128), 128)], hw.at[:, pl.ds(128 * p, 128)], ls.at[p])
+    def begin():
+        for p, b, da, b0 in both:
+            @pl.when(b0 & (da == 0))
+            def _():
+                local(p, b).start()
+    def st0():
+        for p, b, da, b0 in both:
+            @pl.when(b0 & (da == 0))
+            def _():
+                local(p, b).wait()
+                send(p, "Q", 0, pn.right); send(p, "Q", 1, pn.left); send(p, "P", 5, pn.pair)
+                send(p, "P", 3, pn.right); send(p, "P", 4, pn.left); send(p, "Q", 2, pn.pair)
+    def st1():
+        for p, b, da, b0 in both:
+            @pl.when(b0 & (da == 1))
+            def _():
+                wait(p, "Q"); send(p, "Q0", 0, pn.right); send(p, "Q", 2, pn.pair)
+            @pl.when(b0 & (da == 3))
+            def _():
+                wait(p, "Q"); send(p, "Q1", 1, pn.left); send(p, "Q", 2, pn.pair)
+            @pl.when(no(b0) & (da == 0))
+            def _():
+                wait(p, "P"); send(p, "P", 3, pn.right); send(p, "P", 4, pn.left)
+    def st2():
+        for p, b, da, b0 in both:
+            @pl.when(da == 1)
+            def _():
+                wait(p, "P"); send(p, "P0", 3, pn.right)
+            @pl.when(da == 3)
+            def _():
+                wait(p, "P"); send(p, "P1", 4, pn.left)
+    def st3():
+        for p, b, da, b0 in both:
+            @pl.when(b0 & (da == 2))
+            def _():
+                wait(p, "Q0"); wait(p, "Q1"); send(p, "Q", 2, pn.pair)
+    def st4():
+        for p, b, da, b0 in both:
+            @pl.when(da == 2)
+            def _():
+                wait(p, "P0"); wait(p, "P1")
+            @pl.when(no(b0))
+            def _():
+                wait(p, "Q")
+    def done():
+        for p, b, da, b0 in both:
+            @pl.when(b0)
+            def _():
+                wait(p, "Q", 2)
+            @pl.when(b0 & (da == 0))
+            def _():
+                wait(p, "Q", 0); wait(p, "Q", 1); wait(p, "P", 5)
+            @pl.when(da == 0)
+            def _():
+                wait(p, "P", 3); wait(p, "P", 4)
+            @pl.when(b0 & (da == 1))
+            def _():
+                wait(p, "Q0", 0)
+            @pl.when(b0 & (da == 3))
+            def _():
+                wait(p, "Q1", 1)
+            @pl.when(da == 1)
+            def _():
+                wait(p, "P0", 3)
+            @pl.when(da == 3)
+            def _():
+                wait(p, "P1", 4)
+    return begin, [st0, st1, st2, st3, st4], done
+
+def turn(v, keep, ahead, behind):
+    return v * keep + pltpu.roll(v, 120, 1) * ahead + pltpu.roll(v, 8, 1) * behind
+
+def norm_rows(x, gain, shift):
+    average = jnp.mean(x, axis=-1, keepdims=True)
+    centred = x - average
+    inverse = lax.rsqrt(jnp.mean(centred * centred, axis=-1, keepdims=True) + norm_eps)
+    return centred * inverse * gain + shift
+
+def rotary_tables_to(cs, tables):
+    rows = cs.shape[1]
+    c, s = cs[0:8, :], cs[8:16, :]
+    one, nil, z8 = jnp.ones((48, rows), jnp.float32), jnp.zeros((48, rows), jnp.float32), jnp.zeros((8, rows), jnp.float32)
+    tables[0][...] = jnp.concatenate([c, c, one] * 2, axis=0).T
+    tables[1][...] = jnp.concatenate([-s, z8, nil] * 2, axis=0).T
+    tables[2][...] = jnp.concatenate([z8, s, nil] * 2, axis=0).T
+
+def front_kernel(x, gain, shift, weight, bias, cs, start_ref, dy, ow,
+                 rn, hw, q_ref, k_ref, v_ref, ot_ref, lse_ref, att, out_all, dy_all,
+                 own, kept, vt, t0, t1, t2, ob, ox,
+                 ssA, rsA, tsA, trA, ssB, rsB, lsB, ssC, rsC, ssD, rsD, tsD, trD, ssO, rsO, ssT, rsT, lsO, ls):
+    sp, wp = Plane("seq"), Plane("wt")
+    tok = x.shape[0]
+    c, m = sp.c, sp.block(0, 0)
+    A = Gather(sp, own, rn, tok, ssA, rsA, (tsA, trA))
+    begin, fetch, fetch_done = fetch_steps(wp, weight, hw, ssB, rsB, lsB)
+    C = Gather(wp, dy, dy_all, tok, ssC, rsC)
+    D = Gather(wp, ow, out_all, ow.shape[0], ssD, rsD, (tsD, trD))
+    begin()
+    chips = [at(j // 4, j % 4, c, wp.a, wp.b) for j in range(8)]
+    bar = pltpu.get_barrier_semaphore()
+    for j in range(8):
+        @pl.when(m != j)
+        def _():
+            pl.semaphore_signal(bar, inc=1, device_id=chips[j], device_id_type=MESH)
+    for t in (sp.twin, wp.left, wp.right, wp.pair):
+        pl.semaphore_signal(bar, inc=1, device_id=t, device_id_type=MESH)
+    def ln(i, _):
+        r = pl.ds(pl.multiple_of(i * 16, 16), 16)
+        own[r] = norm_rows(x[r].astype(jnp.float32), gain[...], shift[...]).astype(jnp.bfloat16)
+        return 0
+    lax.fori_loop(0, tok // 16, ln, 0)
+    copies = [pltpu.make_async_copy(own, rn.at[2 * m + c], ls.at[0]),
+              pltpu.make_async_copy(dy, dy_all.at[wp.block(0, 0)], ls.at[1]),
+              pltpu.make_async_copy(ow, out_all.at[2 * wp.block(0, 0) + c], ls.at[2])]
+    for cp in copies:
+        cp.start()
+    copies[0].wait()
+    pl.semaphore_wait(bar, 11)
+    A.steps[0]()
+    fetch[0]()
+    rotary_tables_to(cs, (t0, t1, t2))
+    copies[1].wait()
+    copies[2].wait()
+    a, b, cc, d = iter(A.steps[1:]), iter(fetch[1:]), iter(C.steps), iter(D.steps)
+    def pump(*its):
+        for it in its:
+            f = next(it, None)
+            if f is not None:
+                f()
+    pump(a, a, b, a, a, a, b, a, a, b, b, a, a, cc)
+    def project(k):
+        A.wait_twin(k)
+        j = sp.block(*ORDER[k])
+        rows = pl.ds(pl.multiple_of(j * 256, 256), 256)
+        h = rn[pl.ds(2 * j, 2)].reshape(256, rn.shape[2])
+        y = jnp.dot(h, hw[...], preferred_element_type=jnp.float32) + bias[...]
+        tabs = (t0[rows], t1[rows], t2[rows])
+        q_ref[rows] = (turn(y[:, :128], *tabs) * 0.125).astype(jnp.bfloat16)
+        k_ref[rows] = turn(y[:, 128:256], *tabs).astype(jnp.bfloat16)
+        v_ref[rows] = y[:, 256:].astype(jnp.bfloat16)
+    project(0); pump(a); project(1); pump(a); pump(cc); project(2); pump(a); project(3)
+    pump(a); project(4); pump(a, cc); project(5); pump(a, a); pump(cc); project(6); pump(a, a); project(7)
+    halves(k_ref, kept)
+    pump(cc, cc)
+    vt[...] = v_ref[...].astype(jnp.float32).T.astype(jnp.bfloat16)
+    def to_twin(j):
+        return pltpu.make_async_remote_copy(src_ref=ox.at[j], dst_ref=ob.at[j, :, pl.ds(pl.multiple_of(128 * c, 128), 128)],
+                                            send_sem=ssT.at[j], recv_sem=rsT.at[j], device_id=sp.twin, device_id_type=MESH)
+    def from_twin(j):
+        there = ob.at[j, :, pl.ds(pl.multiple_of(128 * (1 - c), 128), 128)]
+        return pltpu.make_async_remote_copy(src_ref=there, dst_ref=there, send_sem=ssT.at[j], recv_sem=rsT.at[j], device_id=sp.twin, device_id_type=MESH)
+    def cols(j):
+        return att.at[:, pl.ds(pl.multiple_of(256 * j, 256), 256)]
+    def to_chip(j):
+        return pltpu.make_async_remote_copy(src_ref=ob.at[j], dst_ref=cols(m), send_sem=ssO.at[j], recv_sem=rsO.at[m], device_id=chips[j], device_id_type=MESH)
+    def ship(i):
+        for j in (2 * i, 2 * i + 1):
+            from_twin(j).wait_recv()
+            @pl.when(m == j)
+            def _():
+                pltpu.make_async_copy(ob.at[j], cols(j), lsO).start()
+            @pl.when(m != j)
+            def _():
+                to_chip(j).start()
+    n = q_ref.shape[0] // QB
+    for i in range(n):
+        q = q_ref[QB * i:QB * (i + 1)]
+        start = start_ref[:, QB * i:QB * (i + 1)]
+        step = functools.partial(attend_step, kept, vt, q, start, i)
+        one = (jnp.full((1, QB), MASKED, jnp.float32), jnp.zeros((1, QB), jnp.float32), jnp.zeros((64, QB), jnp.float32))
+        carry = (one, one)
+        if i == n - 1:
+            for j in range(0, 2 * i + 2, 2):
+                carry = lax.fori_loop(j, j + 2, functools.partial(step, True), carry)
+                pump(cc, d)
+        else:
+            if i:
+                carry = step(True, 0, carry)
+                carry = lax.fori_loop(1, 2 * i, functools.partial(step, False), carry)
+                pump(cc, d) if i == 1 else pump(cc, cc, d)
+            carry = lax.fori_loop(2 * i, 2 * i + 2, functools.partial(step, True), carry)
+            pump(cc, cc)
+        where = pl.ds(QB * i, QB)
+        for h in range(2):
+            top, l, acc = carry[h]
+            ot_ref[64 * h:64 * h + 64, where] = acc / l
+            lse_ref[h:h + 1, where] = top + jnp.log(l)
+        if i:
+            ship(i - 1)
+        o = ot_ref[:, where].T.astype(jnp.bfloat16)
+        for j in (0, 1):
+            mine = pl.ds(pl.multiple_of(128 * c, 128), 128)
+            first, second = o[256 * j:256 * j + 128], o[256 * j + 128:256 * j + 256]
+            @pl.when(c == 0)
+            def _():
+                ob[2 * i + j, :, 0:128] = first
+                ox[2 * i + j] = second
+            @pl.when(c == 1)
+            def _():
+                ob[2 * i + j, :, 128:256] = second
+                ox[2 * i + j] = first
+            to_twin(2 * i + j).start()
+    ship(n - 1)
+    for f in cc:
+        f()
+    for f in d:
+        f()
+    for j in range(8):
+        to_twin(j).wait_send()
+        @pl.when(m == j)
+        def _():
+            pltpu.make_async_copy(ob.at[j], cols(j), lsO).wait()
+        @pl.when(m != j)
+        def _():
+            to_chip(j).wait_send()
+            pltpu.make_async_remote_copy(src_ref=cols(j), dst_ref=cols(j), send_sem=ssO.at[j], recv_sem=rsO.at[j], device_id=chips[j], device_id_type=MESH).wait_recv()
+    A.finish(range(8))
+    fetch_done()
+    C.finish()
+    D.finish()
+
+def attend_step(kept, vt, q, start, i, masked, j, carry):
+    r = pl.ds(pl.multiple_of(j * KB, KB), KB)
+    out = []
+    for h in range(2):
+        m, l, acc = carry[h]
+        s = lax.dot_general(kept[h, r], q, NT, preferred_element_type=jnp.float32)
+        if masked:
+            s = jnp.where(allowed(i, j, start), s, MASKED)
+        top = jnp.maximum(m, jnp.max(s, axis=0, keepdims=True))
+        p = jnp.exp(s - top)
+        fade = jnp.exp(m - top)
+        l = l * fade + jnp.sum(p, axis=0, keepdims=True)
+        acc = acc * fade + jnp.dot(vt[64 * h:64 * h + 64, r], p.astype(jnp.bfloat16), preferred_element_type=jnp.float32)
+        out.append((top, l, acc))
+    return tuple(out)
+
+def front(cid, x, gain, shift, weight, bias, cs, start, dy, ow):
+    tok, width = x.shape
+    rows = start.shape[1]
+    f, b16, f32 = jax.ShapeDtypeStruct, jnp.bfloat16, jnp.float32
+    vm = pltpu.VMEM
+    return pl.pallas_call(
+        front_kernel,
+        out_shape=(f((16, tok, width), b16), f((width, 384), b16), f((rows, 128), b16), f((rows, 128), b16), f((rows, 128), b16),
+                   f((128, rows), f32), f((8, rows), f32), f((tok, width), b16), f((16,) + ow.shape, b16), f((8, tok, width), b16)),
+        in_specs=[VM, VM, VM, ANY, VM, VM, VM, VM, VM], out_specs=(VM,) * 10,
+        scratch_shapes=[vm((tok, width), b16), vm((2, rows, 128), b16), vm((128, rows), b16)] + [vm((rows, 128), f32)] * 3
+        + [vm((8, 128, 256), b16), vm((8, 128, 128), b16)]
+        + [dma(n) for n in (18, 18, 8, 8, 18, 18, 3, 18, 18, 18, 18, 8, 8, 8, 8, 8, 8)] + [pltpu.SemaphoreType.DMA, dma(3)],
+        compiler_params=params(cid), name="front",
+    )(x, gain, shift, weight, bias, cs, start, dy, ow)
 def params(cid):
     return pltpu.CompilerParams(collective_id=cid, has_side_effects=True, vmem_limit_bytes=56 * 2**20)
 
@@ -553,20 +870,20 @@
     return inverse * (weighted - first_mean - scaled * second_mean)
 
 
-def rotary_tables(segment_row):
+def rotary_angles(segment_row):
     rows = segment_row.shape[0]
     ends = [jnp.sum((segment_row < i).astype(jnp.int32)) for i in (1, 2)]
     start = jnp.where(segment_row == 0, 0, jnp.where(segment_row == 1, ends[0], ends[1]))
     offsets = (jnp.arange(rows, dtype=jnp.int32) - start).astype(jnp.float32)
     inv_freq = jnp.exp(jnp.arange(ROT // 2, dtype=jnp.float32) * (-2.0 * math.log(theta_base) / ROT))
-    angles = offsets[:, None] * inv_freq[None, :]
-    c, s = jnp.cos(angles), jnp.sin(angles)
-    one, nil = jnp.ones((rows, 48), jnp.float32), jnp.zeros((rows, 56), jnp.float32)
-    z8 = jnp.zeros((rows, 8), jnp.float32)
-    keep = jnp.concatenate([c, c, one] * 2, axis=1)
-    ahead = jnp.concatenate([-s, nil] * 2, axis=1)
-    behind = jnp.concatenate([z8, s, nil[:, :48]] * 2, axis=1)
-    return start, keep, ahead, behind
+    angles = inv_freq[:, None] * offsets[None, :]
+    return start.reshape(1, rows), jnp.concatenate([jnp.cos(angles), jnp.sin(angles)], axis=0)
+
+
+def wide_tables(cs):
+    c, s = cs[0:8], cs[8:16]
+    one, nil, z8 = jnp.ones((48, c.shape[1]), jnp.float32), jnp.zeros((48, c.shape[1]), jnp.float32), jnp.zeros((8, c.shape[1]), jnp.float32)
+    return [jnp.concatenate(p * 2, axis=0).T for p in ([c, c, one], [-s, z8, nil], [z8, s, nil])]
 
 
 def rotate(v, keep, ahead, behind):
@@ -591,26 +908,20 @@
     scale = 1.0 / math.sqrt(HEAD_DIM)
     inputs = layer_in.reshape(tok, width).astype(f32)
     upstream = layer_grad.reshape(tok, width)
-    start, keep, ahead, behind = rotary_tables(segment_ids.reshape(rows))
-    start = start.reshape(1, rows)
-    normed_one, scaled_one, inverse_one = layer_norm_parts(inputs, norm_one_gain, norm_one_shift)
-    row_normed = gather_both("seq", 0, normed_one.astype(bf16)).reshape(rows, width)
-    head_weight = fetch(1, qkv_weight.reshape(width, 6, 128).transpose(1, 0, 2))
-    head_weight = head_weight.transpose(1, 0, 2).reshape(width, 384)
-    bias = lax.dynamic_index_in_dim(qkv_bias.reshape(3, 16, 128), s, 1, keepdims=False).reshape(384)
-    proj = jnp.dot(row_normed, head_weight, preferred_element_type=f32) + bias
-    q = (rotate(proj[:, :128], keep, ahead, behind) * scale).astype(bf16)
-    k = rotate(proj[:, 128:256], keep, ahead, behind).astype(bf16)
-    v = proj[:, 256:].astype(bf16)
-    o, ot, lse = attention_forward(q, k, v, start)
-    attended = swap("seq", 16, 2, o.reshape(16, tok, 128)).transpose(1, 0, 2).reshape(tok, width)
+    start, cs = rotary_angles(segment_ids.reshape(rows))
+    keep, ahead, behind = wide_tables(cs)
+    _, scaled_one, inverse_one = layer_norm_parts(inputs, norm_one_gain, norm_one_shift)
+    bias = lax.dynamic_index_in_dim(qkv_bias.reshape(3, 16, 128), s, 1, keepdims=False).reshape(1, 384)
     half = lax.dynamic_slice_in_dim(out_weight, (s % 2) * (width // 2), width // 2, 0)
-    out_all = gather_both("wt", 3, half).reshape(8, 2, width // 2, 256)
+    row_normed, head_weight, q, k, v, ot, lse, attended, out_all, all_up = front(
+        0, layer_in.reshape(tok, width), norm_one_gain.reshape(1, width), norm_one_shift.reshape(1, width), qkv_weight, bias, cs, start, upstream, half)
+    row_normed = row_normed.reshape(rows, width)
+    out_all = out_all.reshape(8, 2, width // 2, 256)
+    all_up = all_up.reshape(8 * tok, width)
     branch = jnp.einsum("tck,wckn->twn", attended.reshape(tok, 2, width // 2), out_all, preferred_element_type=f32).reshape(tok, width)
     middle = inputs + branch
     normed_two, scaled_two, inverse_two = layer_norm_parts(middle, norm_two_gain, norm_two_shift)
     all_two = gather("wt", 4, normed_two.astype(bf16)).reshape(8 * tok, width)
-    all_up = gather("wt", 5, upstream).reshape(8 * tok, width)
     weight_gu = gate_up_weight.reshape(width, 2 * hidden)
     gu = jnp.dot(all_two, weight_gu, preferred_element_type=f32)
     g, u = gu[:, :hidden], gu[:, hidden:]

time: 786 us -> 655 us (0.83)
  Pallas kernels: 551 us -> 458 us
  local copies, waits for them, and re-layouts: 83.9 us -> 66.4 us
  matrix products: 89.2 us -> 73.4 us
  other arithmetic: 54.6 us -> 45.4 us
    pallas_call x3 -> x2, Pallas kernels: 108 us -> 72 us  [gather(): pl.pallas_call(functools.partial(gather_kernel, axis), out_shape=jax.Shap...]
    pallas_call x3 -> x2, Pallas kernels: 55.2 us -> 26.7 us  [swap(): pl.pallas_call(functools.partial(swap_kernel, axis, n), out_shape=jax.Sha...]
    pallas_call x4 -> x1, Pallas kernels: 157 us -> 129 us  [front(): pl.pallas_call(front_kernel, out_shape=(f((16, tok, width), b16), f((widt...]
where the time goes in v2:
time: 655 us; the launch traced here: 645 us
  Pallas kernels  458 us (70%)
  matrix products  73.4 us (11%)
  local copies, waits for them, and re-layouts  66.4 us (10%)
  other arithmetic  45.4 us (7%)
    pallas_call x1, Pallas kernels, front(): pl.pallas_call(front_kernel, out_shape=(f((16, tok, width), b16), f((widt...  129 us
    pallas_call x2, Pallas kernels, scatter_both(): pl.pallas_call(functools.partial(scatter_both_kernel, axis), out_shape=ja...  95.7 us
    pallas_call x3, Pallas kernels, scatter(): pl.pallas_call(functools.partial(scatter_kernel, axis), out_shape=jax.Sha...  78.3 us
    pallas_call x2, Pallas kernels, gather(): pl.pallas_call(functools.partial(gather_kernel, axis), out_shape=jax.Shap...  72 us
    pallas_call x1, Pallas kernels, attention_backward(): pl.pallas_call(attn_bwd, out_shape=(f((rows, 128), jnp.float32),) * 3, in...  27.3 us
    pallas_call x2, Pallas kernels, swap(): pl.pallas_call(functools.partial(swap_kernel, axis, n), out_shape=jax.Sha...  26.7 us
    dot_general x4, matrix products, contract_first(): lax.dot_general(left, right, (((0,), (0,)), ((), ())), preferred_element_...  24.6 us
    dot_general x3, matrix products, contract_last(): lax.dot_general(left, right, (((1,), (1,)), ((), ())), preferred_element_...  20.2 us

profile of v2, /device:TPU:1, one launch (start us, length us, event | category | flops | bytes accessed | tf_op | source)
XLA Modules:
  0.0 645.2 jit_solution(15061707545303064678)
XLA Ops:
  6.1 5.8 fusion.25
  17.5 129.5 %front.1 = (bf16[16,128,2048]{2,1,0:T(8,128)(2,1)}, bf16[2048,384]{1,0:T(8,128)(2,1)}, bf16[2048,128]{1,0:T(8,128)(2,1)}, bf16[2048,128]{1,0:T(8,128)(2,1)}, bf1...) custom-call(bf16[128,2048]{1,0:T(8,128)(2,1)} %bitcast.117, ...), custom_call_target="tpu_custom_call" | custom-call | tf_op jit(solution)/shard_map/front/pallas_call | solution.py:592
  147.0 11.7 %copy.85 = bf16[8,256,2,1024]{3,1,0,2:T(8,128)(2,1)} copy(bf16[8,256,2,1024]{1,3,2,0:T(8,128)(2,1)} %bitcast.114) | data formatting | bytes 16777216 | tf_op jit(solution)/shard_map/tck,wckn->twn/dot_general | solution.py:921
  158.7 6.6 %fusion.35 = (f32[128]{0:T(128)S(1)}, f32[128,2048]{1,0:T(8,128)S(1)}) fusion(bf16[2048,2,1024]{2,0,1:T(8,128)(2,1)} %bitcast.116, bf16[16,2,8,1024]{3,2,1,0:T(8,128)(2,1)} %bitcast.130, bf16[1,128,2048]{2,1,0:T(8,128)(2,1)S(1)} %copy-done.3), kind=kOutput, calls=%fused_computation.98 | convolution fusion | flops 1074528128 | bytes 10486272 | tf_op jit(solution)/shard_map/tck,wckn->twn/dot_general | solution.py:921
  166.6 34.9 %gather_wt.2 = bf16[8,128,2048]{2,1,0:T(8,128)(2,1)} custom-call(bf16[128,2048]{1,0:T(8,128)(2,1)} %add_convert_fusion.1.x), custom_call_target="tpu_custom_call" | custom-call | tf_op jit(solution)/shard_map/gather_wt/pallas_call | solution.py:620
  201.5 10.7 %fusion.36 = f32[1024,1408]{1,0:T(8,128)S(1)} fusion(bf16[1024,2048]{1,0:T(8,128)(2,1)} %bitcast.123, bf16[2048,1408]{0,1:T(8,128)(2,1)} %bitcast.141), kind=kOutput, calls=%fused_computation.99 | convolution fusion | flops 5905580032 | bytes 15728640 | tf_op jit(solution)/shard_map/dot_general | solution.py:926
  212.3 4.4 multiply_convert_fusion.1
  216.7 8.8 %convolution_convert_fusion.2 = bf16[1024,2048]{1,0:T(8,128)(2,1)} fusion(bf16[2048,1408]{0,1:T(8,128)(2,1)S(1)} %bitcast.144, bf16[1024,704]{1,0:T(8,128)(2,1)S(1)} %get-tuple-element.96, bf16[1024,704]{1,0:T(8,128)(2,1)S(1)} %get-tuple-element.95), kind=kOutput, calls=%fused_computation.3 | convolution fusion | flops 5913444352 | bytes 12845056 | tf_op jit(solution)/shard_map/dot_general | solution.py:898
  225.6 31.2 %scatter_wt.4 = f32[128,2048]{1,0:T(8,128)} custom-call(bf16[8,128,2048]{2,1,0:T(8,128)(2,1)} %bitcast.121), custom_call_target="tpu_custom_call" | custom-call | tf_op jit(solution)/shard_map/scatter_wt/pallas_call | solution.py:671
  258.4 5.0 convolution_convert_fusion.3
  263.4 31.9 %scatter_wt.3 = f32[128,2048]{1,0:T(8,128)} custom-call(bf16[8,128,2048]{2,1,0:T(8,128)(2,1)} %bitcast.122), custom_call_target="tpu_custom_call" | custom-call | tf_op jit(solution)/shard_map/scatter_wt/pallas_call | solution.py:671
  295.4 3.0 fusion.30
  298.7 6.3 fusion.2
  306.2 16.9 %swap_seq.1 = bf16[16,128,128]{2,1,0:T(8,128)(2,1)} custom-call(bf16[16,128,128]{2,1,0:T(8,128)(2,1)} %bitcast.127), custom_call_target="tpu_custom_call" | custom-call | tf_op jit(solution)/shard_map/swap_seq/pallas_call | solution.py:731
  323.1 27.3 %attend_back.1 = (f32[2048,128]{1,0:T(8,128)}, f32[2048,128]{1,0:T(8,128)}, f32[2048,128]{1,0:T(8,128)}) custom-call(bf16[2048,128]{1,0:T(8,128)(2,1)} %get-tuple-element.27.q_ref, bf16[2048,128]{1,0:T(8,128)(2,1)} %get-tuple-element.28.k_ref, bf16[2048,128]{1,0:T(8,128)(2,1)} %get-tuple-element.29.v_ref, s32[1,2048]{1,0:T(1,128)} %get-tuple-element.94.start_ref, ...), custom_call_target="tpu_custom_call" | custom-call | tf_op jit(solution)/shard_map/attend_back/pallas_call | solution.py:279
  357.3 3.0 concatenate.41
  360.4 4.4 concatenate.45
  364.8 4.3 concatenate.43
  375.6 7.0 %convolution_convert_fusion.1 = bf16[2048,2048]{1,0:T(8,128)(2,1)} fusion(bf16[2048,384]{1,0:T(8,128)(2,1)S(1)} %copy-done.30, bf16[2048,128]{1,0:T(8,128)(2,1)S(1)} %copy-done.17, bf16[2048,128]{1,0:T(8,128)(2,1)S(1)} %get-tuple-element.99, bf16[2048,128]{1,0:T(8,128)(2,1)S(1)} %get-tuple-element.98), kind=kOutput, calls=%fused_computation.2 | convolution fusion | flops 3230138368 | bytes 11534336 | tf_op jit(solution)/shard_map/dot_general | solution.py:898
  382.6 42.9 %scatter_both_seq.2 = f32[128,2048]{1,0:T(8,128)} custom-call(bf16[16,128,2048]{2,1,0:T(8,128)(2,1)} %bitcast.118), custom_call_target="tpu_custom_call" | custom-call | tf_op jit(solution)/shard_map/scatter_both_seq/pallas_call | solution.py:705
  432.4 15.9 %small_sum.1 = f32[1,128]{1,0:T(1,128)} custom-call(f32[8,16,128]{2,1,0:T(8,128)} %bitcast.135), custom_call_target="tpu_custom_call" | custom-call | tf_op jit(solution)/shard_map/small_sum/pallas_call | solution.py:844
  449.7 9.1 %convolution_convert_fusion.5 = bf16[2048,384]{1,0:T(8,128)(2,1)} fusion(bf16[2048,2048]{1,0:T(8,128)(2,1)} %bitcast.140, bf16[2048,128]{1,0:T(8,128)(2,1)S(1)} %copy-done.18, bf16[2048,128]{1,0:T(8,128)(2,1)S(1)} %copy-done.22, bf16[2048,128]{1,0:T(8,128)(2,1)S(1)} %copy-done.20), kind=kOutput, calls=%fused_computation.12 | convolution fusion | flops 3226730496 | bytes 11534336 | tf_op jit(solution)/shard_map/dot_general | solution.py:894
  458.8 15.2 %scatter_wt.5 = f32[256,384]{1,0:T(8,128)} custom-call(bf16[8,256,384]{2,1,0:T(8,128)(2,1)} %bitcast.132), custom_call_target="tpu_custom_call" | custom-call | tf_op jit(solution)/shard_map/scatter_wt/pallas_call | solution.py:671
  475.8 12.8 %place_qkv.1 = bf16[6,128,128]{2,1,0:T(8,128)(2,1)} custom-call(bf16[2,3,128,128]{3,2,1,0:T(8,128)(2,1)} %bitcast.133), custom_call_target="tpu_custom_call" | custom-call | tf_op jit(solution)/shard_map/place_qkv/pallas_call | solution.py:818
  491.2 37.1 %gather_wt.3 = bf16[8,128,2048]{2,1,0:T(8,128)(2,1)} custom-call(bf16[128,2048]{1,0:T(8,128)(2,1)} %get-tuple-element.24.x), custom_call_target="tpu_custom_call" | custom-call | tf_op jit(solution)/shard_map/gather_wt/pallas_call | solution.py:620
  529.4 9.8 %swap_wt.1 = bf16[8,128,256]{2,1,0:T(8,128)(2,1)} custom-call(bf16[8,128,256]{2,1,0:T(8,128)(2,1)} %bitcast.128), custom_call_target="tpu_custom_call" | custom-call | tf_op jit(solution)/shard_map/swap_wt/pallas_call | solution.py:731
  539.2 3.7 fusion
  543.3 3.4 convolution_convert_fusion.4
  546.7 8.3 %convolution_convert_fusion = bf16[2048,1408]{0,1:T(8,128)(2,1)S(1)} fusion(bf16[1024,2048]{1,0:T(8,128)(2,1)S(1)} %bitcast.124, bf16[1024,704]{1,0:T(8,128)(2,1)S(1)} %copy-done.36, bf16[1024,704]{1,0:T(8,128)(2,1)S(1)} %copy-done.34), kind=kOutput, calls=%fused_computation.1 | convolution fusion | flops 5914230784 | bytes 12845056 | tf_op jit(solution)/shard_map/dot_general | solution.py:894
  555.1 15.7 %pad_maximum_fusion = bf16[2048,2368]{0,1:T(8,128)(2,1)} fusion(bf16[2048,256]{0,1:T(8,128)(2,1)S(1)} %fusion, bf16[2048,704]{0,1:T(8,128)(2,1)S(1)} %convolution_convert_fusion.4, bf16[2048,1408]{0,1:T(8,128)(2,1)S(1)} %convolution_convert_fusion), kind=kLoop, calls=%fused_computation | loop fusion | flops 29097984 | bytes 19398656 | tf_op jit(solution)/shard_map/concatenate | solution.py:963
  570.8 13.3 %copy.104 = bf16[2048,2368]{1,0:T(8,128)(2,1)} copy(bf16[2048,2368]{0,1:T(8,128)(2,1)} %pad_maximum_fusion) | data formatting | bytes 19398656 | tf_op jit(solution)/shard_map/concatenate | solution.py:963
  584.0 52.8 %scatter_both_seq.3 = f32[128,2368]{1,0:T(8,128)} custom-call(bf16[16,128,2368]{2,1,0:T(8,128)(2,1)} %bitcast.113), custom_call_target="tpu_custom_call" | custom-call | tf_op jit(solution)/shard_map/scatter_both_seq/pallas_call | solution.py:705
  (145 shorter events, 50.6 us)
Async XLA Ops:
  0.6 211.6 %copy-start = (bf16[704,2048]{1,0:T(8,128)(2,1)S(1)}, bf16[704,2048]{1,0:T(8,128)(2,1)}, u32[]{:S(2)}) copy-start(bf16[704,2048]{1,0:T(8,128)(2,1)} %param.22) | copy-start | bytes 8650756
  146.9 11.7 %copy-start.3 = (bf16[1,128,2048]{2,1,0:T(8,128)(2,1)S(1)}, bf16[1,128,2048]{2,1,0:T(8,128)(2,1)}, u32[]{:S(2)}) copy-start(bf16[1,128,2048]{2,1,0:T(8,128)(2,1)} %param.12) | copy-start | bytes 1572868
  158.7 6.8 %copy-start.24 = (f32[2048]{0:T(1024)S(1)}, f32[2048]{0:T(1024)}, u32[]{:S(2)}) copy-start(f32[2048]{0:T(1024)} %param.19) | copy-start | bytes 24580
  158.7 6.9 %copy-start.27 = (f32[2048]{0:T(1024)S(1)}, f32[2048]{0:T(1024)}, u32[]{:S(2)}) copy-start(f32[2048]{0:T(1024)} %param.20) | copy-start | bytes 24580
  201.5 10.8 %copy-start.28 = (bf16[8,128,2048]{2,1,0:T(8,128)(2,1)S(1)}, bf16[8,128,2048]{2,1,0:T(8,128)(2,1)}, u32[]{:S(2)}) copy-start(bf16[8,128,2048]{2,1,0:T(8,128)(2,1)} %get-tuple-element.26) | copy-start | bytes 12582916
  201.5 15.2 %slice-start = ((s8[5767168]{0:T(1024)(128)(4,1)}), s8[4194304]{0:T(1024)(128)(4,1)S(1)}, s32[]{:S(2)}) async-start(s8[5767168]{0:T(1024)(128)(4,1)} %bitcast.142), calls=%async_computation | async-start | bytes 8388608
  212.3 4.4 slice-start.1
  216.7 8.9 %copy-start.33 = (bf16[1024,704]{1,0:T(8,128)(2,1)}, bf16[1024,704]{1,0:T(8,128)(2,1)S(1)}, u32[]{:S(2)}) copy-start(bf16[1024,704]{1,0:T(8,128)(2,1)S(1)} %get-tuple-element.95) | copy-start | bytes 4325380
  216.7 8.9 %copy-start.35 = (bf16[1024,704]{1,0:T(8,128)(2,1)}, bf16[1024,704]{1,0:T(8,128)(2,1)S(1)}, u32[]{:S(2)}) copy-start(bf16[1024,704]{1,0:T(8,128)(2,1)S(1)} %get-tuple-element.96) | copy-start | bytes 4325380
  216.7 41.7 %copy-start.31 = (bf16[1024,704]{1,0:T(8,128)(2,1)}, bf16[1024,704]{1,0:T(8,128)(2,1)S(1)}, u32[]{:S(2)}) copy-start(bf16[1024,704]{1,0:T(8,128)(2,1)S(1)} %get-tuple-element.97) | copy-start | bytes 4325380
  263.4 31.9 %copy-start.4 = (f32[128,2048]{1,0:T(8,128)S(1)}, f32[128,2048]{1,0:T(8,128)}, u32[]{:S(2)}) copy-start(f32[128,2048]{1,0:T(8,128)} %scatter_wt.4) | copy-start | bytes 3145732
  263.4 32.0 %copy-start.23 = (bf16[1,128,2048]{2,1,0:T(8,128)(2,1)S(1)}, bf16[1,128,2048]{2,1,0:T(8,128)(2,1)}, u32[]{:S(2)}) copy-start(bf16[1,128,2048]{2,1,0:T(8,128)(2,1)} %param.23) | copy-start | bytes 1572868
  370.6 2.2 copy-start.13
  370.9 2.2 copy-start.6
  370.9 2.5 copy-start.7
  371.0 2.8 copy-start.8
  371.0 3.1 copy-start.9
  375.2 7.4 %copy-start.19 = (bf16[2048,128]{1,0:T(8,128)(2,1)}, bf16[2048,128]{1,0:T(8,128)(2,1)S(1)}, u32[]{:S(2)}) copy-start(bf16[2048,128]{1,0:T(8,128)(2,1)S(1)} %get-tuple-element.98) | copy-start | bytes 1572868
  375.2 7.4 %copy-start.21 = (bf16[2048,128]{1,0:T(8,128)(2,1)}, bf16[2048,128]{1,0:T(8,128)(2,1)S(1)}, u32[]{:S(2)}) copy-start(bf16[2048,128]{1,0:T(8,128)(2,1)S(1)} %get-tuple-element.99) | copy-start | bytes 1572868
  382.6 43.4 %copy-start.25 = (f32[2048]{0:T(1024)S(1)}, f32[2048]{0:T(1024)}, u32[]{:S(2)}) copy-start(f32[2048]{0:T(1024)} %param.14) | copy-start | bytes 24580
  425.5 2.3 copy-start.5
  425.5 2.3 copy-start.16
  429.1 20.5 %copy-start.18 = (bf16[2048,128]{1,0:T(8,128)(2,1)S(1)}, bf16[2048,128]{1,0:T(8,128)(2,1)}, u32[]{:S(2)}) copy-start(bf16[2048,128]{1,0:T(8,128)(2,1)} %convert.13) | copy-start | bytes 1572868
  429.1 20.5 %copy-start.20 = (bf16[2048,128]{1,0:T(8,128)(2,1)S(1)}, bf16[2048,128]{1,0:T(8,128)(2,1)}, u32[]{:S(2)}) copy-start(bf16[2048,128]{1,0:T(8,128)(2,1)} %copy-done.19) | copy-start | bytes 1572868
  429.1 20.5 %copy-start.22 = (bf16[2048,128]{1,0:T(8,128)(2,1)S(1)}, bf16[2048,128]{1,0:T(8,128)(2,1)}, u32[]{:S(2)}) copy-start(bf16[2048,128]{1,0:T(8,128)(2,1)} %copy-done.21) | copy-start | bytes 1572868
  458.8 31.9 %copy-start.26 = (f32[1,128]{1,0:T(1,128)S(1)}, f32[1,128]{1,0:T(1,128)}, u32[]{:S(2)}) copy-start(f32[1,128]{1,0:T(1,128)} %small_sum.1) | copy-start | bytes 1540
  539.2 3.8 copy-start.29
  539.2 4.1 copy-start.32
  543.3 3.4 copy-start.15
  543.3 3.4 copy-start.34
  543.3 3.5 copy-start.36
  584.0 60.7 %copy-start.1 = (bf16[704,2048]{1,0:T(8,128)(2,1)S(1)}, bf16[704,2048]{1,0:T(8,128)(2,1)}, u32[]{:S(2)}) copy-start(bf16[704,2048]{1,0:T(8,128)(2,1)} %param.22) | copy-start | bytes 8650756
  (7 other events, 11.4 us)

commit v3 on v2

--- a/solution.py
+++ b/solution.py
@@ -33,6 +33,11 @@
         a, b = lax.rem(self.a + da + 4, 4), lax.rem(self.b + db, 2)
         return a * 2 + b if self.axis == "wt" else b * 4 + a
 
+def cuts(rows, split):
+    p = split or rows // 2
+    q = rows - p
+    return (0, p), (p, q), (0, p // 2), (p // 2, p // 2), (p, q // 2), (p + q // 2, q // 2)
+
 def remote(src, dst, ssem, rsem, k, target):
     return pltpu.make_async_remote_copy(src_ref=src, dst_ref=dst, send_sem=ssem.at[k], recv_sem=rsem.at[k], device_id=target, device_id_type=MESH)
 
@@ -42,11 +47,11 @@
         pl.semaphore_signal(bar, inc=1, device_id=t, device_id_type=MESH)
     pl.semaphore_wait(bar, len(targets))
 
-GATHER_MSGS = 18
-def gather_steps(pn, own, buf, rows, ssem, rsem, index=lambda j: j):
-    h, q = rows // 2, rows // 4
-    P_, Q_ = (0, h), (h, h)
-    P0, P1, Q0, Q1 = (0, q), (q, q), (h, q), (h + q, q)
+def pace(rows, cols):
+    return max(n for n in range(16, rows + 1, 16) if rows % n == 0 and n * cols <= 65536)
+
+def gather_steps(pn, own, buf, rows, ssem, rsem, index=lambda j: j, split=None):
+    P_, Q_, P0, P1, Q0, Q1 = cuts(rows, split)
     L, Rt, Y = pn.left, pn.right, pn.pair
     table = {
         0: (Y, (0, 0), P_, (0, 1)),
@@ -72,13 +77,19 @@
         return buf.at[index(pn.block(*d)), pl.ds(*r)]
     def send(k):
         t, d, r, _ = table[k]
+        if not r[1]:
+            return
         src = own.at[pl.ds(*r)] if d == (0, 0) else part(d, r)
         remote(src, part(d, r), ssem, rsem, k, t).start()
     def got(k):
         t, _, r, d = table[k]
+        if not r[1]:
+            return
         remote(part(d, r), part(d, r), ssem, rsem, k, t).wait_recv()
     def sent(k):
         t, d, r, _ = table[k]
+        if not r[1]:
+            return
         remote(part(d, r), part(d, r), ssem, rsem, k, t).wait_send()
     def first():
         for k in (0, 1, 2, 3, 4, 5): send(k)
@@ -94,11 +105,8 @@
         for k in range(18): sent(k)
     return steps, tail, done
 
-SUM_MSGS = 17
-def sum_steps(pn, buf, land, rows, ssem, rsem, out, index=lambda j: j, add=None):
-    h, q = rows // 2, rows // 4
-    P_, Q_ = (0, h), (h, h)
-    P0, P1, Q0, Q1 = (0, q), (q, q), (h, q), (h + q, q)
+def sum_steps(pn, buf, land, rows, ssem, rsem, out, index=lambda j: j, split=None):
+    P_, Q_, P0, P1, Q0, Q1 = cuts(rows, split)
     L, Rt, Y = pn.left, pn.right, pn.pair
     table = {}
     off = 0
@@ -114,7 +122,7 @@
     msg(12, L, (-2, 0), Q0, (-1, 0)); msg(13, Rt, (2, 0), Q1, (1, 0))
     msg(14, L, (-1, 0), Q_, (0, 0)); msg(15, Rt, (1, 0), Q_, (0, 0))
     msg(16, Y, (0, 1), P_, (0, 0))
-    assert off <= 7 * rows, off
+    assert off <= land.shape[0]
     def part(d, r):
         return buf.at[index(pn.block(*d)), pl.ds(*r)]
     def landing(k):
@@ -122,14 +130,22 @@
         return land.at[pl.ds(o, r[1])]
     def send(k):
         t, d, r, _, _ = table[k]
+        if not r[1]:
+            return
         remote(part(d, r), landing(k), ssem, rsem, k, t).start()
     def got(k):
+        if not table[k][2][1]:
+            return
         remote(landing(k), landing(k), ssem, rsem, k, table[k][0]).wait_recv()
     def sent(k):
+        if not table[k][2][1]:
+            return
         remote(landing(k), landing(k), ssem, rsem, k, table[k][0]).wait_send()
     def accumulate(d, r, ks, to=None):
+        if not r[1]:
+            return
         j = index(pn.block(*d))
-        step = 16
+        step = pace(r[1], buf.shape[2])
         def body(i, _):
             at_ = pl.multiple_of(r[0] + i * step, step)
             v = buf[j, pl.ds(at_, step)].astype(jnp.float32)
@@ -282,13 +298,14 @@
         scratch_shapes=[pltpu.VMEM((2, rows, 128), jnp.bfloat16)] * 4 + [pltpu.VMEM((128, rows), jnp.bfloat16), pltpu.VMEM((128, rows), jnp.float32)],
         compiler_params=pltpu.CompilerParams(vmem_limit_bytes=56 * 2**20), name="attend_back",
     )(q, k, v, start, ot, lse, do)
+SPLIT_A, SPLIT_C, SPLIT_D = 128, 96, 768
 ORDER = [(0, 0), (0, 1), (-1, 1), (1, 1), (-1, 0), (1, 0), (2, 0), (2, 1)]
 
 class Gather:
-    def __init__(self, pn, own, buf, rows, ss, rs, twin=None):
+    def __init__(self, pn, own, buf, rows, ss, rs, twin=None, split=None):
         self.pn, self.buf, self.twin = pn, buf, twin
         self.index = (lambda j: 2 * j + pn.c) if twin else (lambda j: j)
-        steps, tail, done = gather_steps(pn, own, buf, rows, ss, rs, self.index)
+        steps, tail, done = gather_steps(pn, own, buf, rows, ss, rs, self.index, split)
         self.done = done
         ready = {0: [1], 1: [2], 2: [3], 3: [4], 4: [5], 6: [6], 8: [7]}
         def follow(i, f):
@@ -433,6 +450,12 @@
     tables[1][...] = jnp.concatenate([-s, z8, nil] * 2, axis=0).T
     tables[2][...] = jnp.concatenate([z8, s, nil] * 2, axis=0).T
 
+def pump(*its):
+    for it in its:
+        f = next(it, None)
+        if f is not None:
+            f()
+
 def front_kernel(x, gain, shift, weight, bias, cs, start_ref, dy, ow,
                  rn, hw, q_ref, k_ref, v_ref, ot_ref, lse_ref, att, out_all, dy_all,
                  own, kept, vt, t0, t1, t2, ob, ox,
@@ -440,10 +463,10 @@
     sp, wp = Plane("seq"), Plane("wt")
     tok = x.shape[0]
     c, m = sp.c, sp.block(0, 0)
-    A = Gather(sp, own, rn, tok, ssA, rsA, (tsA, trA))
+    A = Gather(sp, own, rn, tok, ssA, rsA, (tsA, trA), SPLIT_A)
     begin, fetch, fetch_done = fetch_steps(wp, weight, hw, ssB, rsB, lsB)
-    C = Gather(wp, dy, dy_all, tok, ssC, rsC)
-    D = Gather(wp, ow, out_all, ow.shape[0], ssD, rsD, (tsD, trD))
+    C = Gather(wp, dy, dy_all, tok, ssC, rsC, None, SPLIT_C)
+    D = Gather(wp, ow, out_all, ow.shape[0], ssD, rsD, (tsD, trD), SPLIT_D)
     begin()
     chips = [at(j // 4, j % 4, c, wp.a, wp.b) for j in range(8)]
     bar = pltpu.get_barrier_semaphore()
@@ -471,11 +494,6 @@
     copies[1].wait()
     copies[2].wait()
     a, b, cc, d = iter(A.steps[1:]), iter(fetch[1:]), iter(C.steps), iter(D.steps)
-    def pump(*its):
-        for it in its:
-            f = next(it, None)
-            if f is not None:
-                f()
     pump(a, a, b, a, a, a, b, a, a, b, b, a, a, cc)
     def project(k):
         A.wait_twin(k)
@@ -599,6 +617,124 @@
         + [dma(n) for n in (18, 18, 8, 8, 18, 18, 3, 18, 18, 18, 18, 8, 8, 8, 8, 8, 8)] + [pltpu.SemaphoreType.DMA, dma(3)],
         compiler_params=params(cid), name="front",
     )(x, gain, shift, weight, bias, cs, start, dy, ow)
+TN = (((0,), (0,)), ((), ()))
+
+def middle_kernel(att, x, out_all, gain, shift, dy_all, wgu, wd,
+                  mid, dh2, ffp, joined,
+                  own, h2, wbuf, dga, tr, dh2p, land, ssG, rsG, ssS, rsS, lsw, ls):
+    wp = Plane("wt")
+    tok, width = mid.shape
+    hidden = wd.shape[0]
+    for t in (wp.left, wp.right, wp.pair):
+        pl.semaphore_signal(pltpu.get_barrier_semaphore(), inc=1, device_id=t, device_id_type=MESH)
+    def load(w, slot):
+        return pltpu.make_async_copy(out_all.at[pl.ds(2 * w, 2)], wbuf.at[slot], lsw.at[slot])
+    load(0, 0).start()
+    def project(w):
+        slot = w % 2
+        load(w, slot).wait()
+        if w < 7:
+            load(w + 1, 1 - slot).start()
+        cols = pl.ds(256 * w, 256)
+        y = jnp.dot(att[:, :width // 2], wbuf[slot, 0], preferred_element_type=jnp.float32)
+        y += jnp.dot(att[:, width // 2:], wbuf[slot, 1], preferred_element_type=jnp.float32)
+        mid[:, cols] = x[:, cols].astype(jnp.float32) + y
+    for w in range(8):
+        project(w)
+    def ln(i, _):
+        r = pl.ds(pl.multiple_of(i * 16, 16), 16)
+        own[r] = norm_rows(mid[r], gain[...], shift[...]).astype(jnp.bfloat16)
+        return 0
+    lax.fori_loop(0, tok // 16, ln, 0)
+    cp = pltpu.make_async_copy(own, h2.at[wp.block(0, 0)], ls)
+    cp.start()
+    pl.semaphore_wait(pltpu.get_barrier_semaphore(), 3)
+    G = Gather(wp, own, h2, tok, ssG, rsG)
+    part = hidden // 2
+    def chunk_up(da):
+        a = lax.rem(wp.a + da + 4, 4)
+        cols = pl.ds(pl.multiple_of(256 * a, 256), 256)
+        hc = h2[pl.ds(2 * a, 2)].reshape(2 * tok, width)
+        dc = dy_all[pl.ds(2 * a, 2)].reshape(2 * tok, width)
+        def tile(i, _):
+            r = pl.ds(pl.multiple_of(i * part, 16), part)
+            r2 = pl.ds(pl.multiple_of(hidden + i * part, 16), part)
+            r3 = pl.ds(pl.multiple_of(2 * hidden + i * part, 16), part)
+            g = lax.dot_general(wgu[r], hc, NT, preferred_element_type=jnp.float32)
+            u = lax.dot_general(wgu[r2], hc, NT, preferred_element_type=jnp.float32)
+            e = lax.dot_general(wd[r], dc, NT, preferred_element_type=jnp.float32)
+            sigma = 1.0 / (1.0 + jnp.exp(-g))
+            gs = g * sigma
+            dga[r, cols] = (e * u * sigma * (1.0 + g * (1.0 - sigma))).astype(jnp.bfloat16)
+            dga[r2, cols] = (e * gs).astype(jnp.bfloat16)
+            dga[r3, cols] = (gs * u).astype(jnp.bfloat16)
+            return 0
+        lax.fori_loop(0, 2, tile, 0)
+    def chunk_down(da):
+        a = lax.rem(wp.a + da + 4, 4)
+        cols = pl.ds(pl.multiple_of(256 * a, 256), 256)
+        def flip(i, _):
+            r = pl.ds(pl.multiple_of(i * 128, 128), 128)
+            tr[:, r] = dga[r, cols].astype(jnp.float32).T.astype(jnp.bfloat16)
+            return 0
+        lax.fori_loop(0, 3 * hidden // 128, flip, 0)
+        last = 3 * hidden // 128 * 128
+        tr[:, last:] = dga[last:, cols].astype(jnp.float32).T.astype(jnp.bfloat16)
+        def tile(i, _):
+            n = pl.ds(pl.multiple_of(i * 512, 512), 512)
+            y = jnp.dot(tr[:, :2 * hidden], wgu[:, n], preferred_element_type=jnp.float32)
+            dh2p[pl.ds(2 * a, 2), :, n] = y.astype(jnp.bfloat16).reshape(2, tok, 512)
+            y = jnp.dot(tr[:, 2 * hidden:], wd[:, n], preferred_element_type=jnp.float32)
+            ffp[pl.ds(2 * a, 2), :, n] = y.astype(jnp.bfloat16).reshape(2, tok, 512)
+            return 0
+        lax.fori_loop(0, width // 512, tile, 0)
+    S = G.steps
+    S[0]()
+    cp.wait()
+    for f in S[1:6]:
+        f()
+    S[10]()
+    chunk_up(0)
+    S[6](); S[7]()
+    chunk_down(0)
+    S[8](); S[9](); S[11](); S[12]()
+    chunk_up(-1)
+    chunk_down(-1)
+    chunk_up(1)
+    chunk_down(1)
+    for f in S[13:]:
+        f()
+    chunk_up(2)
+    chunk_down(2)
+    G.finish()
+    R, done = sum_steps(wp, dh2p, land, tok, ssS, rsS, dh2)
+    def weights(lo, hi):
+        def one(j, _):
+            f = pl.ds(pl.multiple_of(256 * j, 256), 256)
+            for k, other in ((0, h2), (1, h2), (2, dy_all)):
+                r = pl.ds(hidden * k, hidden)
+                y = jnp.dot(dga[r], other[:, :, f].reshape(8 * tok, 256), preferred_element_type=jnp.float32).astype(jnp.bfloat16)
+                joined[2 * j, r] = y[:, :128]
+                joined[2 * j + 1, r] = y[:, 128:]
+            return 0
+        lax.fori_loop(lo, hi, one, 0)
+    R[0]()
+    weights(0, 2); R[1](); R[2](); weights(2, 3); R[3](); weights(3, 4); R[4](); weights(4, 6); R[5](); weights(6, 8); R[6]()
+    done()
+
+def middle_part(cid, att, x, out_all, gain, shift, dy_all, wgu, wd):
+    tok, width = x.shape
+    hidden = wd.shape[0]
+    f, b16, f32, vm = jax.ShapeDtypeStruct, jnp.bfloat16, jnp.float32, pltpu.VMEM
+    return pl.pallas_call(
+        middle_kernel,
+        out_shape=(f((tok, width), f32), f((tok, width), f32), f((8, tok, width), b16), f((16, 3 * hidden, 128), b16)),
+        in_specs=[VM, VM, ANY, VM, VM, VM, VM, VM], out_specs=(VM,) * 4,
+        scratch_shapes=[vm((tok, width), b16), vm((8, tok, width), b16), vm((2, 2) + out_all.shape[1:], b16), vm((3 * hidden, 8 * tok), b16),
+                        vm((2 * tok, 3 * hidden), b16), vm((8, tok, width), b16), vm((7 * tok, width), b16)]
+        + [dma(n) for n in (18, 18, 17, 17, 2)] + [pltpu.SemaphoreType.DMA],
+        compiler_params=params(cid), name="middle",
+    )(att, x, out_all, gain, shift, dy_all, wgu, wd)
 def params(cid):
     return pltpu.CompilerParams(collective_id=cid, has_side_effects=True, vmem_limit_bytes=56 * 2**20)
 
@@ -688,11 +824,12 @@
     for k in range(8):
         j = 2 * pn.block(*order[k]) + pn.c
         remote(tland.at[k], tland.at[k], ts, tr, k, pn.twin).wait_recv()
+        step = pace(rows, x.shape[2])
         def body(i, _):
-            r = pl.ds(pl.multiple_of(i * 16, 16), 16)
+            r = pl.ds(pl.multiple_of(i * step, 16), step)
             buf[j, r] = (buf[j, r].astype(jnp.float32) + tland[k, r].astype(jnp.float32)).astype(buf.dtype)
             return 0
-        lax.fori_loop(0, rows // 16, body, 0)
+        lax.fori_loop(0, rows // step, body, 0)
     steps, done = sum_steps(pn, buf, land, rows, ss, rs, o, lambda j: 2 * j + pn.c)
     for f in steps:
         f()
@@ -917,24 +1054,11 @@
         0, layer_in.reshape(tok, width), norm_one_gain.reshape(1, width), norm_one_shift.reshape(1, width), qkv_weight, bias, cs, start, upstream, half)
     row_normed = row_normed.reshape(rows, width)
     out_all = out_all.reshape(8, 2, width // 2, 256)
-    all_up = all_up.reshape(8 * tok, width)
-    branch = jnp.einsum("tck,wckn->twn", attended.reshape(tok, 2, width // 2), out_all, preferred_element_type=f32).reshape(tok, width)
-    middle = inputs + branch
-    normed_two, scaled_two, inverse_two = layer_norm_parts(middle, norm_two_gain, norm_two_shift)
-    all_two = gather("wt", 4, normed_two.astype(bf16)).reshape(8 * tok, width)
-    weight_gu = gate_up_weight.reshape(width, 2 * hidden)
-    gu = jnp.dot(all_two, weight_gu, preferred_element_type=f32)
-    g, u = gu[:, :hidden], gu[:, hidden:]
-    sigma = jax.nn.sigmoid(g)
-    act = (g * sigma * u).astype(bf16)
-    ffn_part = jnp.dot(act, down_weight, preferred_element_type=f32).astype(bf16)
-    dact = contract_last(all_up, down_weight)
-    dg = (dact * u * sigma * (1.0 + g * (1.0 - sigma))).astype(bf16)
-    du = (dact * g * sigma).astype(bf16)
-    dgu = jnp.concatenate([dg, du], axis=1)
-    dh2_part = contract_last(dgu, weight_gu).astype(bf16)
-    dh2 = scatter("wt", 6, dh2_part.reshape(8, tok, width))
-    ffn_out = scatter("wt", 7, ffn_part.reshape(8, tok, width))
+    middle, dh2, ffn_part, joined = middle_part(
+        4, attended, layer_in.reshape(tok, width), out_all.reshape(16, width // 2, 256), norm_two_gain.reshape(1, width),
+        norm_two_shift.reshape(1, width), all_up, gate_up_weight.transpose(1, 2, 0).reshape(2 * hidden, width), down_weight)
+    _, scaled_two, inverse_two = layer_norm_parts(middle, norm_two_gain, norm_two_shift)
+    ffn_out = scatter("wt", 7, ffn_part)
     layer_out = (middle + ffn_out).astype(bf16).reshape(1, tok, width)
     gain_two = jnp.sum(dh2 * scaled_two, axis=0)
     shift_two = jnp.sum(dh2, axis=0)
@@ -958,13 +1082,10 @@
     all_att = gather("wt", 12, attended).reshape(8 * tok, width)
     da_cols = swap("wt", 8, 13, da.reshape(tok, 8, 256).transpose(1, 0, 2)).reshape(8 * tok, 256)
     out_part = contract_first(all_att, da_cols).astype(bf16)
-    gate_part = contract_first(all_two, dgu).astype(bf16)
-    down_part = contract_first(all_up, act).astype(bf16)
-    joined = jnp.concatenate([gate_part, down_part, out_part], axis=1).reshape(16, 128, 3 * hidden + 256)
+    out_grad = scatter_both("seq", 16, out_part.reshape(16, 128, 256))
     joined = scatter_both("seq", 14, joined)
-    gate_grad = joined[:, :2 * hidden].reshape(128, 2, hidden)
-    down_grad = joined[:, 2 * hidden:3 * hidden].T
-    out_grad = joined[:, 3 * hidden:]
+    gate_grad = joined[:2 * hidden].reshape(2, hidden, 128).transpose(2, 0, 1)
+    down_grad = joined[2 * hidden:]
     bias_grad = lax.dynamic_update_slice(jnp.zeros((3, 16, 128), f32), jnp.sum(dproj.astype(f32), axis=0).reshape(3, 1, 128), (0, s, 0))
     blocks = [t.reshape(16, 8, -1) for t in (gain_one, shift_one, bias_grad, gain_two, shift_two, jnp.zeros((16 * 8 * 16,), f32))]
     small = small_sum(15, jnp.concatenate(blocks, axis=2).transpose(1, 0, 2))[0]

time: 655 us -> 597 us (0.911)
  matrix products: 73.4 us -> 28.5 us
  Pallas kernels: 458 us -> 494 us
  local copies, waits for them, and re-layouts: 66.4 us -> 36.5 us
  other arithmetic: 45.4 us -> 27.5 us
    pallas_call x0 -> x1, Pallas kernels: none -> 101 us  [middle_part(): pl.pallas_call(middle_kernel, out_shape=(f((tok, width), f32), f((tok, wi...]
    pallas_call x2 -> x1, Pallas kernels: 72 us -> 34.6 us  [gather(): pl.pallas_call(functools.partial(gather_kernel, axis), out_shape=jax.Shap...]
    pallas_call x3 -> x2, Pallas kernels: 78.3 us -> 44.9 us  [scatter(): pl.pallas_call(functools.partial(scatter_kernel, axis), out_shape=jax.Sha...]
    dot_general x3 -> x0, matrix products: 22.3 us -> none  [the longest x1 10.7 us: per_device(): gu = jnp.dot(all_two, weight_gu, preferred_element_type=f32)]
    concatenate x1 -> x0, other arithmetic: 15.7 us -> none  [per_device(): jnp.concatenate([gate_part, down_part, out_part], axis=1)]
    concatenate x1 -> x0, local copies, waits for them, and re-layouts: 13.3 us -> none  [per_device(): jnp.concatenate([gate_part, down_part, out_part], axis=1)]
    dot_general x3 -> x1, matrix products: 20.2 us -> 8.4 us  [contract_last(): lax.dot_general(left, right, (((1,), (1,)), ((), ())), preferred_element_...]
    dot_general x1 -> x0, local copies, waits for them, and re-layouts: 11.7 us -> none  [per_device(): jnp.einsum('tck,wckn->twn', attended.reshape(tok, 2, width // 2), out_all...]
where the time goes in v3:
time: 597 us; the launch traced here: 588 us
  Pallas kernels  494 us (83%)
  local copies, waits for them, and re-layouts  36.5 us (6%)
  matrix products  28.5 us (5%)
  other arithmetic  27.5 us (5%)
    pallas_call x1, Pallas kernels, front(): pl.pallas_call(front_kernel, out_shape=(f((16, tok, width), b16), f((widt...  118 us
    pallas_call x3, Pallas kernels, scatter_both(): pl.pallas_call(functools.partial(scatter_both_kernel, axis), out_shape=ja...  106 us
    pallas_call x1, Pallas kernels, middle_part(): pl.pallas_call(middle_kernel, out_shape=(f((tok, width), f32), f((tok, wi...  101 us
    pallas_call x2, Pallas kernels, scatter(): pl.pallas_call(functools.partial(scatter_kernel, axis), out_shape=jax.Sha...  44.9 us
    pallas_call x2, Pallas kernels, swap(): pl.pallas_call(functools.partial(swap_kernel, axis, n), out_shape=jax.Sha...  36 us
    pallas_call x1, Pallas kernels, gather(): pl.pallas_call(functools.partial(gather_kernel, axis), out_shape=jax.Shap...  34.6 us
    pallas_call x1, Pallas kernels, attention_backward(): pl.pallas_call(attn_bwd, out_shape=(f((rows, 128), jnp.float32),) * 3, in...  27.4 us
    pallas_call x1, Pallas kernels, small_sum(): pl.pallas_call(small_kernel, out_shape=jax.ShapeDtypeStruct((1, 128), f),...  14.5 us

profile of v3, /device:TPU:1, one launch (start us, length us, event | category | flops | bytes accessed | tf_op | source)
XLA Modules:
  0.0 587.7 jit_solution(6776822996980006548)
XLA Ops:
  5.3 2.6 subtract_convert_fusion
  7.9 5.3 fusion.22
  14.6 118.1 %front.1 = (bf16[16,128,2048]{2,1,0:T(8,128)(2,1)}, bf16[2048,384]{1,0:T(8,128)(2,1)}, bf16[2048,128]{1,0:T(8,128)(2,1)}, bf16[2048,128]{1,0:T(8,128)(2,1)}, bf1...) custom-call(bf16[128,2048]{1,0:T(8,128)(2,1)} %bitcast.89, ...), custom_call_target="tpu_custom_call" | custom-call | tf_op jit(solution)/shard_map/front/pallas_call | solution.py:610
  132.7 101.1 %middle.1 = (f32[128,2048]{1,0:T(8,128)}, f32[128,2048]{1,0:T(8,128)}, bf16[8,128,2048]{2,1,0:T(8,128)(2,1)}, bf16[16,2112,128]{2,1,0:T(8,128)(2,1)}) custom-call(bf16[128,2048]{1,0:T(8,128)(2,1)} %get-tuple-element.28.att.x, bf16[128,2048]{1,0:T(8,128)(2,1)} %bitcast.90, bf16[16,1024,256]{2,1,0:T(8,128)(2,1)} %get-tuple-element.29.out_all, ...), custom_call_target="tpu_custom_call" | custom-call | tf_op jit(solution)/shard_map/middle/pallas_call | solution.py:729
  233.9 29.3 %scatter_wt.2 = f32[128,2048]{1,0:T(8,128)} custom-call(bf16[8,128,2048]{2,1,0:T(8,128)(2,1)} %get-tuple-element.32.x), custom_call_target="tpu_custom_call" | custom-call | tf_op jit(solution)/shard_map/scatter_wt/pallas_call | solution.py:807
  263.7 1.9 multiply_reduce_fusion
  265.6 2.0 fusion.25
  268.9 6.4 %fusion.1 = bf16[128,2,1024]{2,0,1:T(8,128)(2,1)S(1)} fusion(bf16[128,8,256,1]{0,2,3,1:T(8,128)(2,1)S(1)} %bitcast.93, bf16[8,2,1024,256]{3,2,1,0:T(8,128)(2,1)} %bitcast.88), kind=kOutput, calls=%fused_computation.11 | convolution fusion | flops 1074003968 | bytes 9437184 | tf_op jit(solution)/shard_map/twn,wckn->tck/dot_general | solution.py:1067
  276.6 18.2 %swap_seq.1 = bf16[16,128,128]{2,1,0:T(8,128)(2,1)} custom-call(bf16[16,128,128]{2,1,0:T(8,128)(2,1)} %bitcast.97), custom_call_target="tpu_custom_call" | custom-call | tf_op jit(solution)/shard_map/swap_seq/pallas_call | solution.py:868
  294.9 27.4 %attend_back.1 = (f32[2048,128]{1,0:T(8,128)}, f32[2048,128]{1,0:T(8,128)}, f32[2048,128]{1,0:T(8,128)}) custom-call(bf16[2048,128]{1,0:T(8,128)(2,1)} %get-tuple-element.34.q_ref, bf16[2048,128]{1,0:T(8,128)(2,1)} %get-tuple-element.35.k_ref, bf16[2048,128]{1,0:T(8,128)(2,1)} %get-tuple-element.36.v_ref, s32[1,2048]{1,0:T(1,128)} %get-tuple-element.91.start_ref, ...), custom_call_target="tpu_custom_call" | custom-call | tf_op jit(solution)/shard_map/attend_back/pallas_call | solution.py:295
  323.7 1.7 fusion.29
  325.4 1.7 fusion.26
  327.1 1.6 fusion.27
  328.7 1.6 fusion.28
  330.5 4.4 concatenate.38
  334.9 4.3 concatenate.36
  339.3 3.2 concatenate.34
  342.5 5.8 fusion.16
  348.4 9.1 %convolution_convert_fusion.1 = bf16[2048,384]{1,0:T(8,128)(2,1)} fusion(bf16[2048,2048]{1,0:T(8,128)(2,1)} %bitcast.112, bf16[2048,128]{1,0:T(8,128)(2,1)S(1)} %convert.13, bf16[2048,128]{1,0:T(8,128)(2,1)S(1)} %get-tuple-element.93, bf16[2048,128]{1,0:T(8,128)(2,1)S(1)} %get-tuple-element.92), kind=kOutput, calls=%fused_computation.2 | convolution fusion | flops 3226730496 | bytes 11534336 | tf_op jit(solution)/shard_map/dot_general | solution.py:1031
  357.5 15.5 %scatter_wt.3 = f32[256,384]{1,0:T(8,128)} custom-call(bf16[8,256,384]{2,1,0:T(8,128)(2,1)} %bitcast.101), custom_call_target="tpu_custom_call" | custom-call | tf_op jit(solution)/shard_map/scatter_wt/pallas_call | solution.py:807
  374.8 10.7 %place_qkv.1 = bf16[6,128,128]{2,1,0:T(8,128)(2,1)} custom-call(bf16[2,3,128,128]{3,2,1,0:T(8,128)(2,1)} %bitcast.103), custom_call_target="tpu_custom_call" | custom-call | tf_op jit(solution)/shard_map/place_qkv/pallas_call | solution.py:955
  388.6 17.8 %swap_wt.1 = bf16[8,128,256]{2,1,0:T(8,128)(2,1)} custom-call(bf16[8,128,256]{2,1,0:T(8,128)(2,1)} %bitcast.98), custom_call_target="tpu_custom_call" | custom-call | tf_op jit(solution)/shard_map/swap_wt/pallas_call | solution.py:868
  406.4 34.6 %gather_wt.1 = bf16[8,128,2048]{2,1,0:T(8,128)(2,1)} custom-call(bf16[128,2048]{1,0:T(8,128)(2,1)} %get-tuple-element.28.att.x), custom_call_target="tpu_custom_call" | custom-call | tf_op jit(solution)/shard_map/gather_wt/pallas_call | solution.py:756
  441.0 4.5 fusion
  445.5 16.2 %scatter_both_seq.4 = f32[128,256]{1,0:T(8,128)} custom-call(bf16[16,128,256]{2,1,0:T(8,128)(2,1)} %bitcast.102), custom_call_target="tpu_custom_call" | custom-call | tf_op jit(solution)/shard_map/scatter_both_seq/pallas_call | solution.py:842
  462.3 8.4 %convolution_convert_fusion = bf16[2048,2048]{1,0:T(8,128)(2,1)} fusion(bf16[2048,384]{1,0:T(8,128)(2,1)} %get-tuple-element.42, bf16[2048,128]{1,0:T(8,128)(2,1)S(1)} %convert.13, bf16[2048,128]{1,0:T(8,128)(2,1)S(1)} %get-tuple-element.93, bf16[2048,128]{1,0:T(8,128)(2,1)S(1)} %get-tuple-element.92), kind=kOutput, calls=%fused_computation | convolution fusion | flops 3230138368 | bytes 11534336 | tf_op jit(solution)/shard_map/dot_general | solution.py:1035
  470.7 44.8 %scatter_both_seq.3 = f32[128,2048]{1,0:T(8,128)} custom-call(bf16[16,128,2048]{2,1,0:T(8,128)(2,1)} %bitcast.91), custom_call_target="tpu_custom_call" | custom-call | tf_op jit(solution)/shard_map/scatter_both_seq/pallas_call | solution.py:842
  516.1 1.8 fusion.12
  519.1 14.5 %small_sum.1 = f32[1,128]{1,0:T(1,128)} custom-call(f32[8,16,128]{2,1,0:T(8,128)} %bitcast.105), custom_call_target="tpu_custom_call" | custom-call | tf_op jit(solution)/shard_map/small_sum/pallas_call | solution.py:981
  537.6 45.2 %scatter_both_seq.5 = f32[2112,128]{1,0:T(8,128)} custom-call(bf16[16,2112,128]{2,1,0:T(8,128)(2,1)} %get-tuple-element.44.x), custom_call_target="tpu_custom_call" | custom-call | tf_op jit(solution)/shard_map/scatter_both_seq/pallas_call | solution.py:842
  582.8 2.0 slice.82
  584.8 1.7 slice.83
  (92 shorter events, 22.3 us)
Async XLA Ops:
  0.6 1.2 copy-start
  13.3 119.4 %copy-start.3 = (f32[8,2048]{0,1:T(8,128)}, f32[8,2048]{0,1:T(8,128)S(1)}, u32[]{:S(2)}) copy-start(f32[8,2048]{0,1:T(8,128)S(1)} %get-tuple-element.104) | copy-start | bytes 196612
  233.8 29.4 %copy-start.4 = (f32[128,2048]{1,0:T(8,128)S(1)}, f32[128,2048]{1,0:T(8,128)}, u32[]{:S(2)}) copy-start(f32[128,2048]{1,0:T(8,128)} %get-tuple-element.31) | copy-start | bytes 3145732
  233.8 29.8 %copy-start.17 = (f32[2048]{0:T(1024)S(1)}, f32[2048]{0:T(1024)}, u32[]{:S(2)}) copy-start(f32[2048]{0:T(1024)} %param.19) | copy-start | bytes 24580
  263.2 2.3 copy-start.10
  263.4 2.2 copy-start.11
  263.4 2.2 copy-start.13
  268.9 6.5 %copy-start.6 = (bf16[128,2048]{0,1:T(8,128)(2,1)}, bf16[128,2048]{0,1:T(8,128)(2,1)S(1)}, u32[]{:S(2)}) copy-start(bf16[128,2048]{0,1:T(8,128)(2,1)S(1)} %copy.64) | copy-start | bytes 1572868
  322.3 3.0 copy-start.9
  339.2 3.2 copy-start.8
  342.5 5.9 copy-start.14
  357.5 30.1 %copy-start.7 = (bf16[128,2048]{0,1:T(8,128)(2,1)S(1)}, bf16[128,2048]{0,1:T(8,128)(2,1)}, u32[]{:S(2)}) copy-start(bf16[128,2048]{0,1:T(8,128)(2,1)} %copy-done.6) | copy-start | bytes 1572868
  406.4 34.6 %copy-start.16 = (bf16[8,128,256]{2,1,0:T(8,128)(2,1)S(1)}, bf16[8,128,256]{2,1,0:T(8,128)(2,1)}, u32[]{:S(2)}) copy-start(bf16[8,128,256]{2,1,0:T(8,128)(2,1)} %swap_wt.1) | copy-start | bytes 1572868
  470.7 44.8 %copy-start.2 = (bf16[1,128,2048]{2,1,0:T(8,128)(2,1)S(1)}, bf16[1,128,2048]{2,1,0:T(8,128)(2,1)}, u32[]{:S(2)}) copy-start(bf16[1,128,2048]{2,1,0:T(8,128)(2,1)} %param.12) | copy-start | bytes 1572868
  470.7 45.3 %copy-start.18 = (f32[2048]{0:T(1024)S(1)}, f32[2048]{0:T(1024)}, u32[]{:S(2)}) copy-start(f32[2048]{0:T(1024)} %param.14) | copy-start | bytes 24580
  515.6 20.7 %copy-start.5 = (f32[128,2048]{1,0:T(8,128)S(1)}, f32[128,2048]{1,0:T(8,128)}, u32[]{:S(2)}) copy-start(f32[128,2048]{1,0:T(8,128)} %scatter_both_seq.3) | copy-start | bytes 3145732
  515.6 20.7 %copy-start.12 = (f32[128,2048]{1,0:T(8,128)S(1)}, f32[128,2048]{1,0:T(8,128)}, u32[]{:S(2)}) copy-start(f32[128,2048]{1,0:T(8,128)} %get-tuple-element.89) | copy-start | bytes 3145732
  537.6 48.9 %copy-start.15 = (f32[128,256]{1,0:T(8,128)S(1)}, f32[128,256]{1,0:T(8,128)}, u32[]{:S(2)}) copy-start(f32[128,256]{1,0:T(8,128)} %scatter_both_seq.4) | copy-start | bytes 393220
  537.6 49.6 %copy-start.1 = (bf16[2048,256]{1,0:T(8,128)(2,1)S(1)}, bf16[2048,256]{1,0:T(8,128)(2,1)}, u32[]{:S(2)}) copy-start(bf16[2048,256]{1,0:T(8,128)(2,1)} %param.18) | copy-start | bytes 3145732

commit v4 on v3

--- a/solution.py
+++ b/solution.py
@@ -47,8 +47,14 @@
         pl.semaphore_signal(bar, inc=1, device_id=t, device_id_type=MESH)
     pl.semaphore_wait(bar, len(targets))
 
+def repeat(n, body):
+    if n == 1:
+        body(0, 0)
+    else:
+        lax.fori_loop(0, n, body, 0)
+
 def pace(rows, cols):
-    return max(n for n in range(16, rows + 1, 16) if rows % n == 0 and n * cols <= 65536)
+    return max(n for n in range(16, rows + 1, 16) if rows % n == 0 and n * cols <= 300000)
 
 def gather_steps(pn, own, buf, rows, ssem, rsem, index=lambda j: j, split=None):
     P_, Q_, P0, P1, Q0, Q1 = cuts(rows, split)
@@ -147,16 +153,16 @@
         j = index(pn.block(*d))
         step = pace(r[1], buf.shape[2])
         def body(i, _):
-            at_ = pl.multiple_of(r[0] + i * step, step)
+            at_ = pl.multiple_of(r[0] + i * step, 16)
             v = buf[j, pl.ds(at_, step)].astype(jnp.float32)
             for k in ks:
-                v = v + land[pl.ds(pl.multiple_of(table[k][3] + i * step, step), step)].astype(jnp.float32)
+                v = v + land[pl.ds(pl.multiple_of(table[k][3] + i * step, 16), step)].astype(jnp.float32)
             if to is None:
                 buf[j, pl.ds(at_, step)] = v.astype(buf.dtype)
             else:
                 to[pl.ds(at_, step)] = v.astype(to.dtype)
             return 0
-        lax.fori_loop(0, r[1] // step, body, 0)
+        repeat(r[1] // step, body)
     def s0():
         for k in range(8): send(k)
     def s1():
@@ -179,7 +185,7 @@
         for k in range(17): sent(k)
     return [s0, s1, s2, s3, s4, s5, s6], done
 ANY = pl.BlockSpec(memory_space=pl.ANY)
-QB, KB = 512, 256
+QB, KB = 512, 512
 MASKED = -1e30
 NT = (((1,), (1,)), ((), ()))
 
@@ -195,109 +201,8 @@
     query = i * QB + lax.broadcasted_iota(jnp.int32, (KB, QB), 1)
     return (key <= query) & (key >= start)
 
-def attn_fwd(q_ref, k_ref, v_ref, start_ref, o_ref, ot_ref, lse_ref, kept, vt):
-    halves(k_ref, kept)
-    vt[...] = v_ref[...].astype(jnp.float32).T.astype(jnp.bfloat16)
-    n = q_ref.shape[0] // QB
-    for i in range(n):
-        q = q_ref[QB * i:QB * (i + 1)]
-        start = start_ref[:, QB * i:QB * (i + 1)]
-        def step(masked, j, carry):
-            r = pl.ds(pl.multiple_of(j * KB, KB), KB)
-            out = []
-            for h in range(2):
-                m, l, acc = carry[h]
-                s = lax.dot_general(kept[h, r], q, NT, preferred_element_type=jnp.float32)
-                if masked:
-                    s = jnp.where(allowed(i, j, start), s, MASKED)
-                top = jnp.maximum(m, jnp.max(s, axis=0, keepdims=True))
-                p = jnp.exp(s - top)
-                fade = jnp.exp(m - top)
-                l = l * fade + jnp.sum(p, axis=0, keepdims=True)
-                acc = acc * fade + jnp.dot(vt[64 * h:64 * h + 64, r], p.astype(jnp.bfloat16), preferred_element_type=jnp.float32)
-                out.append((top, l, acc))
-            return tuple(out)
-        one = (jnp.full((1, QB), MASKED, jnp.float32), jnp.zeros((1, QB), jnp.float32), jnp.zeros((64, QB), jnp.float32))
-        carry = (one, one)
-        if i == n - 1:
-            carry = lax.fori_loop(0, 2 * i + 2, functools.partial(step, True), carry)
-        else:
-            if i:
-                carry = step(True, 0, carry)
-                carry = lax.fori_loop(1, 2 * i, functools.partial(step, False), carry)
-            carry = lax.fori_loop(2 * i, 2 * i + 2, functools.partial(step, True), carry)
-        cols = pl.ds(QB * i, QB)
-        for h in range(2):
-            m, l, acc = carry[h]
-            ot_ref[64 * h:64 * h + 64, cols] = acc / l
-            lse_ref[h:h + 1, cols] = m + jnp.log(l)
-        o_ref[QB * i:QB * (i + 1)] = ot_ref[:, cols].T.astype(jnp.bfloat16)
-
-def attn_bwd(q_ref, k_ref, v_ref, start_ref, ot_ref, lse_ref, do_ref, dq_ref, dk_ref, dv_ref, keptk, keptv, keptq, keptd, kt, dot_):
-    halves(k_ref, keptk)
-    halves(v_ref, keptv)
-    halves(q_ref, keptq)
-    halves(do_ref, keptd)
-    kt[...] = k_ref[...].astype(jnp.float32).T.astype(jnp.bfloat16)
-    dot_[...] = do_ref[...].astype(jnp.float32).T
-    dk_ref[...] = jnp.zeros_like(dk_ref)
-    dv_ref[...] = jnp.zeros_like(dv_ref)
-    n = q_ref.shape[0] // QB
-    for i in range(n):
-        rows = pl.ds(QB * i, QB)
-        q = q_ref[rows]
-        do = do_ref[rows]
-        start = start_ref[:, rows]
-        both = ot_ref[:, rows] * dot_[:, rows]
-        inner = [jnp.sum(both[64 * h:64 * h + 64], axis=0, keepdims=True) for h in range(2)]
-        lse = [lse_ref[h:h + 1, rows] for h in range(2)]
-        def step(masked, j, carry):
-            r = pl.ds(pl.multiple_of(j * KB, KB), KB)
-            out, ps, ds = [], [], []
-            for h in range(2):
-                s = lax.dot_general(keptk[h, r], q, NT, preferred_element_type=jnp.float32)
-                if masked:
-                    s = jnp.where(allowed(i, j, start), s, MASKED)
-                p = jnp.exp(s - lse[h])
-                dp = lax.dot_general(keptv[h, r], do, NT, preferred_element_type=jnp.float32)
-                g = (p * (dp - inner[h])).astype(jnp.bfloat16)
-                out.append(carry[h] + jnp.dot(kt[64 * h:64 * h + 64, r], g, preferred_element_type=jnp.float32))
-                ps.append(p.astype(jnp.bfloat16))
-                ds.append(g)
-            dv_ref[r] += sum(jnp.dot(ps[h], keptd[h, rows], preferred_element_type=jnp.float32) for h in range(2))
-            dk_ref[r] += sum(jnp.dot(ds[h], keptq[h, rows], preferred_element_type=jnp.float32) for h in range(2))
-            return tuple(out)
-        carry = (jnp.zeros((64, QB), jnp.float32),) * 2
-        if i == n - 1:
-            carry = lax.fori_loop(0, 2 * i + 2, functools.partial(step, True), carry)
-        else:
-            if i:
-                carry = step(True, 0, carry)
-                carry = lax.fori_loop(1, 2 * i, functools.partial(step, False), carry)
-            carry = lax.fori_loop(2 * i, 2 * i + 2, functools.partial(step, True), carry)
-        dq_ref[rows] = jnp.concatenate(carry, axis=0).T
-
 VM = pl.BlockSpec(memory_space=pltpu.VMEM)
 
-def attention_forward(q, k, v, start):
-    rows = q.shape[0]
-    f = jax.ShapeDtypeStruct
-    return pl.pallas_call(
-        attn_fwd, out_shape=(f((rows, 128), jnp.bfloat16), f((128, rows), jnp.float32), f((8, rows), jnp.float32)),
-        in_specs=[VM] * 4, out_specs=(VM,) * 3,
-        scratch_shapes=[pltpu.VMEM((2, rows, 128), jnp.bfloat16), pltpu.VMEM((128, rows), jnp.bfloat16)],
-        compiler_params=pltpu.CompilerParams(vmem_limit_bytes=56 * 2**20), name="attend",
-    )(q, k, v, start)
-
-def attention_backward(q, k, v, start, ot, lse, do):
-    rows = q.shape[0]
-    f = jax.ShapeDtypeStruct
-    return pl.pallas_call(
-        attn_bwd, out_shape=(f((rows, 128), jnp.float32),) * 3,
-        in_specs=[VM] * 7, out_specs=(VM,) * 3,
-        scratch_shapes=[pltpu.VMEM((2, rows, 128), jnp.bfloat16)] * 4 + [pltpu.VMEM((128, rows), jnp.bfloat16), pltpu.VMEM((128, rows), jnp.float32)],
-        compiler_params=pltpu.CompilerParams(vmem_limit_bytes=56 * 2**20), name="attend_back",
-    )(q, k, v, start, ot, lse, do)
 SPLIT_A, SPLIT_C, SPLIT_D = 128, 96, 768
 ORDER = [(0, 0), (0, 1), (-1, 1), (1, 1), (-1, 0), (1, 0), (2, 0), (2, 1)]
 
@@ -536,17 +441,9 @@
         step = functools.partial(attend_step, kept, vt, q, start, i)
         one = (jnp.full((1, QB), MASKED, jnp.float32), jnp.zeros((1, QB), jnp.float32), jnp.zeros((64, QB), jnp.float32))
         carry = (one, one)
-        if i == n - 1:
-            for j in range(0, 2 * i + 2, 2):
-                carry = lax.fori_loop(j, j + 2, functools.partial(step, True), carry)
-                pump(cc, d)
-        else:
-            if i:
-                carry = step(True, 0, carry)
-                carry = lax.fori_loop(1, 2 * i, functools.partial(step, False), carry)
-                pump(cc, d) if i == 1 else pump(cc, cc, d)
-            carry = lax.fori_loop(2 * i, 2 * i + 2, functools.partial(step, True), carry)
-            pump(cc, cc)
+        for j in range(i + 1):
+            carry = step(j == 0 or j == i or i == n - 1, j, carry)
+            pump(cc, cc, d)
         where = pl.ds(QB * i, QB)
         for h in range(2):
             top, l, acc = carry[h]
@@ -587,7 +484,7 @@
     D.finish()
 
 def attend_step(kept, vt, q, start, i, masked, j, carry):
-    r = pl.ds(pl.multiple_of(j * KB, KB), KB)
+    r = pl.ds(j * KB, KB)
     out = []
     for h in range(2):
         m, l, acc = carry[h]
@@ -735,6 +632,205 @@
         + [dma(n) for n in (18, 18, 17, 17, 2)] + [pltpu.SemaphoreType.DMA],
         compiler_params=params(cid), name="middle",
     )(att, x, out_all, gain, shift, dy_all, wgu, wd)
+class ScatterBoth:
+    def __init__(self, pn, buf, tland, land, ss, rs, ts, tr, out, split=None):
+        self.pn, self.tland, self.ts, self.tr = pn, tland, ts, tr
+        rows, cols = buf.shape[1:]
+        order = [(2, 0), (2, 1), (-1, 1), (1, 1), (-1, 0), (1, 0), (0, 1), (0, 0)]
+        def send(k):
+            j = pn.block(*order[k])
+            remote(buf.at[2 * j + 1 - pn.c], tland.at[k], ts, tr, k, pn.twin).start()
+        def add(k):
+            self.copy(k).wait_recv()
+            j = 2 * pn.block(*order[k]) + pn.c
+            step = pace(rows, cols)
+            def body(i, _):
+                r = pl.ds(pl.multiple_of(i * step, 16), step)
+                buf[j, r] = (buf[j, r].astype(jnp.float32) + tland[k, r].astype(jnp.float32)).astype(buf.dtype)
+                return 0
+            repeat(rows // step, body)
+        self.sends = [functools.partial(send, k) for k in range(8)]
+        self.adds = [functools.partial(add, k) for k in range(8)]
+        self.sums, self.done = sum_steps(pn, buf, land, rows, ss, rs, out, lambda j: 2 * j + pn.c, split)
+
+    def copy(self, k):
+        return remote(self.tland.at[k], self.tland.at[k], self.ts, self.tr, k, self.pn.twin)
+
+    def finish(self):
+        self.done()
+        for k in range(8):
+            self.copy(k).wait_send()
+
+SPLIT_F, SPLIT_J = 96, 1568
+
+def back_kernel(dh2, mid, dy, gain, out_all, q_ref, k_ref, v_ref, start_ref, ot_ref, lse_ref, cs, ffp, joined,
+                mgrad, da, dproj, bias, sums, layer_out, grads,
+                wbuf, dg, inbox, do_ref, keptk, keptv, keptq, keptd, kt, dot_, dq_ref, dk_ref, dv_ref, t0, t1, t2, fbuf, fland, fsum, jbuf, tland, jland,
+                ssO, rsO, ssT, rsT, ssF, rsF, ssJ, rsJ, tsJ, trJ, lsw, ls):
+    sp, wp = Plane("seq"), Plane("wt")
+    tok, width = dh2.shape
+    c, m = sp.c, sp.block(0, 0)
+    chips = [at(j // 4, j % 4, c, wp.a, wp.b) for j in range(8)]
+    bar = pltpu.get_barrier_semaphore()
+    for j in range(8):
+        @pl.when(m != j)
+        def _():
+            pl.semaphore_signal(bar, inc=1, device_id=chips[j], device_id_type=MESH)
+    for t in (sp.twin, wp.left, wp.right, wp.pair):
+        pl.semaphore_signal(bar, inc=1, device_id=t, device_id_type=MESH)
+    def load(w, slot):
+        return pltpu.make_async_copy(out_all.at[pl.ds(2 * w, 2)], wbuf.at[slot], lsw.at[slot])
+    load(0, 0).start()
+    here = [pltpu.make_async_copy(ffp, fbuf, ls.at[0]), pltpu.make_async_copy(joined, jbuf, ls.at[1])]
+    for cp in here:
+        cp.start()
+    def ln(i, carry):
+        r = pl.ds(pl.multiple_of(i * 32, 32), 32)
+        y = mid[r]
+        centred = y - jnp.mean(y, axis=-1, keepdims=True)
+        inverse = lax.rsqrt(jnp.mean(centred * centred, axis=-1, keepdims=True) + norm_eps)
+        scaled = centred * inverse
+        up = dh2[r]
+        w = up * gain[...]
+        back = inverse * (w - jnp.mean(w, axis=-1, keepdims=True) - scaled * jnp.mean(w * scaled, axis=-1, keepdims=True))
+        g = dy[r].astype(jnp.float32) + back
+        mgrad[r] = g
+        da[r] = g.astype(jnp.bfloat16)
+        return carry[0] + jnp.sum((up * scaled).reshape(4, 8, width), axis=0), carry[1] + jnp.sum(up.reshape(4, 8, width), axis=0)
+    nil = jnp.zeros((8, width), jnp.float32)
+    gsum, ssum = lax.fori_loop(0, tok // 32, ln, (nil, nil))
+    sums[0:1] = jnp.sum(gsum, axis=0, keepdims=True)
+    sums[1:2] = jnp.sum(ssum, axis=0, keepdims=True)
+    total = [jnp.zeros((tok, width // 2), jnp.float32)] * 2
+    for w in range(8):
+        load(w, w % 2).wait()
+        if w < 7:
+            load(w + 1, 1 - w % 2).start()
+        g = da[:, 256 * w:256 * w + 256]
+        both = wbuf[w % 2]
+        total = [total[h] + lax.dot_general(g, both[h], NT, preferred_element_type=jnp.float32) for h in range(2)]
+    dg[...] = jnp.concatenate(total, axis=1).astype(jnp.bfloat16)
+    pl.semaphore_wait(bar, 11)
+    def to_chip(j):
+        return pltpu.make_async_remote_copy(src_ref=dg.at[:, pl.ds(256 * j, 256)], dst_ref=inbox.at[m], send_sem=ssO.at[j], recv_sem=rsO.at[m], device_id=chips[j], device_id_type=MESH)
+    for j in range(8):
+        @pl.when(m != j)
+        def _():
+            to_chip(j).start()
+    mine = pltpu.make_async_copy(dg.at[:, pl.ds(pl.multiple_of(256 * m, 256), 256)], inbox.at[m], ls.at[2])
+    mine.start()
+    for cp in here:
+        cp.wait()
+    F, fdone = sum_steps(wp, fbuf, fland, tok, ssF, rsF, fsum, split=SPLIT_F)
+    J = ScatterBoth(sp, jbuf, tland, jland, ssJ, rsJ, tsJ, trJ, grads, SPLIT_J)
+    for f in J.sends:
+        f()
+    F[0]()
+    rotary_tables_to(cs, (t0, t1, t2))
+    halves(k_ref, keptk)
+    halves(v_ref, keptv)
+    halves(q_ref, keptq)
+    kt[...] = k_ref[...].astype(jnp.float32).T.astype(jnp.bfloat16)
+    dk_ref[...] = jnp.zeros_like(dk_ref)
+    dv_ref[...] = jnp.zeros_like(dv_ref)
+    mine.wait()
+    def pass_on(j, own):
+        r = do_ref.at[pl.ds(pl.multiple_of(128 * (2 * j + (c if own else 1 - c)), 128), 128)]
+        src = inbox.at[j, :, pl.ds(pl.multiple_of(128 * (1 - c), 128), 128)] if own else r
+        return pltpu.make_async_remote_copy(src_ref=src, dst_ref=r, send_sem=ssT.at[j], recv_sem=rsT.at[j], device_id=sp.twin, device_id_type=MESH)
+    for j in range(8):
+        @pl.when(m != j)
+        def _():
+            pltpu.make_async_remote_copy(src_ref=inbox.at[j], dst_ref=inbox.at[j], send_sem=ssO.at[j], recv_sem=rsO.at[j], device_id=chips[j], device_id_type=MESH).wait_recv()
+        pass_on(j, True).start()
+        @pl.when(c == 0)
+        def _():
+            do_ref[256 * j:256 * j + 128] = inbox[j, :, 0:128]
+        @pl.when(c == 1)
+        def _():
+            do_ref[256 * j + 128:256 * j + 256] = inbox[j, :, 128:256]
+    for j in range(8):
+        pass_on(j, False).wait_recv()
+    halves(do_ref, keptd)
+    dot_[...] = do_ref[...].astype(jnp.float32).T
+    fi, ji = iter(F[1:]), iter(J.adds + J.sums)
+    n = q_ref.shape[0] // QB
+    for i in range(n):
+        rows = pl.ds(QB * i, QB)
+        q = q_ref[rows]
+        do = do_ref[rows]
+        do_h, q_h = keptd[:, rows], keptq[:, rows]
+        start = start_ref[:, rows]
+        both = ot_ref[:, rows] * dot_[:, rows]
+        inner = [jnp.sum(both[64 * h:64 * h + 64], axis=0, keepdims=True) for h in range(2)]
+        lse2 = lse_ref[:, rows]
+        lse = [lse2[h:h + 1] for h in range(2)]
+        def step(masked, j, carry):
+            r = pl.ds(j * KB, KB)
+            out, ps, ds = [], [], []
+            kk, vv, kk_t = keptk[:, r], keptv[:, r], kt[:, r]
+            for h in range(2):
+                s = lax.dot_general(kk[h], q, NT, preferred_element_type=jnp.float32)
+                if masked:
+                    s = jnp.where(allowed(i, j, start), s, MASKED)
+                p = jnp.exp(s - lse[h])
+                dp = lax.dot_general(vv[h], do, NT, preferred_element_type=jnp.float32)
+                g = (p * (dp - inner[h])).astype(jnp.bfloat16)
+                out.append(carry[h] + jnp.dot(kk_t[64 * h:64 * h + 64], g, preferred_element_type=jnp.float32))
+                ps.append(p.astype(jnp.bfloat16))
+                ds.append(g)
+            dv_ref[r] += sum(jnp.dot(ps[h], do_h[h], preferred_element_type=jnp.float32) for h in range(2))
+            dk_ref[r] += sum(jnp.dot(ds[h], q_h[h], preferred_element_type=jnp.float32) for h in range(2))
+            return tuple(out)
+        carry = (jnp.zeros((64, QB), jnp.float32),) * 2
+        for j in range(i + 1):
+            carry = step(j == 0 or j == i or i == n - 1, j, carry)
+            pump(ji, ji, fi)
+        dq_ref[rows] = jnp.concatenate(carry, axis=0).T
+    def low(v):
+        return v.astype(jnp.bfloat16).astype(jnp.float32)
+    def unturn(i, total):
+        rows = pl.ds(pl.multiple_of(i * 512, 512), 512)
+        keep, ahead, behind = t0[rows], -t1[rows], -t2[rows]
+        parts = (turn(low(dq_ref[rows]) * 0.125, keep, ahead, behind), turn(low(dk_ref[rows]), keep, ahead, behind), dv_ref[rows])
+        new = []
+        for p in range(3):
+            y = parts[p].astype(jnp.bfloat16)
+            dproj[rows, 128 * p:128 * p + 128] = y
+            new.append(total[p] + jnp.sum(y.astype(jnp.float32).reshape(64, 8, 128), axis=0))
+        return tuple(new)
+    total = lax.fori_loop(0, dq_ref.shape[0] // 512, unturn, (jnp.zeros((8, 128), jnp.float32),) * 3)
+    for p in range(3):
+        bias[:, 128 * p:128 * p + 128] = jnp.sum(total[p], axis=0, keepdims=True)
+    for f in fi:
+        f()
+    layer_out[...] = (mid[...] + fsum[...]).astype(jnp.bfloat16)
+    for f in ji:
+        f()
+    fdone()
+    J.finish()
+    for j in range(8):
+        @pl.when(m != j)
+        def _():
+            to_chip(j).wait_send()
+        pass_on(j, True).wait_send()
+
+def back_part(cid, dh2, mid, dy, gain, out_all, q, k, v, start, ot, lse, cs, ffp, joined):
+    tok, width = dy.shape
+    rows = q.shape[0]
+    f, b16, f32, vm = jax.ShapeDtypeStruct, jnp.bfloat16, jnp.float32, pltpu.VMEM
+    wide = joined.shape[1]
+    return pl.pallas_call(
+        back_kernel,
+        out_shape=(f((tok, width), f32), f((tok, width), b16), f((rows, 384), b16), f((1, 384), f32), f((2, width), f32), f((tok, width), b16), f((wide, 128), f32)),
+        in_specs=[VM, VM, VM, VM, ANY, VM, VM, VM, VM, VM, VM, VM, ANY, ANY], out_specs=(VM,) * 7,
+        scratch_shapes=[vm((2, 2) + out_all.shape[1:], b16), vm((tok, width), b16), vm((8, tok, 256), b16), vm((rows, 128), b16)]
+        + [vm((2, rows, 128), b16)] * 4 + [vm((128, rows), b16), vm((128, rows), f32)] + [vm((rows, 128), f32)] * 6
+        + [vm((8, tok, width), b16), vm((7 * tok, width), b16), vm((tok, width), f32)]
+        + [vm((16, wide, 128), b16), vm((8, wide, 128), b16), vm((7 * wide, 128), b16)]
+        + [dma(n) for n in (8, 8, 8, 8, 17, 17, 17, 17, 8, 8, 2, 3)],
+        compiler_params=params(cid), name="back",
+    )(dh2, mid, dy, gain, out_all, q, k, v, start, ot, lse, cs, ffp, joined)
 def params(cid):
     return pltpu.CompilerParams(collective_id=cid, has_side_effects=True, vmem_limit_bytes=56 * 2**20)
 
@@ -829,7 +925,7 @@
             r = pl.ds(pl.multiple_of(i * step, 16), step)
             buf[j, r] = (buf[j, r].astype(jnp.float32) + tland[k, r].astype(jnp.float32)).astype(buf.dtype)
             return 0
-        lax.fori_loop(0, rows // step, body, 0)
+        repeat(rows // step, body)
     steps, done = sum_steps(pn, buf, land, rows, ss, rs, o, lambda j: 2 * j + pn.c)
     for f in steps:
         f()
@@ -1017,16 +1113,6 @@
     return start.reshape(1, rows), jnp.concatenate([jnp.cos(angles), jnp.sin(angles)], axis=0)
 
 
-def wide_tables(cs):
-    c, s = cs[0:8], cs[8:16]
-    one, nil, z8 = jnp.ones((48, c.shape[1]), jnp.float32), jnp.zeros((48, c.shape[1]), jnp.float32), jnp.zeros((8, c.shape[1]), jnp.float32)
-    return [jnp.concatenate(p * 2, axis=0).T for p in ([c, c, one], [-s, z8, nil], [z8, s, nil])]
-
-
-def rotate(v, keep, ahead, behind):
-    return v * keep + jnp.roll(v, -8, axis=1) * ahead + jnp.roll(v, 8, axis=1) * behind
-
-
 def contract_first(left, right):
     return lax.dot_general(left, right, (((0,), (0,)), ((), ())), preferred_element_type=jnp.float32)
 
@@ -1046,7 +1132,6 @@
     inputs = layer_in.reshape(tok, width).astype(f32)
     upstream = layer_grad.reshape(tok, width)
     start, cs = rotary_angles(segment_ids.reshape(rows))
-    keep, ahead, behind = wide_tables(cs)
     _, scaled_one, inverse_one = layer_norm_parts(inputs, norm_one_gain, norm_one_shift)
     bias = lax.dynamic_index_in_dim(qkv_bias.reshape(3, 16, 128), s, 1, keepdims=False).reshape(1, 384)
     half = lax.dynamic_slice_in_dim(out_weight, (s % 2) * (width // 2), width // 2, 0)
@@ -1057,18 +1142,10 @@
     middle, dh2, ffn_part, joined = middle_part(
         4, attended, layer_in.reshape(tok, width), out_all.reshape(16, width // 2, 256), norm_two_gain.reshape(1, width),
         norm_two_shift.reshape(1, width), all_up, gate_up_weight.transpose(1, 2, 0).reshape(2 * hidden, width), down_weight)
-    _, scaled_two, inverse_two = layer_norm_parts(middle, norm_two_gain, norm_two_shift)
-    ffn_out = scatter("wt", 7, ffn_part)
-    layer_out = (middle + ffn_out).astype(bf16).reshape(1, tok, width)
-    gain_two = jnp.sum(dh2 * scaled_two, axis=0)
-    shift_two = jnp.sum(dh2, axis=0)
-    middle_grad = upstream.astype(f32) + layer_norm_back(dh2, scaled_two, inverse_two, norm_two_gain)
-    da = middle_grad.astype(bf16)
-    dout = jnp.einsum("twn,wckn->tck", da.reshape(tok, 8, 256), out_all, preferred_element_type=f32).astype(bf16)
-    do = swap("seq", 16, 8, dout.reshape(tok, 16, 128).transpose(1, 0, 2)).reshape(rows, 128)
-    dq, dk, dv = attention_backward(q, k, v, start, ot, lse, do)
-    low = lambda t: t.astype(bf16).astype(f32)
-    dproj = jnp.concatenate([rotate(low(dq) * scale, keep, -ahead, -behind), rotate(low(dk), keep, -ahead, -behind), dv], axis=1).astype(bf16)
+    middle_grad, da, dproj, bias_sum, sums_two, layer_out, joined = back_part(
+        6, dh2, middle, upstream, norm_two_gain.reshape(1, width), out_all.reshape(16, width // 2, 256), q, k, v, start, ot, lse, cs, ffn_part, joined)
+    layer_out = layer_out.reshape(1, tok, width)
+    gain_two, shift_two = sums_two[0], sums_two[1]
     dh1_part = contract_last(dproj, head_weight).astype(bf16)
     dh1 = scatter_both("seq", 9, dh1_part.reshape(16, tok, width))
     gain_one = jnp.sum(dh1 * scaled_one, axis=0)
@@ -1083,10 +1160,9 @@
     da_cols = swap("wt", 8, 13, da.reshape(tok, 8, 256).transpose(1, 0, 2)).reshape(8 * tok, 256)
     out_part = contract_first(all_att, da_cols).astype(bf16)
     out_grad = scatter_both("seq", 16, out_part.reshape(16, 128, 256))
-    joined = scatter_both("seq", 14, joined)
     gate_grad = joined[:2 * hidden].reshape(2, hidden, 128).transpose(2, 0, 1)
     down_grad = joined[2 * hidden:]
-    bias_grad = lax.dynamic_update_slice(jnp.zeros((3, 16, 128), f32), jnp.sum(dproj.astype(f32), axis=0).reshape(3, 1, 128), (0, s, 0))
+    bias_grad = lax.dynamic_update_slice(jnp.zeros((3, 16, 128), f32), bias_sum.reshape(3, 1, 128), (0, s, 0))
     blocks = [t.reshape(16, 8, -1) for t in (gain_one, shift_one, bias_grad, gain_two, shift_two, jnp.zeros((16 * 8 * 16,), f32))]
     small = small_sum(15, jnp.concatenate(blocks, axis=2).transpose(1, 0, 2))[0]
     return (layer_out, input_grad, small[0:16], small[16:32], qkv_grad, small[32:80], out_grad, small[80:96], small[96:112], gate_grad, down_grad)

time: 597 us -> 535 us (0.90)
  Pallas kernels: 494 us -> 474 us
  local copies, waits for them, and re-layouts: 36.5 us -> 16.5 us
  other arithmetic: 27.5 us -> 11.7 us
  matrix products: 28.5 us -> 22.1 us
    pallas_call x1, Pallas kernels: 27.4 us -> 105 us  [back_part(): pl.pallas_call(back_kernel, out_shape=(f((tok, width), f32), f((tok, widt...]
    pallas_call x3 -> x2, Pallas kernels: 106 us -> 61.6 us  [scatter_both(): pl.pallas_call(functools.partial(scatter_both_kernel, axis), out_shape=ja...]
    pallas_call x2 -> x1, Pallas kernels: 44.9 us -> 15.3 us  [scatter(): pl.pallas_call(functools.partial(scatter_kernel, axis), out_shape=jax.Sha...]
    pallas_call x2 -> x1, Pallas kernels: 36 us -> 9.6 us  [swap(): pl.pallas_call(functools.partial(swap_kernel, axis, n), out_shape=jax.Sha...]
    concatenate x3 -> x0, local copies, waits for them, and re-layouts: 11.9 us -> none  [wide_tables(): jnp.concatenate(p * 2, axis=0)]
    slice x4 -> x1, local copies, waits for them, and re-layouts: 6.61 us -> 0.04 us  [per_device(): gain_two, shift_two = (sums_two[0], sums_two[1])]
    dot_general x1 -> x0, matrix products: 6.45 us -> none  [per_device(): jnp.einsum('twn,wckn->tck', da.reshape(tok, 8, 256), out_all, preferred_e...]
where the time goes in v4:
time: 535 us; the launch traced here: 526 us
  Pallas kernels  474 us (89%)
  matrix products  22.1 us (4%)
  local copies, waits for them, and re-layouts  16.5 us (3%)
  other arithmetic  11.7 us (2%)
    pallas_call x1, Pallas kernels, front(): pl.pallas_call(front_kernel, out_shape=(f((16, tok, width), b16), f((widt...  118 us
    pallas_call x1, Pallas kernels, back_part(): pl.pallas_call(back_kernel, out_shape=(f((tok, width), f32), f((tok, widt...  105 us
    pallas_call x1, Pallas kernels, middle_part(): pl.pallas_call(middle_kernel, out_shape=(f((tok, width), f32), f((tok, wi...  101 us
    pallas_call x2, Pallas kernels, scatter_both(): pl.pallas_call(functools.partial(scatter_both_kernel, axis), out_shape=ja...  61.6 us
    pallas_call x1, Pallas kernels, gather(): pl.pallas_call(functools.partial(gather_kernel, axis), out_shape=jax.Shap...  35 us
    pallas_call x1, Pallas kernels, scatter(): pl.pallas_call(functools.partial(scatter_kernel, axis), out_shape=jax.Sha...  15.3 us
    pallas_call x1, Pallas kernels, small_sum(): pl.pallas_call(small_kernel, out_shape=jax.ShapeDtypeStruct((1, 128), f),...  14.8 us
    dot_general x2, matrix products, contract_first(): lax.dot_general(left, right, (((0,), (0,)), ((), ())), preferred_element_...  13.7 us

profile of v4, /device:TPU:1, one launch (start us, length us, event | category | flops | bytes accessed | tf_op | source)
XLA Modules:
  0.0 525.6 jit_solution(395908048500598694)
XLA Ops:
  0.7 1.2 copy-done
  1.9 0.8 constant_dynamic-slice_fusion.ow
  2.7 1.3 dynamic-slice_bitcast_fusion.bias
  4.0 1.4 fusion.14
  5.3 2.6 subtract_convert_fusion
  8.9 118.1 %front.1 = (bf16[16,128,2048]{2,1,0:T(8,128)(2,1)}, bf16[2048,384]{1,0:T(8,128)(2,1)}, bf16[2048,128]{1,0:T(8,128)(2,1)}, bf16[2048,128]{1,0:T(8,128)(2,1)}, bf1...) custom-call(bf16[128,2048]{1,0:T(8,128)(2,1)} %bitcast.58, ...), custom_call_target="tpu_custom_call" | custom-call | tf_op jit(solution)/shard_map/front/pallas_call | solution.py:507
  127.0 101.0 %middle.1 = (f32[128,2048]{1,0:T(8,128)}, f32[128,2048]{1,0:T(8,128)}, bf16[8,128,2048]{2,1,0:T(8,128)(2,1)}, bf16[16,2112,128]{2,1,0:T(8,128)(2,1)}) custom-call(bf16[128,2048]{1,0:T(8,128)(2,1)} %get-tuple-element.32.att.x, bf16[128,2048]{1,0:T(8,128)(2,1)} %bitcast.59, bf16[16,1024,256]{2,1,0:T(8,128)(2,1)} %get-tuple-element.33.out_all, ...), custom_call_target="tpu_custom_call" | custom-call | tf_op jit(solution)/shard_map/middle/pallas_call | solution.py:626
  228.0 105.3 %back.1 = (f32[128,2048]{1,0:T(8,128)}, bf16[128,2048]{1,0:T(8,128)(2,1)}, bf16[2048,384]{1,0:T(8,128)(2,1)}, f32[1,384]{1,0:T(1,128)}, f32[2,2048]{1,0:T(2,128)...) custom-call(f32[128,2048]{1,0:T(8,128)} %get-tuple-element.35.dh2, f32[128,2048]{1,0:T(8,128)} %get-tuple-element.36.mid, ...), custom_call_target="tpu_custom_call" | custom-call | tf_op jit(solution)/shard_map/back/pallas_call | solution.py:823
  333.3 1.3 copy.33
  334.6 1.0 copy.34
  335.6 9.6 %swap_wt.1 = bf16[8,128,256]{2,1,0:T(8,128)(2,1)} custom-call(bf16[8,128,256]{2,1,0:T(8,128)(2,1)} %bitcast.63), custom_call_target="tpu_custom_call" | custom-call | tf_op jit(solution)/shard_map/swap_wt/pallas_call | solution.py:964
  345.2 35.0 %gather_wt.1 = bf16[8,128,2048]{2,1,0:T(8,128)(2,1)} custom-call(bf16[128,2048]{1,0:T(8,128)(2,1)} %get-tuple-element.32.att.x), custom_call_target="tpu_custom_call" | custom-call | tf_op jit(solution)/shard_map/gather_wt/pallas_call | solution.py:852
  380.3 4.6 fusion
  384.9 15.4 %scatter_both_seq.3 = f32[128,256]{1,0:T(8,128)} custom-call(bf16[16,128,256]{2,1,0:T(8,128)(2,1)} %bitcast.68), custom_call_target="tpu_custom_call" | custom-call | tf_op jit(solution)/shard_map/scatter_both_seq/pallas_call | solution.py:938
  400.3 9.1 %convolution_convert_fusion.1 = bf16[2048,384]{1,0:T(8,128)(2,1)} fusion(bf16[2048,2048]{1,0:T(8,128)(2,1)} %bitcast.81, bf16[2048,384]{1,0:T(8,128)(2,1)S(1)} %copy-done.11), kind=kOutput, calls=%fused_computation.1 | convolution fusion | flops 3222011904 | bytes 11534336 | tf_op jit(solution)/shard_map/dot_general | solution.py:1117
  409.4 15.3 %scatter_wt.1 = f32[256,384]{1,0:T(8,128)} custom-call(bf16[8,256,384]{2,1,0:T(8,128)(2,1)} %bitcast.67), custom_call_target="tpu_custom_call" | custom-call | tf_op jit(solution)/shard_map/scatter_wt/pallas_call | solution.py:903
  424.7 1.0 convert_element_type.46
  425.8 0.7 copy.41
  426.5 13.5 %place_qkv.1 = bf16[6,128,128]{2,1,0:T(8,128)(2,1)} custom-call(bf16[2,3,128,128]{3,2,1,0:T(8,128)(2,1)} %bitcast.69), custom_call_target="tpu_custom_call" | custom-call | tf_op jit(solution)/shard_map/place_qkv/pallas_call | solution.py:1051
  440.0 1.0 convert_bitcast_fusion
  441.1 0.9 copy.36
  442.0 8.4 %convolution_convert_fusion = bf16[2048,2048]{1,0:T(8,128)(2,1)} fusion(bf16[2048,384]{1,0:T(8,128)(2,1)} %get-tuple-element.46, bf16[2048,384]{1,0:T(8,128)(2,1)S(1)} %copy-done.10), kind=kOutput, calls=%fused_computation | convolution fusion | flops 3225419776 | bytes 11534336 | tf_op jit(solution)/shard_map/dot_general | solution.py:1121
  450.5 46.2 %scatter_both_seq.2 = f32[128,2048]{1,0:T(8,128)} custom-call(bf16[16,128,2048]{2,1,0:T(8,128)(2,1)} %bitcast.60), custom_call_target="tpu_custom_call" | custom-call | tf_op jit(solution)/shard_map/scatter_both_seq/pallas_call | solution.py:938
  497.2 1.7 fusion.11
  499.6 0.8 concatenate.7
  500.3 14.8 %small_sum.1 = f32[1,128]{1,0:T(1,128)} custom-call(f32[8,16,128]{2,1,0:T(8,128)} %bitcast.72), custom_call_target="tpu_custom_call" | custom-call | tf_op jit(solution)/shard_map/small_sum/pallas_call | solution.py:1077
  515.1 1.3 slice_bitcast_fusion
  516.5 1.2 slice_bitcast_fusion.2
  517.6 2.6 fusion.13
  520.2 2.0 slice.54
  522.2 1.7 slice.55
  524.0 0.8 copy.45
  (48 shorter events, 2.9 us)
Async XLA Ops:
  0.6 1.2 copy-start
  345.2 35.0 %copy-start.6 = (bf16[8,128,256]{2,1,0:T(8,128)(2,1)S(1)}, bf16[8,128,256]{2,1,0:T(8,128)(2,1)}, u32[]{:S(2)}) copy-start(bf16[8,128,256]{2,1,0:T(8,128)(2,1)} %swap_wt.1) | copy-start | bytes 1572868
  380.3 20.1 %copy-start.11 = (bf16[2048,384]{1,0:T(8,128)(2,1)S(1)}, bf16[2048,384]{1,0:T(8,128)(2,1)}, u32[]{:S(2)}) copy-start(bf16[2048,384]{1,0:T(8,128)(2,1)} %get-tuple-element.46) | copy-start | bytes 4718596
  409.4 32.6 %copy-start.10 = (bf16[2048,384]{1,0:T(8,128)(2,1)S(1)}, bf16[2048,384]{1,0:T(8,128)(2,1)}, u32[]{:S(2)}) copy-start(bf16[2048,384]{1,0:T(8,128)(2,1)} %get-tuple-element.47) | copy-start | bytes 4718596
  450.4 46.2 %copy-start.2 = (bf16[1,128,2048]{2,1,0:T(8,128)(2,1)S(1)}, bf16[1,128,2048]{2,1,0:T(8,128)(2,1)}, u32[]{:S(2)}) copy-start(bf16[1,128,2048]{2,1,0:T(8,128)(2,1)} %param.12) | copy-start | bytes 1572868
  450.4 46.7 %copy-start.7 = (f32[2048]{0:T(1024)S(1)}, f32[2048]{0:T(1024)}, u32[]{:S(2)}) copy-start(f32[2048]{0:T(1024)} %param.14) | copy-start | bytes 24580
  450.4 48.6 %copy-start.9 = (f32[1,384]{1,0:T(1,128)S(1)}, f32[1,384]{1,0:T(1,128)}, u32[]{:S(2)}) copy-start(f32[1,384]{1,0:T(1,128)} %get-tuple-element.48) | copy-start | bytes 4612
  496.7 2.6 copy-start.8
  496.7 20.9 %copy-start.3 = (f32[128,2048]{1,0:T(8,128)S(1)}, f32[128,2048]{1,0:T(8,128)}, u32[]{:S(2)}) copy-start(f32[128,2048]{1,0:T(8,128)} %scatter_both_seq.2) | copy-start | bytes 3145732
  499.4 24.6 %copy-start.5 = (bf16[128,2048]{1,0:T(8,128)(2,1)S(1)}, bf16[128,2048]{1,0:T(8,128)(2,1)}, u32[]{:S(2)}) copy-start(bf16[128,2048]{1,0:T(8,128)(2,1)} %get-tuple-element.44) | copy-start | bytes 1572868
  517.6 7.8 %copy-start.1 = (bf16[2048,256]{1,0:T(8,128)(2,1)S(1)}, bf16[2048,256]{1,0:T(8,128)(2,1)}, u32[]{:S(2)}) copy-start(bf16[2048,256]{1,0:T(8,128)(2,1)} %param.18) | copy-start | bytes 3145732
  517.6 7.2 %copy-start.4 = (f32[128,256]{1,0:T(8,128)S(1)}, f32[128,256]{1,0:T(8,128)}, u32[]{:S(2)}) copy-start(f32[128,256]{1,0:T(8,128)} %scatter_both_seq.3) | copy-start | bytes 393220
